TPU v7x, 32 devices: a whole 2x2x4 slice. The times are simulated.
32 devices in a mesh: pool: 16 (over z, x, core), head: 2 (over y).
Axes of the slice: x: 2, y: 2, z: 4, core: 2. Of those that a mesh axis runs over, the one named last changes fastest.
Arguments:
- queries: bfloat16 [16, 128, 4096], P('pool', None, 'head'), may hold values from -128 to 128
- request_keys: bfloat16 [16, 128, 1024], P('pool', None, 'head'), may hold values from -8 to 8
- request_values: bfloat16 [16, 128, 1024], P('pool', None, 'head'), may hold values from -6 to 6
- cache_keys: bfloat16 [32, 8, 128, 128], P('pool', 'head'), may hold values from -6 to 6
- cache_values: bfloat16 [32, 8, 128, 128], P('pool', 'head'), may hold values from -6 to 6
- passage_ids: int32 [16, 16], P('pool'), may hold values from 0 to 31, as said below
- passage_order: int32 [16, 16], P('pool'), may hold values from 0 to 15, each once within a row
- out_weight: bfloat16 [4096, 4096], P(('head', 'pool')), may hold values from -6 to 6
Outputs:
- mixed: bfloat16 [16, 128, 4096], P('pool', None, 'head')
Inputs may be any that keep to these rules, and one draw needn't show every extreme that they name: `passage_ids`: the 16 passages of one request are held by 16 different indices of pool, one passage of each index; passage i is held by index i // 2.
All inputs are finite; a program needn't handle non-finite values.
Results may differ from a plain program's by a relative error of at most 0.012.
Values may be sent and summed in bfloat16 or wider, within the bound.
No kernel may reach another device: no remote copies, remote signals or barrier semaphores. Data moves between devices by JAX's collectives and lax.ppermute only.
A program may use at most 128 MiB of HBM per device.

v0:
```python
import functools
import math

import jax
import jax.numpy as jnp
from jax import lax
from jax.experimental import pallas as pl
from jax.experimental.pallas import tpu as pltpu
from jax.sharding import PartitionSpec as P

CORES = 2
ROWS = 4
LANES = 128
MIB = 1024 * 1024


def frequency_table(head_dim):
    pair_index = jnp.arange(head_dim // 2, dtype=jnp.float32)
    return jnp.exp(pair_index * (-2.0 / head_dim) * jnp.log(jnp.float32(500000.0)))


def reposition(vectors, offset, head_dim):
    angles = offset.astype(jnp.float32) * frequency_table(head_dim)
    cosine = jnp.cos(angles)
    sine_term = jnp.sin(angles)
    front_half = vectors[..., : head_dim // 2]
    back_half = vectors[..., head_dim // 2 :]
    return jnp.concatenate(
        [front_half * cosine - back_half * sine_term, back_half * cosine + front_half * sine_term],
        axis=-1,
    )


def absorb(state, query_rows, keys_block, values_block, allowed):
    running_peak, running_total, running_sum = state
    scores = jnp.einsum(
        "hrd,hnd->hrn", query_rows, keys_block, preferred_element_type=jnp.float32
    ) * query_rows.shape[2] ** (-0.5)
    if allowed is not None:
        scores = jnp.where(allowed[None], scores, -jnp.inf)
    new_peak = jnp.maximum(running_peak, jnp.max(scores, axis=-1))
    factor = jnp.exp(running_peak - new_peak)
    exponent = jnp.exp(scores - new_peak[..., None])
    weights = exponent.astype(jnp.bfloat16)
    new_total = running_total * factor + jnp.sum(exponent, axis=-1)
    new_sum = running_sum * factor[..., None] + jnp.einsum(
        "hrn,hnd->hrd", weights, values_block, preferred_element_type=jnp.float32
    )
    return (new_peak, new_total, new_sum)


def plain_body(
    queries,
    request_keys,
    request_values,
    cache_keys,
    cache_values,
    passage_ids,
    passage_order,
    out_weight,
):
    owned, kv_local, pass_len, head_dim = cache_keys.shape
    query_len = queries.shape[1]
    groups = queries.shape[2] // (kv_local * head_dim)
    row_count = query_len * groups
    query_rows = (
        queries[0]
        .reshape(query_len, kv_local, groups, head_dim)
        .transpose(1, 0, 2, 3)
        .reshape(kv_local, row_count, head_dim)
    )
    own_keys = request_keys[0].reshape(query_len, kv_local, head_dim).transpose(1, 0, 2)
    own_values = request_values[0].reshape(query_len, kv_local, head_dim).transpose(1, 0, 2)
    query_token = jnp.arange(row_count) // groups
    causal = jnp.arange(query_len)[None, :] <= query_token[:, None]
    state = (
        jnp.full((kv_local, row_count), -jnp.inf, jnp.float32),
        jnp.zeros((kv_local, row_count), jnp.float32),
        jnp.zeros((kv_local, row_count, head_dim), jnp.float32),
    )
    state = absorb(state, query_rows, own_keys, own_values, causal)
    slots = passage_ids[0]
    offsets = passage_order[0] * pass_len
    piece_keys = lax.all_gather(cache_keys, "pool", axis=0, tiled=True)
    piece_values = lax.all_gather(cache_values, "pool", axis=0, tiled=True)

    def visit_one(position, current):
        matches = slots == position
        offset = jnp.sum(jnp.where(matches, offsets, 0))

        def absorb_one(inner):
            placed = reposition(piece_keys[position].astype(jnp.float32), offset, head_dim).astype(
                jnp.bfloat16
            )
            return absorb(inner, query_rows, placed, piece_values[position], None)

        return lax.cond(jnp.any(matches), absorb_one, lambda inner: inner, current)

    state = lax.fori_loop(0, piece_keys.shape[0], visit_one, state)
    running_peak, running_total, running_sum = state
    attended = (running_sum / running_total[..., None]).astype(jnp.bfloat16)
    attended = (
        attended.reshape(kv_local, query_len, groups, head_dim)
        .transpose(1, 0, 2, 3)
        .reshape(query_len, kv_local * groups * head_dim)
    )
    partial_value = jnp.dot(
        attended,
        lax.all_gather(out_weight, "pool", axis=0, tiled=True),
        preferred_element_type=jnp.float32,
    )
    summed = lax.psum_scatter(
        partial_value.astype(jnp.bfloat16), "head", scatter_dimension=1, tiled=True
    )
    return summed[None]


def ring_order(chips):
    columns = chips // ROWS
    cells = []
    for row in range(ROWS):
        across = range(1, columns) if row % 2 == 0 else range(columns - 1, 0, -1)
        cells += [row * columns + column for column in across]
    return cells + [row * columns for row in reversed(range(ROWS))]


def shift(value, order, step):
    chips = len(order)
    pairs = [
        (order[at] * CORES + core, order[(at + step) % chips] * CORES + core)
        for at in range(chips)
        for core in range(CORES)
    ]
    return lax.ppermute(value, "pool", pairs)


def onward(pieces, step, order):
    chips = len(order)
    pieces[step] = shift(pieces[step - 1], order, 1)
    pieces[chips - step] = shift(pieces[(chips - step + 1) % chips], order, -1)


def after(value, *earlier):
    return lax.optimization_barrier((value, earlier))[0]


def swap_core(value, pool):
    return lax.ppermute(value, "pool", [(at, at ^ 1) for at in range(pool)])


def swap_plane(value):
    return lax.ppermute(value, "head", [(0, 1), (1, 0)])


def holder(ring, me, back):
    chips = ring.shape[0] // 2
    chip = lax.div(me[0], CORES)
    place = lax.rem(ring[chips + chip] + chips - back, chips)
    return ring[place] * CORES + lax.rem(me[0], CORES)


def attend_kernel(pieces, owned, ids, ranks, ring, me, queries, cosine, sine, *refs):
    key_pieces, value_pieces, refs = refs[:pieces], refs[pieces : 2 * pieces], refs[2 * pieces :]
    stats, keys, values, within, rank_of, key_sem, value_sem = refs[-7:]
    slots = ids.shape[0]
    kv_local, _, head_dim = keys.shape
    near, sums = refs[: -7 - kv_local], refs[-7 - kv_local : -7]
    length = key_pieces[0].shape[2]
    tokens = queries.shape[0]
    groups = queries.shape[1] // (kv_local * head_dim)
    heads = kv_local * groups
    factor = math.log2(math.e) / math.sqrt(head_dim)
    across = (((1,), (1,)), ((), ()))

    for slot in range(slots):
        passage = ids[slot]
        home = lax.div(passage, owned)
        within[home] = passage - home * owned
        rank_of[home] = ranks[slot]
    homes = [holder(ring, me, piece) for piece in range(pieces)]

    def copy(source, target, sem, piece):
        rows = pl.ds(piece * length, length)
        return pltpu.make_async_copy(
            source[piece].at[within[homes[piece]]], target.at[:, rows], sem.at[piece]
        )

    key_copies = [copy(key_pieces, keys, key_sem, piece) for piece in range(pieces)]
    value_copies = [copy(value_pieces, values, value_sem, piece) for piece in range(pieces)]
    for each in key_copies + value_copies:
        each.start()
    for piece in range(pieces):
        key_copies[piece].wait()
        rank = rank_of[homes[piece]]
        cos = cosine[pl.ds(rank, 1), :]
        sin = sine[pl.ds(rank, 1), :]
        rows = pl.ds(piece * length, length)
        for head in range(kv_local):
            block = keys[head, rows, :].astype(jnp.float32)
            turned = block * cos + pltpu.roll(block, head_dim // 2, 1) * sin
            keys[head, rows, :] = turned.astype(jnp.bfloat16)
    for each in value_copies:
        each.wait()

    lane = lax.broadcasted_iota(jnp.int32, (tokens, LANES), 1)
    marks = jnp.zeros((tokens, LANES), jnp.float32)
    for head in range(kv_local):
        spans = [
            slice((head * groups + g) * head_dim, (head * groups + g + 1) * head_dim)
            for g in range(groups)
        ]
        rows = jnp.concatenate([queries[:, span] for span in spans], axis=0)
        scores = lax.dot_general(rows, keys[head], across, preferred_element_type=jnp.float32)
        peak = jnp.max(scores, axis=1, keepdims=True)
        if near:
            own = slice(head * head_dim, (head + 1) * head_dim)
            close = lax.dot_general(
                rows, near[0][:, own], across, preferred_element_type=jnp.float32
            )
            token = lax.rem(lax.broadcasted_iota(jnp.int32, close.shape, 0), tokens)
            column = lax.broadcasted_iota(jnp.int32, close.shape, 1)
            close = jnp.where(column <= token, close, -jnp.inf)
            peak = jnp.maximum(peak, jnp.max(close, axis=1, keepdims=True))
        exponent = jnp.exp2((scores - peak) * factor)
        total = jnp.sum(exponent, axis=1, keepdims=True)
        summed = jnp.dot(
            exponent.astype(jnp.bfloat16), values[head], preferred_element_type=jnp.float32
        )
        if near:
            exponent = jnp.exp2((close - peak) * factor)
            total = total + jnp.sum(exponent, axis=1, keepdims=True)
            summed = summed + jnp.dot(
                exponent.astype(jnp.bfloat16), near[1][:, own], preferred_element_type=jnp.float32
            )
        for g in range(groups):
            part = slice(g * tokens, (g + 1) * tokens)
            sums[head][:, g * head_dim : (g + 1) * head_dim] = summed[part]
            at = head * groups + g
            marks = jnp.where(lane == at, peak[part], marks)
            marks = jnp.where(lane == heads + at, total[part], marks)
    stats[...] = marks


def attend(ids, ranks, ring, me, queries, tables, near, passages, effort=24):
    pieces = len(passages[0])
    key_pieces, value_pieces = passages
    owned, kv_local, length, head_dim = key_pieces[0].shape
    tokens, features = queries.shape
    holders = ids.shape[0]
    smem = pl.BlockSpec(memory_space=pltpu.SMEM)
    vmem = pl.BlockSpec(memory_space=pltpu.VMEM)
    seen = pieces * length
    scores = tokens * (features // head_dim) * (seen + (length if near else 0))
    return pl.pallas_call(
        functools.partial(attend_kernel, pieces, owned),
        out_shape=[jax.ShapeDtypeStruct((tokens, features // kv_local), jnp.float32)] * kv_local
        + [jax.ShapeDtypeStruct((tokens, LANES), jnp.float32)],
        in_specs=[smem] * 4
        + [vmem] * 3
        + [pl.BlockSpec(memory_space=pl.ANY)] * (2 * pieces)
        + [vmem] * len(near),
        out_specs=[vmem] * (kv_local + 1),
        scratch_shapes=[
            pltpu.VMEM((kv_local, seen, head_dim), jnp.bfloat16),
            pltpu.VMEM((kv_local, seen, head_dim), jnp.bfloat16),
            pltpu.SMEM((holders,), jnp.int32),
            pltpu.SMEM((holders,), jnp.int32),
            pltpu.SemaphoreType.DMA((pieces,)),
            pltpu.SemaphoreType.DMA((pieces,)),
        ],
        compiler_params=pltpu.CompilerParams(vmem_limit_bytes=32 * MIB),
        cost_estimate=pl.CostEstimate(
            flops=effort * scores * head_dim, bytes_accessed=4 * MIB, transcendentals=scores
        ),
        name="attend",
    )(ids, ranks, ring, me, queries, *tables, *key_pieces, *value_pieces, *near)


def combine_kernel(head_dim, *refs):
    attended, refs = refs[-1], refs[:-1]
    count = len(refs) // 2
    sums, stats = refs[: count - 1], refs[count - 1]
    sums_in, stats_in = refs[count:-1], refs[-1]
    groups = sums[0].shape[1] // head_dim
    heads = groups * len(sums)
    factor = math.log2(math.e) / math.sqrt(head_dim)
    for head in range(heads):
        block, at = divmod(head, groups)
        columns = slice(at * head_dim, (at + 1) * head_dim)
        peak_a, peak_b = stats[:, head : head + 1], stats_in[:, head : head + 1]
        at = heads + head
        total_a, total_b = stats[:, at : at + 1], stats_in[:, at : at + 1]
        peak = jnp.maximum(peak_a, peak_b)
        part_a = jnp.exp2((peak_a - peak) * factor)
        part_b = jnp.exp2((peak_b - peak) * factor)
        total = total_a * part_a + total_b * part_b
        value = sums[block][:, columns] * part_a + sums_in[block][:, columns] * part_b
        columns = slice(head * head_dim, (head + 1) * head_dim)
        attended[:, columns] = (value / total).astype(attended.dtype)


def combine(head_dim, state, state_in):
    tokens, width = state[0].shape
    size = tokens * width * (len(state) - 1)
    vmem = pl.BlockSpec(memory_space=pltpu.VMEM)
    return pl.pallas_call(
        functools.partial(combine_kernel, head_dim),
        out_shape=jax.ShapeDtypeStruct((tokens, size // tokens), jnp.bfloat16),
        in_specs=[vmem] * (2 * len(state)),
        out_specs=vmem,
        compiler_params=pltpu.CompilerParams(vmem_limit_bytes=24 * MIB),
        cost_estimate=pl.CostEstimate(flops=4 * size, bytes_accessed=10 * size, transcendentals=0),
        name="combine",
    )(*state, *state_in)


def project_kernel(items, based, ring, me, own_rows, other_rows, *refs):
    count = sum(number for _, _, number in items)
    blocks, refs = refs[:count], refs[count:]
    base = None
    if based:
        base, refs = refs[0], refs[1:]
    results, (held, total, sems) = refs[:-3], refs[-3:]
    span = held.shape[2]
    copies, at = [], 0
    for item, (_, _, number) in enumerate(items):
        targets = [held.at[item]] if number == 1 else [held.at[item, pl.ds(i, 1)] for i in range(number)]
        copies.append(
            [
                pltpu.make_async_copy(blocks[at + i], target, sems.at[at + i])
                for i, target in enumerate(targets)
            ]
        )
        at += number
    for group in copies:
        for copy in group:
            copy.start()
    for item, (place, crossed, _) in enumerate(items):
        for copy in copies[item]:
            copy.wait()
        home = holder(ring, me, place)
        if crossed:
            home = home + 1 - 2 * lax.rem(home, CORES)
        columns = pl.ds(pl.multiple_of(home * span, span), span)
        value = jnp.dot(
            jnp.concatenate([rows[:, columns] for rows in (own_rows, other_rows)], axis=1),
            jnp.concatenate([held[item, plane] for plane in range(2)], axis=0),
            preferred_element_type=jnp.float32,
        )
        if item:
            value = value + total[...]
        elif base is not None:
            value = value + base[...]
        if item + 1 < len(items):
            total[...] = value
    tokens = results[0].shape[0]
    for part, result in enumerate(results):
        result[...] = value[part * tokens : (part + 1) * tokens].astype(result.dtype)


def project(ring, me, rows, blocks, base, shapes):
    items = tuple((place, crossed, len(parts)) for (place, crossed), parts in blocks.items())
    flat = [part for parts in blocks.values() for part in parts]
    tokens = rows[0].shape[0]
    span, width = flat[0].shape[1:]
    size = len(items) * 2 * span * width
    smem = pl.BlockSpec(memory_space=pltpu.SMEM)
    vmem = pl.BlockSpec(memory_space=pltpu.VMEM)
    return pl.pallas_call(
        functools.partial(project_kernel, items, base is not None),
        out_shape=shapes,
        in_specs=[smem] * 2
        + [vmem] * 2
        + [pl.BlockSpec(memory_space=pl.ANY)] * len(flat)
        + ([vmem] if base is not None else []),
        out_specs=[vmem] * len(shapes),
        scratch_shapes=[
            pltpu.VMEM((len(items), 2, span, width), jnp.bfloat16),
            pltpu.VMEM((tokens, width), jnp.float32),
            pltpu.SemaphoreType.DMA((len(flat),)),
        ],
        compiler_params=pltpu.CompilerParams(vmem_limit_bytes=32 * MIB),
        cost_estimate=pl.CostEstimate(
            flops=2 * tokens * size, bytes_accessed=2 * size + 4 * tokens * width, transcendentals=0
        ),
        name="project",
    )(ring, me, *rows, *flat, *([base] if base is not None else []))


def rotation_tables(ranks, length, head_dim):
    offsets = (jnp.arange(ranks) * length).astype(jnp.float32)
    angles = offsets[:, None] * frequency_table(head_dim)[None, :]
    cosine, sine = jnp.cos(angles), jnp.sin(angles)
    return (
        jnp.concatenate([cosine, cosine], axis=1),
        jnp.concatenate([-sine, sine], axis=1),
    )


def ring_body(
    pool,
    queries,
    request_keys,
    request_values,
    cache_keys,
    cache_values,
    passage_ids,
    passage_order,
    out_weight,
):
    _, _, pass_len, head_dim = cache_keys.shape
    tokens = queries.shape[1]
    chips = pool // CORES
    half = chips // 2
    order = ring_order(chips)
    ring = jnp.asarray(order + [order.index(chip) for chip in range(chips)], jnp.int32)
    index = lax.axis_index("pool")
    me = jnp.reshape(index, (1,))
    core = lax.rem(index, CORES)
    plane = lax.axis_index("head")

    span = out_weight.shape[1] // 2
    width = span // CORES
    other_queries = swap_core(queries[0], pool)
    weight, other_queries = lax.optimization_barrier((out_weight, other_queries))
    across = swap_plane(
        lax.dynamic_slice_in_dim(weight, (1 - plane) * span, span, axis=1)
    )

    kept = {0: cache_keys}, {0: cache_values}
    for pieces in kept:
        onward(pieces, 1, order)
    for step in range(2, half):
        for pieces in kept:
            onward(pieces, step, order)

    out_weight, across = after(
        (out_weight, across),
        kept[0][2], kept[0][chips - 2],
    )

    def columns(to_core):
        first = to_core * width
        return jnp.stack(
            [
                lax.dynamic_slice_in_dim(out_weight, plane * span + first, width, axis=1),
                lax.dynamic_slice_in_dim(across, first, width, axis=1),
            ]
        )

    near, far = heavy = {0: columns(core)}, {0: swap_core(columns(1 - core), pool)}
    near[0] = after(near[0], *[kept[1][at] for at in (2, chips - 2)])
    far[0] = after(far[0], *[kept[0][at] for at in (half - 1, half + 1)])
    for step in range(1, half):
        for pieces in heavy:
            onward(pieces, step, order)

    queries, picks, last_keys, last_values = after(
        (
            queries[0],
            jnp.concatenate([passage_ids, passage_order], axis=0),
            kept[0][half - 1],
            kept[1][half + 1],
        ),
        near[1],
        near[chips - 1],
    )
    kept[0][half] = shift(last_keys, order, 1)
    kept[1][half] = shift(last_values, order, -1)
    passages = [[pieces[at] for at in range(chips)] for pieces in kept]

    picks_in = swap_core(picks, pool)
    other_queries = after(
        other_queries, far[1], far[chips - 1]
    )
    tables = rotation_tables(passage_ids.shape[1], pass_len, head_dim)
    other = attend(picks_in[0], picks_in[1], ring, me, other_queries, tables, (), passages)
    own_block = (request_keys[0], request_values[0])
    other_in = [swap_core(value, pool) for value in other]
    queries, other_in = after((queries, other_in), near[2], near[chips - 2])
    own = attend(picks[0], picks[1], ring, me, queries, tables, own_block, passages, 1)
    own = after(own, far[2], far[chips - 2])

    attended = combine(head_dim, own, other_in)
    turned = after(swap_plane(attended), near[3], near[chips - 3])
    quarters = {}

    def last(crossed):
        part = heavy[crossed]
        quarters[(half, crossed)] = (
            shift(part[half - 1][:1], order, 1),
            shift(part[half + 1][1:], order, -1),
        )

    last(0)
    last(1)
    crossed_rows = swap_core(turned, pool)
    crossed_rows = after(crossed_rows, far[3], far[chips - 3])
    rows = [
        jnp.concatenate([attended, swap_core(attended, pool)], axis=0),
        jnp.concatenate([turned, crossed_rows], axis=0),
    ]

    def blocks(places):
        return {(at, part): (heavy[part][at],) for at in places for part in range(2)}

    sums = [jax.ShapeDtypeStruct((CORES * tokens, width), jnp.float32)]
    early = [0] + [at for step in range(1, half - 1) for at in (step, chips - step)]
    total = project(ring, me, rows, blocks(early), None, sums)[0]
    middle = blocks([half - 1, half + 1]) | {(half, 0): quarters[half, 0]}
    total = project(ring, me, rows, middle, total, sums)[0]
    own_out, other_out = project(
        ring,
        me,
        rows,
        {(half, 1): quarters[half, 1]},
        total,
        [jax.ShapeDtypeStruct((tokens, width), jnp.bfloat16)] * 2,
    )
    beside = swap_core(other_out, pool)
    result = jnp.where(
        core == 0,
        jnp.concatenate([own_out, beside], axis=1),
        jnp.concatenate([beside, own_out], axis=1),
    )
    return result[None]


def solution(mesh):
    pool, heads_axis = mesh.shape["pool"], mesh.shape["head"]

    def body(*args):
        weight = args[-1]
        tiled = weight.shape[0] % LANES == 0 and weight.shape[1] % (2 * CORES * LANES) == 0
        if tiled and heads_axis == 2 and pool % (2 * ROWS * CORES) == 0:
            return ring_body(pool, *args)
        return plain_body(*args)

    placed = (
        P("pool", None, "head"),
        P("pool", None, "head"),
        P("pool", None, "head"),
        P("pool", "head", None, None),
        P("pool", "head", None, None),
        P("pool", None),
        P("pool", None),
        P(("head", "pool"), None),
    )
    return jax.shard_map(
        body, mesh=mesh, in_specs=placed, out_specs=P("pool", None, "head"), check_vma=False
    )
```

profile of v0, /device:TPU:0, one launch (start us, length us, event | category | flops | bytes accessed | tf_op | source)
XLA Modules:
  0.0 129.3 jit_solution(10687837752637455201)
XLA Ops:
  0.5 2.5 %collective-permute-start = (bf16[2,4,128,128]{3,2,1,0:T(8,128)(2,1)}, bf16[2,4,128,128]{3,2,1,0:T(8,128)(2,1)S(1)}, u32[]{:S(2)}, u32[]{:S(2)}) collective-permute-start(bf16[2,4,128,128]{3,2,1,0:T(8,128)(2,1)} %refs_0_.3), channel_id=1, source_target_pairs={{4,12},{6,14},{12,20},{14,22},{20,28},{22,30},{28,24},{30,26},{24,... | collective-permute-start | bytes 786440 | tf_op jit(solution)/shard_map/ppermute | solution.py:134
  4.2 2.0 %collective-permute-start.7 = (bf16[128,2048]{1,0:T(8,128)(2,1)S(1)}, bf16[128,2048]{1,0:T(8,128)(2,1)S(1)}, u32[]{:S(2)}, u32[]{:S(2)}) collective-permute-start(bf16[128,2048]{1,0:T(8,128)(2,1)S(1)} %constant_dynamic-slice_fusion), channel_id=1, source_target_pairs={{0,1},{1,0},{2,3},{3,2},{4,5},{5,4},{6,7},{7,6},{8,9},{9,8},{10,11... | collective-permute-start | bytes 1572872 | tf_op jit(solution)/shard_map/ppermute | solution.py:152
  8.3 2.2 %collective-permute-done.refs_1_ = bf16[2,4,128,128]{3,2,1,0:T(8,128)(2,1)S(1)} collective-permute-done((bf16[2,4,128,128]{3,2,1,0:T(8,128)(2,1)}, bf16[2,4,128,128]{3,2,1,0:T(8,128)(2,1)S(1)}, u32[]{:S(2)}, u32[]{:S(2)}) %collective-permute-start) | collective-permute-done | bytes 262176 | tf_op jit(solution)/shard_map/ppermute | solution.py:134
  10.4 1.9 %collective-permute-start.1 = (bf16[2,4,128,128]{3,2,1,0:T(8,128)(2,1)S(1)}, bf16[2,4,128,128]{3,2,1,0:T(8,128)(2,1)S(1)}, u32[]{:S(2)}, u32[]{:S(2)}) collective-permute-start(bf16[2,4,128,128]{3,2,1,0:T(8,128)(2,1)S(1)} %collective-permute-done.refs_1_), channel_id=1, source_target_pairs={{4,12},{6,14},{12,20},{14,22},{20,28},{22,30},{28,24},{30,26},{24,... | collective-permute-start | bytes 786440 | tf_op jit(solution)/shard_map/ppermute | solution.py:134
  12.5 3.6 %collective-permute-done.10.refs_9_ = bf16[2,4,128,128]{3,2,1,0:T(8,128)(2,1)S(1)} collective-permute-done((bf16[2,4,128,128]{3,2,1,0:T(8,128)(2,1)S(1)}, bf16[2,4,128,128]{3,2,1,0:T(8,128)(2,1)S(1)}, u32[]{:S(2)}, u32[]{:S(2)}) %collective-permute-start.10) | collective-permute-done | bytes 262176 | tf_op jit(solution)/shard_map/ppermute | solution.py:134
  16.1 1.9 %collective-permute-start.11 = (bf16[2,4,128,128]{3,2,1,0:T(8,128)(2,1)S(1)}, bf16[2,4,128,128]{3,2,1,0:T(8,128)(2,1)S(1)}, u32[]{:S(2)}, u32[]{:S(2)}) collective-permute-start(bf16[2,4,128,128]{3,2,1,0:T(8,128)(2,1)S(1)} %collective-permute-done.10.refs_9_), channel_id=1, source_target_pairs={{4,12},{6,14},{12,20},{14,22},{20,28},{22,30},{28,24},{30,26},{24,... | collective-permute-start | bytes 786440 | tf_op jit(solution)/shard_map/ppermute | solution.py:134
  18.1 3.6 %collective-permute-done.1.refs_2_ = bf16[2,4,128,128]{3,2,1,0:T(8,128)(2,1)S(1)} collective-permute-done((bf16[2,4,128,128]{3,2,1,0:T(8,128)(2,1)S(1)}, bf16[2,4,128,128]{3,2,1,0:T(8,128)(2,1)S(1)}, u32[]{:S(2)}, u32[]{:S(2)}) %collective-permute-start.1) | collective-permute-done | bytes 262176 | tf_op jit(solution)/shard_map/ppermute | solution.py:134
  21.7 1.9 %collective-permute-done.9.refs_6_ = bf16[2,4,128,128]{3,2,1,0:T(8,128)(2,1)S(1)} collective-permute-done((bf16[2,4,128,128]{3,2,1,0:T(8,128)(2,1)S(1)}, bf16[2,4,128,128]{3,2,1,0:T(8,128)(2,1)S(1)}, u32[]{:S(2)}, u32[]{:S(2)}) %collective-permute-start.9) | collective-permute-done | bytes 262176 | tf_op jit(solution)/shard_map/ppermute | solution.py:134
  24.9 1.6 %collective-permute-start.2 = (bf16[2,4,128,128]{3,2,1,0:T(8,128)(2,1)S(1)}, bf16[2,4,128,128]{3,2,1,0:T(8,128)(2,1)S(1)}, u32[]{:S(2)}, u32[]{:S(2)}) collective-permute-start(bf16[2,4,128,128]{3,2,1,0:T(8,128)(2,1)S(1)} %collective-permute-done.1.refs_2_), channel_id=1, source_target_pairs={{4,12},{6,14},{12,20},{14,22},{20,28},{22,30},{28,24},{30,26},{24,... | collective-permute-start | bytes 786440 | tf_op jit(solution)/shard_map/ppermute | solution.py:134
  28.4 1.6 %collective-permute-start.12 = (bf16[2,128,1024]{2,1,0:T(8,128)(2,1)S(1)}, bf16[2,128,1024]{2,1,0:T(8,128)(2,1)S(1)}, u32[]{:S(2)}, u32[]{:S(2)}) collective-permute-start(bf16[2,128,1024]{2,1,0:T(8,128)(2,1)S(1)} %pad_maximum_fusion.1.refs_0_), channel_id=1, source_target_pairs={{4,12},{6,14},{12,20},{14,22},{20,28},{22,30},{28,24},{30,26},{24,... | collective-permute-start | bytes 1572872 | tf_op jit(solution)/shard_map/ppermute | solution.py:134
  30.5 3.5 %collective-permute-done.2.refs_3_ = bf16[2,4,128,128]{3,2,1,0:T(8,128)(2,1)S(1)} collective-permute-done((bf16[2,4,128,128]{3,2,1,0:T(8,128)(2,1)S(1)}, bf16[2,4,128,128]{3,2,1,0:T(8,128)(2,1)S(1)}, u32[]{:S(2)}, u32[]{:S(2)}) %collective-permute-start.2) | collective-permute-done | bytes 262176 | tf_op jit(solution)/shard_map/ppermute | solution.py:134
  35.7 1.6 %collective-permute-start.17 = (bf16[2,128,1024]{2,1,0:T(8,128)(2,1)S(1)}, bf16[2,128,1024]{2,1,0:T(8,128)(2,1)S(1)}, u32[]{:S(2)}, u32[]{:S(2)}) collective-permute-start(bf16[2,128,1024]{2,1,0:T(8,128)(2,1)S(1)} %collective-permute-done.15.refs_1_), channel_id=1, source_target_pairs={{4,12},{6,14},{12,20},{14,22},{20,28},{22,30},{28,24},{30,26},{24,... | collective-permute-start | bytes 1572872 | tf_op jit(solution)/shard_map/ppermute | solution.py:134
  37.8 14.7 %collective-permute-done.5.refs_13_ = bf16[2,4,128,128]{3,2,1,0:T(8,128)(2,1)S(1)} collective-permute-done((bf16[2,4,128,128]{3,2,1,0:T(8,128)(2,1)S(1)}, bf16[2,4,128,128]{3,2,1,0:T(8,128)(2,1)S(1)}, u32[]{:S(2)}, u32[]{:S(2)}) %collective-permute-start.5) | collective-permute-done | bytes 262176 | tf_op jit(solution)/shard_map/ppermute | solution.py:134
  52.5 1.6 %collective-permute-start.20 = (bf16[2,4,128,128]{3,2,1,0:T(8,128)(2,1)S(1)}, bf16[2,4,128,128]{3,2,1,0:T(8,128)(2,1)S(1)}, u32[]{:S(2)}, u32[]{:S(2)}) collective-permute-start(bf16[2,4,128,128]{3,2,1,0:T(8,128)(2,1)S(1)} %collective-permute-done.11.refs_10_), channel_id=1, source_target_pairs={{4,12},{6,14},{12,20},{14,22},{20,28},{22,30},{28,24},{30,26},{24,... | collective-permute-start | bytes 786440 | tf_op jit(solution)/shard_map/ppermute | solution.py:134
  54.1 1.6 %collective-permute-start.19 = (bf16[2,4,128,128]{3,2,1,0:T(8,128)(2,1)S(1)}, bf16[2,4,128,128]{3,2,1,0:T(8,128)(2,1)S(1)}, u32[]{:S(2)}, u32[]{:S(2)}) collective-permute-start(bf16[2,4,128,128]{3,2,1,0:T(8,128)(2,1)S(1)} %collective-permute-done.2.refs_3_), channel_id=1, source_target_pairs={{4,12},{6,14},{12,20},{14,22},{20,28},{22,30},{28,24},{30,26},{24,... | collective-permute-start | bytes 786440 | tf_op jit(solution)/shard_map/ppermute | solution.py:134
  58.1 5.7 %collective-permute-done.18.refs_5_ = bf16[2,128,1024]{2,1,0:T(8,128)(2,1)S(1)} collective-permute-done((bf16[2,128,1024]{2,1,0:T(8,128)(2,1)S(1)}, bf16[2,128,1024]{2,1,0:T(8,128)(2,1)S(1)}, u32[]{:S(2)}, u32[]{:S(2)}) %collective-permute-start.18) | collective-permute-done | bytes 524320 | tf_op jit(solution)/shard_map/ppermute | solution.py:134
  64.2 3.5 %collective-permute-done.19.refs_4_ = bf16[2,4,128,128]{3,2,1,0:T(8,128)(2,1)S(1)} collective-permute-done((bf16[2,4,128,128]{3,2,1,0:T(8,128)(2,1)S(1)}, bf16[2,4,128,128]{3,2,1,0:T(8,128)(2,1)S(1)}, u32[]{:S(2)}, u32[]{:S(2)}) %collective-permute-start.19) | collective-permute-done | bytes 262176 | tf_op jit(solution)/shard_map/ppermute | solution.py:134
  67.7 1.6 %collective-permute-done.21.refs_12_ = bf16[2,4,128,128]{3,2,1,0:T(8,128)(2,1)S(1)} collective-permute-done((bf16[2,4,128,128]{3,2,1,0:T(8,128)(2,1)S(1)}, bf16[2,4,128,128]{3,2,1,0:T(8,128)(2,1)S(1)}, u32[]{:S(2)}, u32[]{:S(2)}) %collective-permute-start.21) | collective-permute-done | bytes 262176 | tf_op jit(solution)/shard_map/ppermute | solution.py:134
  69.4 5.6 %attend.2 = (f32[128,512]{1,0:T(8,128)S(1)}, f32[128,512]{1,0:T(8,128)S(1)}, f32[128,512]{1,0:T(8,128)S(1)}, f32[128,512]{1,0:T(8,128)S(1)}, f32[128,128]{1,0:T(8,128)S(1)}) custom-call(s32[16]{0:T(128)S(1)} %get-tuple-element.85.ids, s32[16]{0:T(128)S(1)} %get-tuple-element.84.ranks, s32[16]{0:T(128)S(1)} %copy-done.5, s32[1]{0:T(128)} %bitcast.me, ...), custom_call_target="tpu_custom_call" | custom-call | flops 6442450944 | bytes 4194304 | tf_op jit(solution)/shard_map/attend/pallas_call | solution.py:254
  75.1 1.6 %collective-permute-start.29 = (bf16[2,128,1024]{2,1,0:T(8,128)(2,1)S(1)}, bf16[2,128,1024]{2,1,0:T(8,128)(2,1)S(1)}, u32[]{:S(2)}, u32[]{:S(2)}) collective-permute-start(bf16[2,128,1024]{2,1,0:T(8,128)(2,1)S(1)} %collective-permute-done.17.refs_3_), channel_id=1, source_target_pairs={{4,12},{6,14},{12,20},{14,22},{20,28},{22,30},{28,24},{30,26},{24,... | collective-permute-start | bytes 1572872 | tf_op jit(solution)/shard_map/ppermute | solution.py:134
  77.2 1.6 %collective-permute-done.27.refs_6_ = bf16[2,128,1024]{2,1,0:T(8,128)(2,1)S(1)} collective-permute-done((bf16[2,128,1024]{2,1,0:T(8,128)(2,1)S(1)}, bf16[2,128,1024]{2,1,0:T(8,128)(2,1)S(1)}, u32[]{:S(2)}, u32[]{:S(2)}) %collective-permute-start.27) | collective-permute-done | bytes 524320 | tf_op jit(solution)/shard_map/ppermute | solution.py:134
  83.9 6.3 %attend.3 = (f32[128,512]{1,0:T(8,128)S(1)}, f32[128,512]{1,0:T(8,128)S(1)}, f32[128,512]{1,0:T(8,128)S(1)}, f32[128,512]{1,0:T(8,128)S(1)}, f32[128,128]{1,0:T(8,128)S(1)}) custom-call(s32[16]{0:T(128)S(1)} %get-tuple-element.87.ids, s32[16]{0:T(128)S(1)} %get-tuple-element.86.ranks, s32[16]{0:T(128)S(1)} %copy-done.5, s32[1]{0:T(128)} %bitcast.me, ...), custom_call_target="tpu_custom_call" | custom-call | flops 301989888 | bytes 4194304 | tf_op jit(solution)/shard_map/attend/pallas_call | solution.py:254
  91.5 1.8 %combine.1 = bf16[128,2048]{1,0:T(8,128)(2,1)S(1)} custom-call(f32[128,512]{1,0:T(8,128)S(1)} %get-tuple-element.63.refs_0_, f32[128,512]{1,0:T(8,128)S(1)} %get-tuple-element.64.refs_1_, f32[128,512]{1,0:T(8,128)S(1)} %get-tuple-element.65.refs_2_, f32[128,512]{1,0:T(8,128)S(1)} %get-tuple-element.66.refs_3_, f32[128,128]{1,0:T(8,128)S(1)} %get-tuple-element.67.refs_4_, ...), custom_call_target="tpu_custom_call" | custom-call | flops 1048576 | bytes 2621440 | tf_op jit(solution)/shard_map/combine/pallas_call | solution.py:306
  93.3 1.6 %collective-permute-start.32 = (bf16[128,2048]{1,0:T(8,128)(2,1)S(1)}, bf16[128,2048]{1,0:T(8,128)(2,1)S(1)}, u32[]{:S(2)}, u32[]{:S(2)}) collective-permute-start(bf16[128,2048]{1,0:T(8,128)(2,1)S(1)} %combine.1), channel_id=1, source_target_pairs={{0,1},{1,0},{2,3},{3,2},{4,5},{5,4},{6,7},{7,6},{8,9},{9,8},{10,11... | collective-permute-start | bytes 1572872 | tf_op jit(solution)/shard_map/ppermute | solution.py:152
  96.9 4.3 %collective-permute-done.33.refs_0_ = bf16[2,128,1024]{2,1,0:T(8,128)(2,1)S(1)} collective-permute-done((bf16[2,128,1024]{2,1,0:T(8,128)(2,1)S(1)}, bf16[2,128,1024]{2,1,0:T(8,128)(2,1)S(1)}, u32[]{:S(2)}, u32[]{:S(2)}) %collective-permute-start.33) | collective-permute-done | bytes 524320 | tf_op jit(solution)/shard_map/ppermute | solution.py:134
  102.7 3.7 %collective-permute-done.32 = bf16[128,2048]{1,0:T(8,128)(2,1)S(1)} collective-permute-done((bf16[128,2048]{1,0:T(8,128)(2,1)S(1)}, bf16[128,2048]{1,0:T(8,128)(2,1)S(1)}, u32[]{:S(2)}, u32[]{:S(2)}) %collective-permute-start.32) | collective-permute-done | bytes 524320 | tf_op jit(solution)/shard_map/ppermute | solution.py:152
  106.5 1.6 %collective-permute-start.40 = (bf16[1,128,1024]{2,1,0:T(8,128)(2,1)S(1)}, bf16[1,128,1024]{2,1,0:T(8,128)(2,1)S(1)}, u32[]{:S(2)}, u32[]{:S(2)}) collective-permute-start(bf16[1,128,1024]{2,1,0:T(8,128)(2,1)S(1)} %slice.34), channel_id=1, source_target_pairs={{4,12},{6,14},{12,20},{14,22},{20,28},{22,30},{28,24},{30,26},{24,... | collective-permute-start | bytes 786440 | tf_op jit(solution)/shard_map/ppermute | solution.py:134
  108.1 4.4 %collective-permute-done.36.refs_1_ = bf16[2,128,1024]{2,1,0:T(8,128)(2,1)S(1)} collective-permute-done((bf16[2,128,1024]{2,1,0:T(8,128)(2,1)S(1)}, bf16[2,128,1024]{2,1,0:T(8,128)(2,1)S(1)}, u32[]{:S(2)}, u32[]{:S(2)}) %collective-permute-start.36) | collective-permute-done | bytes 524320 | tf_op jit(solution)/shard_map/ppermute | solution.py:134
  115.9 3.0 %project.3.refs_6_ = f32[256,1024]{1,0:T(8,128)S(1)} custom-call(s32[16]{0:T(128)S(1)} %copy-done.5, s32[1]{0:T(128)} %bitcast.me, bf16[256,2048]{1,0:T(8,128)(2,1)S(1)} %pad_maximum_fusion.own_rows, bf16[256,2048]{1,0:T(8,128)(2,1)S(1)} %constant_dynamic-update-slice_fusion.other_rows, bf16[2,128,1024]{2,1,0:T(8,128)(2,1)S(1)} %pad_maximum_fusion.1.refs_0_, ...), custom_call_target="tpu_custom_call" | custom-call | flops 1342177280 | bytes 6291456 | tf_op jit(solution)/shard_map/project/pallas_call | solution.py:369
  119.0 2.8 %collective-permute-done.41.refs_5_ = bf16[1,128,1024]{2,1,0:T(8,128)(2,1)S(1)} collective-permute-done((bf16[1,128,1024]{2,1,0:T(8,128)(2,1)S(1)}, bf16[1,128,1024]{2,1,0:T(8,128)(2,1)S(1)}, u32[]{:S(2)}, u32[]{:S(2)}) %collective-permute-start.41) | collective-permute-done | bytes 262176 | tf_op jit(solution)/shard_map/ppermute | solution.py:134
  121.7 1.9 %project.4.refs_2_ = f32[256,1024]{1,0:T(8,128)S(1)} custom-call(s32[16]{0:T(128)S(1)} %copy-done.5, s32[1]{0:T(128)} %bitcast.me, bf16[256,2048]{1,0:T(8,128)(2,1)S(1)} %pad_maximum_fusion.own_rows, bf16[256,2048]{1,0:T(8,128)(2,1)S(1)} %constant_dynamic-update-slice_fusion.other_rows, bf16[2,128,1024]{2,1,0:T(8,128)(2,1)S(1)} %collective-permute-done.33.refs_0_, ...), custom_call_target="tpu_custom_call" | custom-call | flops 671088640 | bytes 3670016 | tf_op jit(solution)/shard_map/project/pallas_call | solution.py:369
  123.7 2.2 %collective-permute-done.39.refs_1_ = bf16[1,128,1024]{2,1,0:T(8,128)(2,1)S(1)} collective-permute-done((bf16[1,128,1024]{2,1,0:T(8,128)(2,1)S(1)}, bf16[1,128,1024]{2,1,0:T(8,128)(2,1)S(1)}, u32[]{:S(2)}, u32[]{:S(2)}) %collective-permute-start.39) | collective-permute-done | bytes 262176 | tf_op jit(solution)/shard_map/ppermute | solution.py:134
  (95 shorter events, 29.9 us)
Async XLA Ops:
  0.5 10.0 %collective-permute-start = (bf16[2,4,128,128]{3,2,1,0:T(8,128)(2,1)}, bf16[2,4,128,128]{3,2,1,0:T(8,128)(2,1)S(1)}, u32[]{:S(2)}, u32[]{:S(2)}) collective-permute-start(bf16[2,4,128,128]{3,2,1,0:T(8,128)(2,1)} %refs_0_.3), channel_id=1, source_target_pairs={{4,12},{6,14},{12,20},{14,22},{20,28},{22,30},{28,24},{30,26},{24,... | collective-permute-start | bytes 786440 | tf_op jit(solution)/shard_map/ppermute | solution.py:134
  3.0 9.4 %collective-permute-start.8 = (bf16[2,4,128,128]{3,2,1,0:T(8,128)(2,1)}, bf16[2,4,128,128]{3,2,1,0:T(8,128)(2,1)S(1)}, u32[]{:S(2)}, u32[]{:S(2)}) collective-permute-start(bf16[2,4,128,128]{3,2,1,0:T(8,128)(2,1)} %refs_0_.3), channel_id=1, source_target_pairs={{4,0},{6,2},{12,4},{14,6},{20,12},{22,14},{28,20},{30,22},{24,28},... | collective-permute-start | bytes 786440 | tf_op jit(solution)/shard_map/ppermute | solution.py:134
  4.2 19.4 %collective-permute-start.7 = (bf16[128,2048]{1,0:T(8,128)(2,1)S(1)}, bf16[128,2048]{1,0:T(8,128)(2,1)S(1)}, u32[]{:S(2)}, u32[]{:S(2)}) collective-permute-start(bf16[128,2048]{1,0:T(8,128)(2,1)S(1)} %constant_dynamic-slice_fusion), channel_id=1, source_target_pairs={{0,1},{1,0},{2,3},{3,2},{4,5},{5,4},{6,7},{7,6},{8,9},{9,8},{10,11... | collective-permute-start | bytes 1572872 | tf_op jit(solution)/shard_map/ppermute | solution.py:152
  6.2 9.8 %collective-permute-start.10 = (bf16[2,4,128,128]{3,2,1,0:T(8,128)(2,1)S(1)}, bf16[2,4,128,128]{3,2,1,0:T(8,128)(2,1)S(1)}, u32[]{:S(2)}, u32[]{:S(2)}) collective-permute-start(bf16[2,4,128,128]{3,2,1,0:T(8,128)(2,1)S(1)} %copy-done.2), channel_id=1, source_target_pairs={{4,12},{6,14},{12,20},{14,22},{20,28},{22,30},{28,24},{30,26},{24,... | collective-permute-start | bytes 786440 | tf_op jit(solution)/shard_map/ppermute | solution.py:134
  7.7 10.2 %collective-permute-start.3 = (bf16[2,4,128,128]{3,2,1,0:T(8,128)(2,1)S(1)}, bf16[2,4,128,128]{3,2,1,0:T(8,128)(2,1)S(1)}, u32[]{:S(2)}, u32[]{:S(2)}) collective-permute-start(bf16[2,4,128,128]{3,2,1,0:T(8,128)(2,1)S(1)} %copy-done.2), channel_id=1, source_target_pairs={{4,0},{6,2},{12,4},{14,6},{20,12},{22,14},{28,20},{30,22},{24,28},... | collective-permute-start | bytes 786440 | tf_op jit(solution)/shard_map/ppermute | solution.py:134
  10.4 11.2 %collective-permute-start.1 = (bf16[2,4,128,128]{3,2,1,0:T(8,128)(2,1)S(1)}, bf16[2,4,128,128]{3,2,1,0:T(8,128)(2,1)S(1)}, u32[]{:S(2)}, u32[]{:S(2)}) collective-permute-start(bf16[2,4,128,128]{3,2,1,0:T(8,128)(2,1)S(1)} %collective-permute-done.refs_1_), channel_id=1, source_target_pairs={{4,12},{6,14},{12,20},{14,22},{20,28},{22,30},{28,24},{30,26},{24,... | collective-permute-start | bytes 786440 | tf_op jit(solution)/shard_map/ppermute | solution.py:134
  12.4 11.2 %collective-permute-start.9 = (bf16[2,4,128,128]{3,2,1,0:T(8,128)(2,1)S(1)}, bf16[2,4,128,128]{3,2,1,0:T(8,128)(2,1)S(1)}, u32[]{:S(2)}, u32[]{:S(2)}) collective-permute-start(bf16[2,4,128,128]{3,2,1,0:T(8,128)(2,1)S(1)} %collective-permute-done.8.refs_7_), channel_id=1, source_target_pairs={{4,0},{6,2},{12,4},{14,6},{20,12},{22,14},{28,20},{30,22},{24,28},... | collective-permute-start | bytes 786440 | tf_op jit(solution)/shard_map/ppermute | solution.py:134
  16.1 11.0 %collective-permute-start.11 = (bf16[2,4,128,128]{3,2,1,0:T(8,128)(2,1)S(1)}, bf16[2,4,128,128]{3,2,1,0:T(8,128)(2,1)S(1)}, u32[]{:S(2)}, u32[]{:S(2)}) collective-permute-start(bf16[2,4,128,128]{3,2,1,0:T(8,128)(2,1)S(1)} %collective-permute-done.10.refs_9_), channel_id=1, source_target_pairs={{4,12},{6,14},{12,20},{14,22},{20,28},{22,30},{28,24},{30,26},{24,... | collective-permute-start | bytes 786440 | tf_op jit(solution)/shard_map/ppermute | solution.py:134
  18.0 10.5 %collective-permute-start.4 = (bf16[2,4,128,128]{3,2,1,0:T(8,128)(2,1)S(1)}, bf16[2,4,128,128]{3,2,1,0:T(8,128)(2,1)S(1)}, u32[]{:S(2)}, u32[]{:S(2)}) collective-permute-start(bf16[2,4,128,128]{3,2,1,0:T(8,128)(2,1)S(1)} %collective-permute-done.3.refs_15_), channel_id=1, source_target_pairs={{4,0},{6,2},{12,4},{14,6},{20,12},{22,14},{28,20},{30,22},{24,28},... | collective-permute-start | bytes 786440 | tf_op jit(solution)/shard_map/ppermute | solution.py:134
  24.8 10.9 %collective-permute-start.15 = (bf16[2,128,1024]{2,1,0:T(8,128)(2,1)S(1)}, bf16[2,128,1024]{2,1,0:T(8,128)(2,1)S(1)}, u32[]{:S(2)}, u32[]{:S(2)}) collective-permute-start(bf16[2,128,1024]{2,1,0:T(8,128)(2,1)S(1)} %pad_maximum_fusion.2), channel_id=1, source_target_pairs={{0,2},{2,0},{4,6},{6,4},{8,10},{10,8},{12,14},{14,12},{16,18},{18,... | collective-permute-start | bytes 1572872 | tf_op jit(solution)/shard_map/ppermute | solution.py:148
  28.4 25.6 %collective-permute-start.12 = (bf16[2,128,1024]{2,1,0:T(8,128)(2,1)S(1)}, bf16[2,128,1024]{2,1,0:T(8,128)(2,1)S(1)}, u32[]{:S(2)}, u32[]{:S(2)}) collective-permute-start(bf16[2,128,1024]{2,1,0:T(8,128)(2,1)S(1)} %pad_maximum_fusion.1.refs_0_), channel_id=1, source_target_pairs={{4,12},{6,14},{12,20},{14,22},{20,28},{22,30},{28,24},{30,26},{24,... | collective-permute-start | bytes 1572872 | tf_op jit(solution)/shard_map/ppermute | solution.py:134
  30.0 24.1 %collective-permute-start.13 = (bf16[2,128,1024]{2,1,0:T(8,128)(2,1)S(1)}, bf16[2,128,1024]{2,1,0:T(8,128)(2,1)S(1)}, u32[]{:S(2)}, u32[]{:S(2)}) collective-permute-start(bf16[2,128,1024]{2,1,0:T(8,128)(2,1)S(1)} %pad_maximum_fusion.1.refs_0_), channel_id=1, source_target_pairs={{4,0},{6,2},{12,4},{14,6},{20,12},{22,14},{28,20},{30,22},{24,28},... | collective-permute-start | bytes 1572872 | tf_op jit(solution)/shard_map/ppermute | solution.py:134
  34.0 18.5 %collective-permute-start.5 = (bf16[2,4,128,128]{3,2,1,0:T(8,128)(2,1)S(1)}, bf16[2,4,128,128]{3,2,1,0:T(8,128)(2,1)S(1)}, u32[]{:S(2)}, u32[]{:S(2)}) collective-permute-start(bf16[2,4,128,128]{3,2,1,0:T(8,128)(2,1)S(1)} %collective-permute-done.4.refs_14_), channel_id=1, source_target_pairs={{4,0},{6,2},{12,4},{14,6},{20,12},{22,14},{28,20},{30,22},{24,28},... | collective-permute-start | bytes 786440 | tf_op jit(solution)/shard_map/ppermute | solution.py:134
  35.7 20.8 %collective-permute-start.17 = (bf16[2,128,1024]{2,1,0:T(8,128)(2,1)S(1)}, bf16[2,128,1024]{2,1,0:T(8,128)(2,1)S(1)}, u32[]{:S(2)}, u32[]{:S(2)}) collective-permute-start(bf16[2,128,1024]{2,1,0:T(8,128)(2,1)S(1)} %collective-permute-done.15.refs_1_), channel_id=1, source_target_pairs={{4,12},{6,14},{12,20},{14,22},{20,28},{22,30},{28,24},{30,26},{24,... | collective-permute-start | bytes 1572872 | tf_op jit(solution)/shard_map/ppermute | solution.py:134
  37.2 26.5 %collective-permute-start.18 = (bf16[2,128,1024]{2,1,0:T(8,128)(2,1)S(1)}, bf16[2,128,1024]{2,1,0:T(8,128)(2,1)S(1)}, u32[]{:S(2)}, u32[]{:S(2)}) collective-permute-start(bf16[2,128,1024]{2,1,0:T(8,128)(2,1)S(1)} %collective-permute-done.15.refs_1_), channel_id=1, source_target_pairs={{4,0},{6,2},{12,4},{14,6},{20,12},{22,14},{28,20},{30,22},{24,28},... | collective-permute-start | bytes 1572872 | tf_op jit(solution)/shard_map/ppermute | solution.py:134
  52.5 11.7 %collective-permute-start.20 = (bf16[2,4,128,128]{3,2,1,0:T(8,128)(2,1)S(1)}, bf16[2,4,128,128]{3,2,1,0:T(8,128)(2,1)S(1)}, u32[]{:S(2)}, u32[]{:S(2)}) collective-permute-start(bf16[2,4,128,128]{3,2,1,0:T(8,128)(2,1)S(1)} %collective-permute-done.11.refs_10_), channel_id=1, source_target_pairs={{4,12},{6,14},{12,20},{14,22},{20,28},{22,30},{28,24},{30,26},{24,... | collective-permute-start | bytes 786440 | tf_op jit(solution)/shard_map/ppermute | solution.py:134
  54.1 13.6 %collective-permute-start.19 = (bf16[2,4,128,128]{3,2,1,0:T(8,128)(2,1)S(1)}, bf16[2,4,128,128]{3,2,1,0:T(8,128)(2,1)S(1)}, u32[]{:S(2)}, u32[]{:S(2)}) collective-permute-start(bf16[2,4,128,128]{3,2,1,0:T(8,128)(2,1)S(1)} %collective-permute-done.2.refs_3_), channel_id=1, source_target_pairs={{4,12},{6,14},{12,20},{14,22},{20,28},{22,30},{28,24},{30,26},{24,... | collective-permute-start | bytes 786440 | tf_op jit(solution)/shard_map/ppermute | solution.py:134
  55.7 13.6 %collective-permute-start.21 = (bf16[2,4,128,128]{3,2,1,0:T(8,128)(2,1)S(1)}, bf16[2,4,128,128]{3,2,1,0:T(8,128)(2,1)S(1)}, u32[]{:S(2)}, u32[]{:S(2)}) collective-permute-start(bf16[2,4,128,128]{3,2,1,0:T(8,128)(2,1)S(1)} %collective-permute-done.5.refs_13_), channel_id=1, source_target_pairs={{4,0},{6,2},{12,4},{14,6},{20,12},{22,14},{28,20},{30,22},{24,28},... | collective-permute-start | bytes 786440 | tf_op jit(solution)/shard_map/ppermute | solution.py:134
  56.5 22.3 %collective-permute-start.27 = (bf16[2,128,1024]{2,1,0:T(8,128)(2,1)S(1)}, bf16[2,128,1024]{2,1,0:T(8,128)(2,1)S(1)}, u32[]{:S(2)}, u32[]{:S(2)}) collective-permute-start(bf16[2,128,1024]{2,1,0:T(8,128)(2,1)S(1)} %collective-permute-done.12.refs_2_), channel_id=1, source_target_pairs={{4,12},{6,14},{12,20},{14,22},{20,28},{22,30},{28,24},{30,26},{24,... | collective-permute-start | bytes 1572872 | tf_op jit(solution)/shard_map/ppermute | solution.py:134
  63.7 16.4 %collective-permute-start.28 = (bf16[2,128,1024]{2,1,0:T(8,128)(2,1)S(1)}, bf16[2,128,1024]{2,1,0:T(8,128)(2,1)S(1)}, u32[]{:S(2)}, u32[]{:S(2)}) collective-permute-start(bf16[2,128,1024]{2,1,0:T(8,128)(2,1)S(1)} %collective-permute-done.13.refs_4_), channel_id=1, source_target_pairs={{4,0},{6,2},{12,4},{14,6},{20,12},{22,14},{28,20},{30,22},{24,28},... | collective-permute-start | bytes 1572872 | tf_op jit(solution)/shard_map/ppermute | solution.py:134
  75.1 15.1 %collective-permute-start.29 = (bf16[2,128,1024]{2,1,0:T(8,128)(2,1)S(1)}, bf16[2,128,1024]{2,1,0:T(8,128)(2,1)S(1)}, u32[]{:S(2)}, u32[]{:S(2)}) collective-permute-start(bf16[2,128,1024]{2,1,0:T(8,128)(2,1)S(1)} %collective-permute-done.17.refs_3_), channel_id=1, source_target_pairs={{4,12},{6,14},{12,20},{14,22},{20,28},{22,30},{28,24},{30,26},{24,... | collective-permute-start | bytes 1572872 | tf_op jit(solution)/shard_map/ppermute | solution.py:134
  76.7 14.8 %collective-permute-start.30 = (bf16[2,128,1024]{2,1,0:T(8,128)(2,1)S(1)}, bf16[2,128,1024]{2,1,0:T(8,128)(2,1)S(1)}, u32[]{:S(2)}, u32[]{:S(2)}) collective-permute-start(bf16[2,128,1024]{2,1,0:T(8,128)(2,1)S(1)} %collective-permute-done.18.refs_5_), channel_id=1, source_target_pairs={{4,0},{6,2},{12,4},{14,6},{20,12},{22,14},{28,20},{30,22},{24,28},... | collective-permute-start | bytes 1572872 | tf_op jit(solution)/shard_map/ppermute | solution.py:134
  81.9 19.4 %collective-permute-start.33 = (bf16[2,128,1024]{2,1,0:T(8,128)(2,1)S(1)}, bf16[2,128,1024]{2,1,0:T(8,128)(2,1)S(1)}, u32[]{:S(2)}, u32[]{:S(2)}) collective-permute-start(bf16[2,128,1024]{2,1,0:T(8,128)(2,1)S(1)} %collective-permute-done.27.refs_6_), channel_id=1, source_target_pairs={{4,12},{6,14},{12,20},{14,22},{20,28},{22,30},{28,24},{30,26},{24,... | collective-permute-start | bytes 1572872 | tf_op jit(solution)/shard_map/ppermute | solution.py:134
  83.5 19.3 %collective-permute-start.34 = (bf16[2,128,1024]{2,1,0:T(8,128)(2,1)S(1)}, bf16[2,128,1024]{2,1,0:T(8,128)(2,1)S(1)}, u32[]{:S(2)}, u32[]{:S(2)}) collective-permute-start(bf16[2,128,1024]{2,1,0:T(8,128)(2,1)S(1)} %collective-permute-done.28.refs_8_), channel_id=1, source_target_pairs={{4,0},{6,2},{12,4},{14,6},{20,12},{22,14},{28,20},{30,22},{24,28},... | collective-permute-start | bytes 1572872 | tf_op jit(solution)/shard_map/ppermute | solution.py:134
  93.3 13.1 %collective-permute-start.32 = (bf16[128,2048]{1,0:T(8,128)(2,1)S(1)}, bf16[128,2048]{1,0:T(8,128)(2,1)S(1)}, u32[]{:S(2)}, u32[]{:S(2)}) collective-permute-start(bf16[128,2048]{1,0:T(8,128)(2,1)S(1)} %combine.1), channel_id=1, source_target_pairs={{0,1},{1,0},{2,3},{3,2},{4,5},{5,4},{6,7},{7,6},{8,9},{9,8},{10,11... | collective-permute-start | bytes 1572872 | tf_op jit(solution)/shard_map/ppermute | solution.py:152
  94.9 17.6 %collective-permute-start.36 = (bf16[2,128,1024]{2,1,0:T(8,128)(2,1)S(1)}, bf16[2,128,1024]{2,1,0:T(8,128)(2,1)S(1)}, u32[]{:S(2)}, u32[]{:S(2)}) collective-permute-start(bf16[2,128,1024]{2,1,0:T(8,128)(2,1)S(1)} %collective-permute-done.29.refs_7_), channel_id=1, source_target_pairs={{4,12},{6,14},{12,20},{14,22},{20,28},{22,30},{28,24},{30,26},{24,... | collective-permute-start | bytes 1572872 | tf_op jit(solution)/shard_map/ppermute | solution.py:134
  96.5 17.1 %collective-permute-start.37 = (bf16[2,128,1024]{2,1,0:T(8,128)(2,1)S(1)}, bf16[2,128,1024]{2,1,0:T(8,128)(2,1)S(1)}, u32[]{:S(2)}, u32[]{:S(2)}) collective-permute-start(bf16[2,128,1024]{2,1,0:T(8,128)(2,1)S(1)} %collective-permute-done.30.refs_9_), channel_id=1, source_target_pairs={{4,0},{6,2},{12,4},{14,6},{20,12},{22,14},{28,20},{30,22},{24,28},... | collective-permute-start | bytes 1572872 | tf_op jit(solution)/shard_map/ppermute | solution.py:134
  101.3 13.9 %collective-permute-start.31 = (bf16[128,2048]{1,0:T(8,128)(2,1)S(1)}, bf16[128,2048]{1,0:T(8,128)(2,1)S(1)}, u32[]{:S(2)}, u32[]{:S(2)}) collective-permute-start(bf16[128,2048]{1,0:T(8,128)(2,1)S(1)} %combine.1), channel_id=1, source_target_pairs={{0,2},{2,0},{4,6},{6,4},{8,10},{10,8},{12,14},{14,12},{16,18},{18,... | collective-permute-start | bytes 1572872 | tf_op jit(solution)/shard_map/ppermute | solution.py:148
  106.5 9.4 %collective-permute-start.35 = (bf16[128,2048]{1,0:T(8,128)(2,1)S(1)}, bf16[128,2048]{1,0:T(8,128)(2,1)S(1)}, u32[]{:S(2)}, u32[]{:S(2)}) collective-permute-start(bf16[128,2048]{1,0:T(8,128)(2,1)S(1)} %collective-permute-done.32), channel_id=1, source_target_pairs={{0,2},{2,0},{4,6},{6,4},{8,10},{10,8},{12,14},{14,12},{16,18},{18,... | collective-permute-start | bytes 1572872 | tf_op jit(solution)/shard_map/ppermute | solution.py:148
  106.5 12.5 %collective-permute-start.40 = (bf16[1,128,1024]{2,1,0:T(8,128)(2,1)S(1)}, bf16[1,128,1024]{2,1,0:T(8,128)(2,1)S(1)}, u32[]{:S(2)}, u32[]{:S(2)}) collective-permute-start(bf16[1,128,1024]{2,1,0:T(8,128)(2,1)S(1)} %slice.34), channel_id=1, source_target_pairs={{4,12},{6,14},{12,20},{14,22},{20,28},{22,30},{28,24},{30,26},{24,... | collective-permute-start | bytes 786440 | tf_op jit(solution)/shard_map/ppermute | solution.py:134
  113.5 10.1 %collective-permute-start.38 = (bf16[1,128,1024]{2,1,0:T(8,128)(2,1)S(1)}, bf16[1,128,1024]{2,1,0:T(8,128)(2,1)S(1)}, u32[]{:S(2)}, u32[]{:S(2)}) collective-permute-start(bf16[1,128,1024]{2,1,0:T(8,128)(2,1)S(1)} %slice.32), channel_id=1, source_target_pairs={{4,12},{6,14},{12,20},{14,22},{20,28},{22,30},{28,24},{30,26},{24,... | collective-permute-start | bytes 786440 | tf_op jit(solution)/shard_map/ppermute | solution.py:134
  115.2 10.7 %collective-permute-start.39 = (bf16[1,128,1024]{2,1,0:T(8,128)(2,1)S(1)}, bf16[1,128,1024]{2,1,0:T(8,128)(2,1)S(1)}, u32[]{:S(2)}, u32[]{:S(2)}) collective-permute-start(bf16[1,128,1024]{2,1,0:T(8,128)(2,1)S(1)} %slice.33), channel_id=1, source_target_pairs={{4,0},{6,2},{12,4},{14,6},{20,12},{22,14},{28,20},{30,22},{24,28},... | collective-permute-start | bytes 786440 | tf_op jit(solution)/shard_map/ppermute | solution.py:134
  (19 other events, 200.0 us)
where the time goes:
time: 130 us; the launch traced here: 129 us
  waiting for transfers between devices  68.8 us (53%)
  starting transfers between devices  37 us (28%)
  Pallas kernels  19.5 us (15%)
  local copies, waits for them, and re-layouts  2.38 us (2%)
  other arithmetic  1.33 us (1%)
    ppermute x30, waiting for transfers between devices, shift(): return lax.ppermute(value, 'pool', pairs)  62.2 us
    ppermute x30, starting transfers between devices, shift(): return lax.ppermute(value, 'pool', pairs)  32.2 us
    pallas_call x2, Pallas kernels, attend(): pl.pallas_call(functools.partial(attend_kernel, pieces, owned), out_shape...  11.9 us
    pallas_call x3, Pallas kernels, project(): pl.pallas_call(functools.partial(project_kernel, items, base is not None)...  5.83 us
    ppermute x2, waiting for transfers between devices, swap_plane(): return lax.ppermute(value, 'head', [(0, 1), (1, 0)])  3.75 us
    ppermute x2, starting transfers between devices, swap_plane(): return lax.ppermute(value, 'head', [(0, 1), (1, 0)])  3.59 us
    ppermute x11, waiting for transfers between devices, swap_core(): return lax.ppermute(value, 'pool', [(at, at ^ 1) for at in range(pool)])  2.79 us
  transfers between devices with their start and end apart: 43, of which 24 were waited for; matrix products, arithmetic and copies ran while one was open for 2% of the time, Pallas kernels for 14%

commit v1 on v0

--- a/solution.py
+++ b/solution.py
@@ -315,23 +315,20 @@
 
 
 def project_kernel(items, based, ring, me, own_rows, other_rows, *refs):
-    count = sum(number for _, _, number in items)
+    count = sum(len(heights) for _, _, heights in items)
     blocks, refs = refs[:count], refs[count:]
     base = None
     if based:
         base, refs = refs[0], refs[1:]
     results, (held, total, sems) = refs[:-3], refs[-3:]
-    span = held.shape[2]
+    span = held.shape[1] // 2
     copies, at = [], 0
-    for item, (_, _, number) in enumerate(items):
-        targets = [held.at[item]] if number == 1 else [held.at[item, pl.ds(i, 1)] for i in range(number)]
-        copies.append(
-            [
-                pltpu.make_async_copy(blocks[at + i], target, sems.at[at + i])
-                for i, target in enumerate(targets)
-            ]
-        )
-        at += number
+    for item, (_, _, heights) in enumerate(items):
+        copies.append([])
+        for i, height in enumerate(heights):
+            target = held.at[item, pl.ds(sum(heights[:i]), height)]
+            copies[-1].append(pltpu.make_async_copy(blocks[at], target, sems.at[at]))
+            at += 1
     for group in copies:
         for copy in group:
             copy.start()
@@ -344,7 +341,7 @@
         columns = pl.ds(pl.multiple_of(home * span, span), span)
         value = jnp.dot(
             jnp.concatenate([rows[:, columns] for rows in (own_rows, other_rows)], axis=1),
-            jnp.concatenate([held[item, plane] for plane in range(2)], axis=0),
+            held[item],
             preferred_element_type=jnp.float32,
         )
         if item:
@@ -359,11 +356,15 @@
 
 
 def project(ring, me, rows, blocks, base, shapes):
-    items = tuple((place, crossed, len(parts)) for (place, crossed), parts in blocks.items())
-    flat = [part for parts in blocks.values() for part in parts]
-    tokens = rows[0].shape[0]
-    span, width = flat[0].shape[1:]
-    size = len(items) * 2 * span * width
+    flat = [part.reshape(-1, part.shape[-1]) for parts in blocks.values() for part in parts]
+    heights = iter([part.shape[0] for part in flat])
+    items = tuple(
+        (place, crossed, tuple(next(heights) for _ in parts))
+        for (place, crossed), parts in blocks.items()
+    )
+    tokens, width = rows[0].shape[0], flat[0].shape[1]
+    height = sum(items[0][2])
+    size = len(items) * height * width
     smem = pl.BlockSpec(memory_space=pltpu.SMEM)
     vmem = pl.BlockSpec(memory_space=pltpu.VMEM)
     return pl.pallas_call(
@@ -375,7 +376,7 @@
         + ([vmem] if base is not None else []),
         out_specs=[vmem] * len(shapes),
         scratch_shapes=[
-            pltpu.VMEM((len(items), 2, span, width), jnp.bfloat16),
+            pltpu.VMEM((len(items), height, width), jnp.bfloat16),
             pltpu.VMEM((tokens, width), jnp.float32),
             pltpu.SemaphoreType.DMA((len(flat),)),
         ],
@@ -485,15 +486,15 @@
     turned = after(swap_plane(attended), near[3], near[chips - 3])
     quarters = {}
 
-    def last(crossed):
-        part = heavy[crossed]
-        quarters[(half, crossed)] = (
-            shift(part[half - 1][:1], order, 1),
-            shift(part[half + 1][1:], order, -1),
+    def last(crossed, cut):
+        ahead, back = (
+            heavy[crossed][at].reshape(-1, width) for at in (half - 1, half + 1)
         )
-
-    last(0)
-    last(1)
+        quarters[(half, crossed)] = (shift(ahead[:cut], order, 1), shift(back[cut:], order, -1))
+
+    rows_held = CORES * heavy[0][0].shape[1]
+    last(0, rows_held * 9 // 16)
+    last(1, rows_held * 8 // 16)
     crossed_rows = swap_core(turned, pool)
     crossed_rows = after(crossed_rows, far[3], far[chips - 3])
     rows = [

time: 130 us -> 128 us (0.985)
  waiting for transfers between devices: 68.8 us -> 67.3 us
    ppermute x2, waiting for transfers between devices: 3.75 us -> 2.15 us  [swap_plane(): return lax.ppermute(value, 'head', [(0, 1), (1, 0)])]
  transfers between devices with their start and end apart: 43 -> 43, of which waited for: 24 -> 24; matrix products, arithmetic and copies ran while one was open for 2% -> 2% of each run, Pallas kernels for 14% -> 15%
where the time goes in v1:
time: 128 us
  waiting for transfers between devices  67.3 us (53%)
  starting transfers between devices  36.4 us (28%)
  Pallas kernels  19.9 us (16%)
  local copies, waits for them, and re-layouts  2.38 us (2%)
  other arithmetic  1.33 us (1%)
    ppermute x30, waiting for transfers between devices, shift(): return lax.ppermute(value, 'pool', pairs)  62.7 us
    ppermute x30, starting transfers between devices, shift(): return lax.ppermute(value, 'pool', pairs)  31.5 us
    pallas_call x2, Pallas kernels, attend(): pl.pallas_call(functools.partial(attend_kernel, pieces, owned), out_shape...  11.9 us
    pallas_call x3, Pallas kernels, project(): pl.pallas_call(functools.partial(project_kernel, items, base is not None)...  6.16 us
    ppermute x2, starting transfers between devices, swap_plane(): return lax.ppermute(value, 'head', [(0, 1), (1, 0)])  3.59 us
  transfers between devices with their start and end apart: 43, of which 24 were waited for; matrix products, arithmetic and copies ran while one was open for 2% of the time, Pallas kernels for 15%

profile of v1, /device:TPU:0, one launch (start us, length us, event | category | flops | bytes accessed | tf_op | source)
XLA Modules:
  0.0 127.6 jit_solution(14883352693399962917)
XLA Ops:
  0.5 2.5 %collective-permute-start = (bf16[2,4,128,128]{3,2,1,0:T(8,128)(2,1)}, bf16[2,4,128,128]{3,2,1,0:T(8,128)(2,1)S(1)}, u32[]{:S(2)}, u32[]{:S(2)}) collective-permute-start(bf16[2,4,128,128]{3,2,1,0:T(8,128)(2,1)} %refs_0_.3), channel_id=1, source_target_pairs={{4,12},{6,14},{12,20},{14,22},{20,28},{22,30},{28,24},{30,26},{24,... | collective-permute-start | bytes 786440 | tf_op jit(solution)/shard_map/ppermute | solution.py:134
  4.2 2.0 %collective-permute-start.7 = (bf16[128,2048]{1,0:T(8,128)(2,1)S(1)}, bf16[128,2048]{1,0:T(8,128)(2,1)S(1)}, u32[]{:S(2)}, u32[]{:S(2)}) collective-permute-start(bf16[128,2048]{1,0:T(8,128)(2,1)S(1)} %constant_dynamic-slice_fusion), channel_id=1, source_target_pairs={{0,1},{1,0},{2,3},{3,2},{4,5},{5,4},{6,7},{7,6},{8,9},{9,8},{10,11... | collective-permute-start | bytes 1572872 | tf_op jit(solution)/shard_map/ppermute | solution.py:152
  8.3 2.2 %collective-permute-done.refs_1_ = bf16[2,4,128,128]{3,2,1,0:T(8,128)(2,1)S(1)} collective-permute-done((bf16[2,4,128,128]{3,2,1,0:T(8,128)(2,1)}, bf16[2,4,128,128]{3,2,1,0:T(8,128)(2,1)S(1)}, u32[]{:S(2)}, u32[]{:S(2)}) %collective-permute-start) | collective-permute-done | bytes 262176 | tf_op jit(solution)/shard_map/ppermute | solution.py:134
  10.4 1.9 %collective-permute-start.1 = (bf16[2,4,128,128]{3,2,1,0:T(8,128)(2,1)S(1)}, bf16[2,4,128,128]{3,2,1,0:T(8,128)(2,1)S(1)}, u32[]{:S(2)}, u32[]{:S(2)}) collective-permute-start(bf16[2,4,128,128]{3,2,1,0:T(8,128)(2,1)S(1)} %collective-permute-done.refs_1_), channel_id=1, source_target_pairs={{4,12},{6,14},{12,20},{14,22},{20,28},{22,30},{28,24},{30,26},{24,... | collective-permute-start | bytes 786440 | tf_op jit(solution)/shard_map/ppermute | solution.py:134
  12.5 3.6 %collective-permute-done.10.refs_9_ = bf16[2,4,128,128]{3,2,1,0:T(8,128)(2,1)S(1)} collective-permute-done((bf16[2,4,128,128]{3,2,1,0:T(8,128)(2,1)S(1)}, bf16[2,4,128,128]{3,2,1,0:T(8,128)(2,1)S(1)}, u32[]{:S(2)}, u32[]{:S(2)}) %collective-permute-start.10) | collective-permute-done | bytes 262176 | tf_op jit(solution)/shard_map/ppermute | solution.py:134
  16.1 1.9 %collective-permute-start.11 = (bf16[2,4,128,128]{3,2,1,0:T(8,128)(2,1)S(1)}, bf16[2,4,128,128]{3,2,1,0:T(8,128)(2,1)S(1)}, u32[]{:S(2)}, u32[]{:S(2)}) collective-permute-start(bf16[2,4,128,128]{3,2,1,0:T(8,128)(2,1)S(1)} %collective-permute-done.10.refs_9_), channel_id=1, source_target_pairs={{4,12},{6,14},{12,20},{14,22},{20,28},{22,30},{28,24},{30,26},{24,... | collective-permute-start | bytes 786440 | tf_op jit(solution)/shard_map/ppermute | solution.py:134
  18.1 3.6 %collective-permute-done.1.refs_2_ = bf16[2,4,128,128]{3,2,1,0:T(8,128)(2,1)S(1)} collective-permute-done((bf16[2,4,128,128]{3,2,1,0:T(8,128)(2,1)S(1)}, bf16[2,4,128,128]{3,2,1,0:T(8,128)(2,1)S(1)}, u32[]{:S(2)}, u32[]{:S(2)}) %collective-permute-start.1) | collective-permute-done | bytes 262176 | tf_op jit(solution)/shard_map/ppermute | solution.py:134
  21.7 1.9 %collective-permute-done.9.refs_6_ = bf16[2,4,128,128]{3,2,1,0:T(8,128)(2,1)S(1)} collective-permute-done((bf16[2,4,128,128]{3,2,1,0:T(8,128)(2,1)S(1)}, bf16[2,4,128,128]{3,2,1,0:T(8,128)(2,1)S(1)}, u32[]{:S(2)}, u32[]{:S(2)}) %collective-permute-start.9) | collective-permute-done | bytes 262176 | tf_op jit(solution)/shard_map/ppermute | solution.py:134
  24.9 1.6 %collective-permute-start.2 = (bf16[2,4,128,128]{3,2,1,0:T(8,128)(2,1)S(1)}, bf16[2,4,128,128]{3,2,1,0:T(8,128)(2,1)S(1)}, u32[]{:S(2)}, u32[]{:S(2)}) collective-permute-start(bf16[2,4,128,128]{3,2,1,0:T(8,128)(2,1)S(1)} %collective-permute-done.1.refs_2_), channel_id=1, source_target_pairs={{4,12},{6,14},{12,20},{14,22},{20,28},{22,30},{28,24},{30,26},{24,... | collective-permute-start | bytes 786440 | tf_op jit(solution)/shard_map/ppermute | solution.py:134
  28.4 1.6 %collective-permute-start.12 = (bf16[2,128,1024]{2,1,0:T(8,128)(2,1)S(1)}, bf16[2,128,1024]{2,1,0:T(8,128)(2,1)S(1)}, u32[]{:S(2)}, u32[]{:S(2)}) collective-permute-start(bf16[2,128,1024]{2,1,0:T(8,128)(2,1)S(1)} %pad_maximum_fusion.1), channel_id=1, source_target_pairs={{4,12},{6,14},{12,20},{14,22},{20,28},{22,30},{28,24},{30,26},{24,... | collective-permute-start | bytes 1572872 | tf_op jit(solution)/shard_map/ppermute | solution.py:134
  30.5 3.5 %collective-permute-done.2.refs_3_ = bf16[2,4,128,128]{3,2,1,0:T(8,128)(2,1)S(1)} collective-permute-done((bf16[2,4,128,128]{3,2,1,0:T(8,128)(2,1)S(1)}, bf16[2,4,128,128]{3,2,1,0:T(8,128)(2,1)S(1)}, u32[]{:S(2)}, u32[]{:S(2)}) %collective-permute-start.2) | collective-permute-done | bytes 262176 | tf_op jit(solution)/shard_map/ppermute | solution.py:134
  35.7 1.6 %collective-permute-start.17 = (bf16[2,128,1024]{2,1,0:T(8,128)(2,1)S(1)}, bf16[2,128,1024]{2,1,0:T(8,128)(2,1)S(1)}, u32[]{:S(2)}, u32[]{:S(2)}) collective-permute-start(bf16[2,128,1024]{2,1,0:T(8,128)(2,1)S(1)} %collective-permute-done.15), channel_id=1, source_target_pairs={{4,12},{6,14},{12,20},{14,22},{20,28},{22,30},{28,24},{30,26},{24,... | collective-permute-start | bytes 1572872 | tf_op jit(solution)/shard_map/ppermute | solution.py:134
  37.8 14.7 %collective-permute-done.5.refs_13_ = bf16[2,4,128,128]{3,2,1,0:T(8,128)(2,1)S(1)} collective-permute-done((bf16[2,4,128,128]{3,2,1,0:T(8,128)(2,1)S(1)}, bf16[2,4,128,128]{3,2,1,0:T(8,128)(2,1)S(1)}, u32[]{:S(2)}, u32[]{:S(2)}) %collective-permute-start.5) | collective-permute-done | bytes 262176 | tf_op jit(solution)/shard_map/ppermute | solution.py:134
  52.5 1.6 %collective-permute-start.20 = (bf16[2,4,128,128]{3,2,1,0:T(8,128)(2,1)S(1)}, bf16[2,4,128,128]{3,2,1,0:T(8,128)(2,1)S(1)}, u32[]{:S(2)}, u32[]{:S(2)}) collective-permute-start(bf16[2,4,128,128]{3,2,1,0:T(8,128)(2,1)S(1)} %collective-permute-done.11.refs_10_), channel_id=1, source_target_pairs={{4,12},{6,14},{12,20},{14,22},{20,28},{22,30},{28,24},{30,26},{24,... | collective-permute-start | bytes 786440 | tf_op jit(solution)/shard_map/ppermute | solution.py:134
  54.1 1.6 %collective-permute-start.19 = (bf16[2,4,128,128]{3,2,1,0:T(8,128)(2,1)S(1)}, bf16[2,4,128,128]{3,2,1,0:T(8,128)(2,1)S(1)}, u32[]{:S(2)}, u32[]{:S(2)}) collective-permute-start(bf16[2,4,128,128]{3,2,1,0:T(8,128)(2,1)S(1)} %collective-permute-done.2.refs_3_), channel_id=1, source_target_pairs={{4,12},{6,14},{12,20},{14,22},{20,28},{22,30},{28,24},{30,26},{24,... | collective-permute-start | bytes 786440 | tf_op jit(solution)/shard_map/ppermute | solution.py:134
  56.5 1.6 %collective-permute-start.27 = (bf16[2,128,1024]{2,1,0:T(8,128)(2,1)S(1)}, bf16[2,128,1024]{2,1,0:T(8,128)(2,1)S(1)}, u32[]{:S(2)}, u32[]{:S(2)}) collective-permute-start(bf16[2,128,1024]{2,1,0:T(8,128)(2,1)S(1)} %collective-permute-done.12), channel_id=1, source_target_pairs={{4,12},{6,14},{12,20},{14,22},{20,28},{22,30},{28,24},{30,26},{24,... | collective-permute-start | bytes 1572872 | tf_op jit(solution)/shard_map/ppermute | solution.py:134
  58.1 5.7 %collective-permute-done.18 = bf16[2,128,1024]{2,1,0:T(8,128)(2,1)S(1)} collective-permute-done((bf16[2,128,1024]{2,1,0:T(8,128)(2,1)S(1)}, bf16[2,128,1024]{2,1,0:T(8,128)(2,1)S(1)}, u32[]{:S(2)}, u32[]{:S(2)}) %collective-permute-start.18) | collective-permute-done | bytes 524320 | tf_op jit(solution)/shard_map/ppermute | solution.py:134
  64.2 3.5 %collective-permute-done.19.refs_4_ = bf16[2,4,128,128]{3,2,1,0:T(8,128)(2,1)S(1)} collective-permute-done((bf16[2,4,128,128]{3,2,1,0:T(8,128)(2,1)S(1)}, bf16[2,4,128,128]{3,2,1,0:T(8,128)(2,1)S(1)}, u32[]{:S(2)}, u32[]{:S(2)}) %collective-permute-start.19) | collective-permute-done | bytes 262176 | tf_op jit(solution)/shard_map/ppermute | solution.py:134
  67.7 1.6 %collective-permute-done.21.refs_12_ = bf16[2,4,128,128]{3,2,1,0:T(8,128)(2,1)S(1)} collective-permute-done((bf16[2,4,128,128]{3,2,1,0:T(8,128)(2,1)S(1)}, bf16[2,4,128,128]{3,2,1,0:T(8,128)(2,1)S(1)}, u32[]{:S(2)}, u32[]{:S(2)}) %collective-permute-start.21) | collective-permute-done | bytes 262176 | tf_op jit(solution)/shard_map/ppermute | solution.py:134
  69.4 5.6 %attend.2 = (f32[128,512]{1,0:T(8,128)S(1)}, f32[128,512]{1,0:T(8,128)S(1)}, f32[128,512]{1,0:T(8,128)S(1)}, f32[128,512]{1,0:T(8,128)S(1)}, f32[128,128]{1,0:T(8,128)S(1)}) custom-call(s32[16]{0:T(128)S(1)} %get-tuple-element.85.ids, s32[16]{0:T(128)S(1)} %get-tuple-element.84.ranks, s32[16]{0:T(128)S(1)} %copy-done.5, s32[1]{0:T(128)} %bitcast.me, ...), custom_call_target="tpu_custom_call" | custom-call | flops 6442450944 | bytes 4194304 | tf_op jit(solution)/shard_map/attend/pallas_call | solution.py:254
  75.1 1.6 %collective-permute-start.29 = (bf16[2,128,1024]{2,1,0:T(8,128)(2,1)S(1)}, bf16[2,128,1024]{2,1,0:T(8,128)(2,1)S(1)}, u32[]{:S(2)}, u32[]{:S(2)}) collective-permute-start(bf16[2,128,1024]{2,1,0:T(8,128)(2,1)S(1)} %collective-permute-done.17), channel_id=1, source_target_pairs={{4,12},{6,14},{12,20},{14,22},{20,28},{22,30},{28,24},{30,26},{24,... | collective-permute-start | bytes 1572872 | tf_op jit(solution)/shard_map/ppermute | solution.py:134
  77.2 1.6 %collective-permute-done.27 = bf16[2,128,1024]{2,1,0:T(8,128)(2,1)S(1)} collective-permute-done((bf16[2,128,1024]{2,1,0:T(8,128)(2,1)S(1)}, bf16[2,128,1024]{2,1,0:T(8,128)(2,1)S(1)}, u32[]{:S(2)}, u32[]{:S(2)}) %collective-permute-start.27) | collective-permute-done | bytes 524320 | tf_op jit(solution)/shard_map/ppermute | solution.py:134
  83.7 6.3 %attend.3 = (f32[128,512]{1,0:T(8,128)S(1)}, f32[128,512]{1,0:T(8,128)S(1)}, f32[128,512]{1,0:T(8,128)S(1)}, f32[128,512]{1,0:T(8,128)S(1)}, f32[128,128]{1,0:T(8,128)S(1)}) custom-call(s32[16]{0:T(128)S(1)} %get-tuple-element.87.ids, s32[16]{0:T(128)S(1)} %get-tuple-element.86.ranks, s32[16]{0:T(128)S(1)} %copy-done.5, s32[1]{0:T(128)} %bitcast.me, ...), custom_call_target="tpu_custom_call" | custom-call | flops 301989888 | bytes 4194304 | tf_op jit(solution)/shard_map/attend/pallas_call | solution.py:254
  91.5 1.8 %combine.1 = bf16[128,2048]{1,0:T(8,128)(2,1)S(1)} custom-call(f32[128,512]{1,0:T(8,128)S(1)} %get-tuple-element.63.refs_0_, f32[128,512]{1,0:T(8,128)S(1)} %get-tuple-element.64.refs_1_, f32[128,512]{1,0:T(8,128)S(1)} %get-tuple-element.65.refs_2_, f32[128,512]{1,0:T(8,128)S(1)} %get-tuple-element.66.refs_3_, f32[128,128]{1,0:T(8,128)S(1)} %get-tuple-element.67.refs_4_, ...), custom_call_target="tpu_custom_call" | custom-call | flops 1048576 | bytes 2621440 | tf_op jit(solution)/shard_map/combine/pallas_call | solution.py:306
  93.3 1.6 %collective-permute-start.32 = (bf16[128,2048]{1,0:T(8,128)(2,1)S(1)}, bf16[128,2048]{1,0:T(8,128)(2,1)S(1)}, u32[]{:S(2)}, u32[]{:S(2)}) collective-permute-start(bf16[128,2048]{1,0:T(8,128)(2,1)S(1)} %combine.1), channel_id=1, source_target_pairs={{0,1},{1,0},{2,3},{3,2},{4,5},{5,4},{6,7},{7,6},{8,9},{9,8},{10,11... | collective-permute-start | bytes 1572872 | tf_op jit(solution)/shard_map/ppermute | solution.py:152
  94.9 1.6 %collective-permute-start.36 = (bf16[2,128,1024]{2,1,0:T(8,128)(2,1)S(1)}, bf16[2,128,1024]{2,1,0:T(8,128)(2,1)S(1)}, u32[]{:S(2)}, u32[]{:S(2)}) collective-permute-start(bf16[2,128,1024]{2,1,0:T(8,128)(2,1)S(1)} %collective-permute-done.29), channel_id=1, source_target_pairs={{4,12},{6,14},{12,20},{14,22},{20,28},{22,30},{28,24},{30,26},{24,... | collective-permute-start | bytes 1572872 | tf_op jit(solution)/shard_map/ppermute | solution.py:134
  96.9 4.3 %collective-permute-done.33 = bf16[2,128,1024]{2,1,0:T(8,128)(2,1)S(1)} collective-permute-done((bf16[2,128,1024]{2,1,0:T(8,128)(2,1)S(1)}, bf16[2,128,1024]{2,1,0:T(8,128)(2,1)S(1)}, u32[]{:S(2)}, u32[]{:S(2)}) %collective-permute-start.33) | collective-permute-done | bytes 524320 | tf_op jit(solution)/shard_map/ppermute | solution.py:134
  104.3 2.1 %collective-permute-done.32 = bf16[128,2048]{1,0:T(8,128)(2,1)S(1)} collective-permute-done((bf16[128,2048]{1,0:T(8,128)(2,1)S(1)}, bf16[128,2048]{1,0:T(8,128)(2,1)S(1)}, u32[]{:S(2)}, u32[]{:S(2)}) %collective-permute-start.32) | collective-permute-done | bytes 524320 | tf_op jit(solution)/shard_map/ppermute | solution.py:152
  107.0 5.5 %collective-permute-done.36 = bf16[2,128,1024]{2,1,0:T(8,128)(2,1)S(1)} collective-permute-done((bf16[2,128,1024]{2,1,0:T(8,128)(2,1)S(1)}, bf16[2,128,1024]{2,1,0:T(8,128)(2,1)S(1)}, u32[]{:S(2)}, u32[]{:S(2)}) %collective-permute-start.36) | collective-permute-done | bytes 524320 | tf_op jit(solution)/shard_map/ppermute | solution.py:134
  116.2 3.0 %project.3.refs_6_ = f32[256,1024]{1,0:T(8,128)S(1)} custom-call(s32[16]{0:T(128)S(1)} %copy-done.5, s32[1]{0:T(128)} %bitcast.me, bf16[256,2048]{1,0:T(8,128)(2,1)S(1)} %pad_maximum_fusion.own_rows, bf16[256,2048]{1,0:T(8,128)(2,1)S(1)} %constant_dynamic-update-slice_fusion.other_rows, bf16[256,1024]{1,0:T(8,128)(2,1)S(1)} %bitcast.40, ...), custom_call_target="tpu_custom_call" | custom-call | flops 1342177280 | bytes 6291456 | tf_op jit(solution)/shard_map/project/pallas_call | solution.py:370
  119.3 2.2 %project.4.refs_2_ = f32[256,1024]{1,0:T(8,128)S(1)} custom-call(s32[16]{0:T(128)S(1)} %copy-done.5, s32[1]{0:T(128)} %bitcast.me, bf16[256,2048]{1,0:T(8,128)(2,1)S(1)} %pad_maximum_fusion.own_rows, bf16[256,2048]{1,0:T(8,128)(2,1)S(1)} %constant_dynamic-update-slice_fusion.other_rows, bf16[256,1024]{1,0:T(8,128)(2,1)S(1)} %bitcast.42, ...), custom_call_target="tpu_custom_call" | custom-call | flops 671088640 | bytes 3670016 | tf_op jit(solution)/shard_map/project/pallas_call | solution.py:370
  121.5 2.6 %collective-permute-done.38.refs_0_ = bf16[128,1024]{1,0:T(8,128)(2,1)S(1)} collective-permute-done((bf16[128,1024]{1,0:T(8,128)(2,1)S(1)}, bf16[128,1024]{1,0:T(8,128)(2,1)S(1)}, u32[]{:S(2)}, u32[]{:S(2)}) %collective-permute-start.38) | collective-permute-done | bytes 262176 | tf_op jit(solution)/shard_map/ppermute | solution.py:134
  (95 shorter events, 29.1 us)
Async XLA Ops:
  0.5 10.0 %collective-permute-start = (bf16[2,4,128,128]{3,2,1,0:T(8,128)(2,1)}, bf16[2,4,128,128]{3,2,1,0:T(8,128)(2,1)S(1)}, u32[]{:S(2)}, u32[]{:S(2)}) collective-permute-start(bf16[2,4,128,128]{3,2,1,0:T(8,128)(2,1)} %refs_0_.3), channel_id=1, source_target_pairs={{4,12},{6,14},{12,20},{14,22},{20,28},{22,30},{28,24},{30,26},{24,... | collective-permute-start | bytes 786440 | tf_op jit(solution)/shard_map/ppermute | solution.py:134
  3.0 9.4 %collective-permute-start.8 = (bf16[2,4,128,128]{3,2,1,0:T(8,128)(2,1)}, bf16[2,4,128,128]{3,2,1,0:T(8,128)(2,1)S(1)}, u32[]{:S(2)}, u32[]{:S(2)}) collective-permute-start(bf16[2,4,128,128]{3,2,1,0:T(8,128)(2,1)} %refs_0_.3), channel_id=1, source_target_pairs={{4,0},{6,2},{12,4},{14,6},{20,12},{22,14},{28,20},{30,22},{24,28},... | collective-permute-start | bytes 786440 | tf_op jit(solution)/shard_map/ppermute | solution.py:134
  4.2 19.4 %collective-permute-start.7 = (bf16[128,2048]{1,0:T(8,128)(2,1)S(1)}, bf16[128,2048]{1,0:T(8,128)(2,1)S(1)}, u32[]{:S(2)}, u32[]{:S(2)}) collective-permute-start(bf16[128,2048]{1,0:T(8,128)(2,1)S(1)} %constant_dynamic-slice_fusion), channel_id=1, source_target_pairs={{0,1},{1,0},{2,3},{3,2},{4,5},{5,4},{6,7},{7,6},{8,9},{9,8},{10,11... | collective-permute-start | bytes 1572872 | tf_op jit(solution)/shard_map/ppermute | solution.py:152
  6.2 9.8 %collective-permute-start.10 = (bf16[2,4,128,128]{3,2,1,0:T(8,128)(2,1)S(1)}, bf16[2,4,128,128]{3,2,1,0:T(8,128)(2,1)S(1)}, u32[]{:S(2)}, u32[]{:S(2)}) collective-permute-start(bf16[2,4,128,128]{3,2,1,0:T(8,128)(2,1)S(1)} %copy-done.2), channel_id=1, source_target_pairs={{4,12},{6,14},{12,20},{14,22},{20,28},{22,30},{28,24},{30,26},{24,... | collective-permute-start | bytes 786440 | tf_op jit(solution)/shard_map/ppermute | solution.py:134
  7.7 10.2 %collective-permute-start.3 = (bf16[2,4,128,128]{3,2,1,0:T(8,128)(2,1)S(1)}, bf16[2,4,128,128]{3,2,1,0:T(8,128)(2,1)S(1)}, u32[]{:S(2)}, u32[]{:S(2)}) collective-permute-start(bf16[2,4,128,128]{3,2,1,0:T(8,128)(2,1)S(1)} %copy-done.2), channel_id=1, source_target_pairs={{4,0},{6,2},{12,4},{14,6},{20,12},{22,14},{28,20},{30,22},{24,28},... | collective-permute-start | bytes 786440 | tf_op jit(solution)/shard_map/ppermute | solution.py:134
  10.4 11.2 %collective-permute-start.1 = (bf16[2,4,128,128]{3,2,1,0:T(8,128)(2,1)S(1)}, bf16[2,4,128,128]{3,2,1,0:T(8,128)(2,1)S(1)}, u32[]{:S(2)}, u32[]{:S(2)}) collective-permute-start(bf16[2,4,128,128]{3,2,1,0:T(8,128)(2,1)S(1)} %collective-permute-done.refs_1_), channel_id=1, source_target_pairs={{4,12},{6,14},{12,20},{14,22},{20,28},{22,30},{28,24},{30,26},{24,... | collective-permute-start | bytes 786440 | tf_op jit(solution)/shard_map/ppermute | solution.py:134
  12.4 11.2 %collective-permute-start.9 = (bf16[2,4,128,128]{3,2,1,0:T(8,128)(2,1)S(1)}, bf16[2,4,128,128]{3,2,1,0:T(8,128)(2,1)S(1)}, u32[]{:S(2)}, u32[]{:S(2)}) collective-permute-start(bf16[2,4,128,128]{3,2,1,0:T(8,128)(2,1)S(1)} %collective-permute-done.8.refs_7_), channel_id=1, source_target_pairs={{4,0},{6,2},{12,4},{14,6},{20,12},{22,14},{28,20},{30,22},{24,28},... | collective-permute-start | bytes 786440 | tf_op jit(solution)/shard_map/ppermute | solution.py:134
  16.1 11.0 %collective-permute-start.11 = (bf16[2,4,128,128]{3,2,1,0:T(8,128)(2,1)S(1)}, bf16[2,4,128,128]{3,2,1,0:T(8,128)(2,1)S(1)}, u32[]{:S(2)}, u32[]{:S(2)}) collective-permute-start(bf16[2,4,128,128]{3,2,1,0:T(8,128)(2,1)S(1)} %collective-permute-done.10.refs_9_), channel_id=1, source_target_pairs={{4,12},{6,14},{12,20},{14,22},{20,28},{22,30},{28,24},{30,26},{24,... | collective-permute-start | bytes 786440 | tf_op jit(solution)/shard_map/ppermute | solution.py:134
  18.0 10.5 %collective-permute-start.4 = (bf16[2,4,128,128]{3,2,1,0:T(8,128)(2,1)S(1)}, bf16[2,4,128,128]{3,2,1,0:T(8,128)(2,1)S(1)}, u32[]{:S(2)}, u32[]{:S(2)}) collective-permute-start(bf16[2,4,128,128]{3,2,1,0:T(8,128)(2,1)S(1)} %collective-permute-done.3.refs_15_), channel_id=1, source_target_pairs={{4,0},{6,2},{12,4},{14,6},{20,12},{22,14},{28,20},{30,22},{24,28},... | collective-permute-start | bytes 786440 | tf_op jit(solution)/shard_map/ppermute | solution.py:134
  24.8 10.9 %collective-permute-start.15 = (bf16[2,128,1024]{2,1,0:T(8,128)(2,1)S(1)}, bf16[2,128,1024]{2,1,0:T(8,128)(2,1)S(1)}, u32[]{:S(2)}, u32[]{:S(2)}) collective-permute-start(bf16[2,128,1024]{2,1,0:T(8,128)(2,1)S(1)} %pad_maximum_fusion.2), channel_id=1, source_target_pairs={{0,2},{2,0},{4,6},{6,4},{8,10},{10,8},{12,14},{14,12},{16,18},{18,... | collective-permute-start | bytes 1572872 | tf_op jit(solution)/shard_map/ppermute | solution.py:148
  24.9 9.2 %collective-permute-start.2 = (bf16[2,4,128,128]{3,2,1,0:T(8,128)(2,1)S(1)}, bf16[2,4,128,128]{3,2,1,0:T(8,128)(2,1)S(1)}, u32[]{:S(2)}, u32[]{:S(2)}) collective-permute-start(bf16[2,4,128,128]{3,2,1,0:T(8,128)(2,1)S(1)} %collective-permute-done.1.refs_2_), channel_id=1, source_target_pairs={{4,12},{6,14},{12,20},{14,22},{20,28},{22,30},{28,24},{30,26},{24,... | collective-permute-start | bytes 786440 | tf_op jit(solution)/shard_map/ppermute | solution.py:134
  28.4 25.6 %collective-permute-start.12 = (bf16[2,128,1024]{2,1,0:T(8,128)(2,1)S(1)}, bf16[2,128,1024]{2,1,0:T(8,128)(2,1)S(1)}, u32[]{:S(2)}, u32[]{:S(2)}) collective-permute-start(bf16[2,128,1024]{2,1,0:T(8,128)(2,1)S(1)} %pad_maximum_fusion.1), channel_id=1, source_target_pairs={{4,12},{6,14},{12,20},{14,22},{20,28},{22,30},{28,24},{30,26},{24,... | collective-permute-start | bytes 1572872 | tf_op jit(solution)/shard_map/ppermute | solution.py:134
  30.0 24.1 %collective-permute-start.13 = (bf16[2,128,1024]{2,1,0:T(8,128)(2,1)S(1)}, bf16[2,128,1024]{2,1,0:T(8,128)(2,1)S(1)}, u32[]{:S(2)}, u32[]{:S(2)}) collective-permute-start(bf16[2,128,1024]{2,1,0:T(8,128)(2,1)S(1)} %pad_maximum_fusion.1), channel_id=1, source_target_pairs={{4,0},{6,2},{12,4},{14,6},{20,12},{22,14},{28,20},{30,22},{24,28},... | collective-permute-start | bytes 1572872 | tf_op jit(solution)/shard_map/ppermute | solution.py:134
  34.0 18.5 %collective-permute-start.5 = (bf16[2,4,128,128]{3,2,1,0:T(8,128)(2,1)S(1)}, bf16[2,4,128,128]{3,2,1,0:T(8,128)(2,1)S(1)}, u32[]{:S(2)}, u32[]{:S(2)}) collective-permute-start(bf16[2,4,128,128]{3,2,1,0:T(8,128)(2,1)S(1)} %collective-permute-done.4.refs_14_), channel_id=1, source_target_pairs={{4,0},{6,2},{12,4},{14,6},{20,12},{22,14},{28,20},{30,22},{24,28},... | collective-permute-start | bytes 786440 | tf_op jit(solution)/shard_map/ppermute | solution.py:134
  35.7 20.8 %collective-permute-start.17 = (bf16[2,128,1024]{2,1,0:T(8,128)(2,1)S(1)}, bf16[2,128,1024]{2,1,0:T(8,128)(2,1)S(1)}, u32[]{:S(2)}, u32[]{:S(2)}) collective-permute-start(bf16[2,128,1024]{2,1,0:T(8,128)(2,1)S(1)} %collective-permute-done.15), channel_id=1, source_target_pairs={{4,12},{6,14},{12,20},{14,22},{20,28},{22,30},{28,24},{30,26},{24,... | collective-permute-start | bytes 1572872 | tf_op jit(solution)/shard_map/ppermute | solution.py:134
  37.2 26.5 %collective-permute-start.18 = (bf16[2,128,1024]{2,1,0:T(8,128)(2,1)S(1)}, bf16[2,128,1024]{2,1,0:T(8,128)(2,1)S(1)}, u32[]{:S(2)}, u32[]{:S(2)}) collective-permute-start(bf16[2,128,1024]{2,1,0:T(8,128)(2,1)S(1)} %collective-permute-done.15), channel_id=1, source_target_pairs={{4,0},{6,2},{12,4},{14,6},{20,12},{22,14},{28,20},{30,22},{24,28},... | collective-permute-start | bytes 1572872 | tf_op jit(solution)/shard_map/ppermute | solution.py:134
  52.5 11.7 %collective-permute-start.20 = (bf16[2,4,128,128]{3,2,1,0:T(8,128)(2,1)S(1)}, bf16[2,4,128,128]{3,2,1,0:T(8,128)(2,1)S(1)}, u32[]{:S(2)}, u32[]{:S(2)}) collective-permute-start(bf16[2,4,128,128]{3,2,1,0:T(8,128)(2,1)S(1)} %collective-permute-done.11.refs_10_), channel_id=1, source_target_pairs={{4,12},{6,14},{12,20},{14,22},{20,28},{22,30},{28,24},{30,26},{24,... | collective-permute-start | bytes 786440 | tf_op jit(solution)/shard_map/ppermute | solution.py:134
  54.1 13.6 %collective-permute-start.19 = (bf16[2,4,128,128]{3,2,1,0:T(8,128)(2,1)S(1)}, bf16[2,4,128,128]{3,2,1,0:T(8,128)(2,1)S(1)}, u32[]{:S(2)}, u32[]{:S(2)}) collective-permute-start(bf16[2,4,128,128]{3,2,1,0:T(8,128)(2,1)S(1)} %collective-permute-done.2.refs_3_), channel_id=1, source_target_pairs={{4,12},{6,14},{12,20},{14,22},{20,28},{22,30},{28,24},{30,26},{24,... | collective-permute-start | bytes 786440 | tf_op jit(solution)/shard_map/ppermute | solution.py:134
  55.7 13.6 %collective-permute-start.21 = (bf16[2,4,128,128]{3,2,1,0:T(8,128)(2,1)S(1)}, bf16[2,4,128,128]{3,2,1,0:T(8,128)(2,1)S(1)}, u32[]{:S(2)}, u32[]{:S(2)}) collective-permute-start(bf16[2,4,128,128]{3,2,1,0:T(8,128)(2,1)S(1)} %collective-permute-done.5.refs_13_), channel_id=1, source_target_pairs={{4,0},{6,2},{12,4},{14,6},{20,12},{22,14},{28,20},{30,22},{24,28},... | collective-permute-start | bytes 786440 | tf_op jit(solution)/shard_map/ppermute | solution.py:134
  56.5 22.3 %collective-permute-start.27 = (bf16[2,128,1024]{2,1,0:T(8,128)(2,1)S(1)}, bf16[2,128,1024]{2,1,0:T(8,128)(2,1)S(1)}, u32[]{:S(2)}, u32[]{:S(2)}) collective-permute-start(bf16[2,128,1024]{2,1,0:T(8,128)(2,1)S(1)} %collective-permute-done.12), channel_id=1, source_target_pairs={{4,12},{6,14},{12,20},{14,22},{20,28},{22,30},{28,24},{30,26},{24,... | collective-permute-start | bytes 1572872 | tf_op jit(solution)/shard_map/ppermute | solution.py:134
  63.7 16.4 %collective-permute-start.28 = (bf16[2,128,1024]{2,1,0:T(8,128)(2,1)S(1)}, bf16[2,128,1024]{2,1,0:T(8,128)(2,1)S(1)}, u32[]{:S(2)}, u32[]{:S(2)}) collective-permute-start(bf16[2,128,1024]{2,1,0:T(8,128)(2,1)S(1)} %collective-permute-done.13), channel_id=1, source_target_pairs={{4,0},{6,2},{12,4},{14,6},{20,12},{22,14},{28,20},{30,22},{24,28},... | collective-permute-start | bytes 1572872 | tf_op jit(solution)/shard_map/ppermute | solution.py:134
  75.1 14.9 %collective-permute-start.29 = (bf16[2,128,1024]{2,1,0:T(8,128)(2,1)S(1)}, bf16[2,128,1024]{2,1,0:T(8,128)(2,1)S(1)}, u32[]{:S(2)}, u32[]{:S(2)}) collective-permute-start(bf16[2,128,1024]{2,1,0:T(8,128)(2,1)S(1)} %collective-permute-done.17), channel_id=1, source_target_pairs={{4,12},{6,14},{12,20},{14,22},{20,28},{22,30},{28,24},{30,26},{24,... | collective-permute-start | bytes 1572872 | tf_op jit(solution)/shard_map/ppermute | solution.py:134
  76.7 14.8 %collective-permute-start.30 = (bf16[2,128,1024]{2,1,0:T(8,128)(2,1)S(1)}, bf16[2,128,1024]{2,1,0:T(8,128)(2,1)S(1)}, u32[]{:S(2)}, u32[]{:S(2)}) collective-permute-start(bf16[2,128,1024]{2,1,0:T(8,128)(2,1)S(1)} %collective-permute-done.18), channel_id=1, source_target_pairs={{4,0},{6,2},{12,4},{14,6},{20,12},{22,14},{28,20},{30,22},{24,28},... | collective-permute-start | bytes 1572872 | tf_op jit(solution)/shard_map/ppermute | solution.py:134
  81.6 19.6 %collective-permute-start.33 = (bf16[2,128,1024]{2,1,0:T(8,128)(2,1)S(1)}, bf16[2,128,1024]{2,1,0:T(8,128)(2,1)S(1)}, u32[]{:S(2)}, u32[]{:S(2)}) collective-permute-start(bf16[2,128,1024]{2,1,0:T(8,128)(2,1)S(1)} %collective-permute-done.27), channel_id=1, source_target_pairs={{4,12},{6,14},{12,20},{14,22},{20,28},{22,30},{28,24},{30,26},{24,... | collective-permute-start | bytes 1572872 | tf_op jit(solution)/shard_map/ppermute | solution.py:134
  83.2 19.5 %collective-permute-start.34 = (bf16[2,128,1024]{2,1,0:T(8,128)(2,1)S(1)}, bf16[2,128,1024]{2,1,0:T(8,128)(2,1)S(1)}, u32[]{:S(2)}, u32[]{:S(2)}) collective-permute-start(bf16[2,128,1024]{2,1,0:T(8,128)(2,1)S(1)} %collective-permute-done.28), channel_id=1, source_target_pairs={{4,0},{6,2},{12,4},{14,6},{20,12},{22,14},{28,20},{30,22},{24,28},... | collective-permute-start | bytes 1572872 | tf_op jit(solution)/shard_map/ppermute | solution.py:134
  93.3 13.1 %collective-permute-start.32 = (bf16[128,2048]{1,0:T(8,128)(2,1)S(1)}, bf16[128,2048]{1,0:T(8,128)(2,1)S(1)}, u32[]{:S(2)}, u32[]{:S(2)}) collective-permute-start(bf16[128,2048]{1,0:T(8,128)(2,1)S(1)} %combine.1), channel_id=1, source_target_pairs={{0,1},{1,0},{2,3},{3,2},{4,5},{5,4},{6,7},{7,6},{8,9},{9,8},{10,11... | collective-permute-start | bytes 1572872 | tf_op jit(solution)/shard_map/ppermute | solution.py:152
  94.9 17.6 %collective-permute-start.36 = (bf16[2,128,1024]{2,1,0:T(8,128)(2,1)S(1)}, bf16[2,128,1024]{2,1,0:T(8,128)(2,1)S(1)}, u32[]{:S(2)}, u32[]{:S(2)}) collective-permute-start(bf16[2,128,1024]{2,1,0:T(8,128)(2,1)S(1)} %collective-permute-done.29), channel_id=1, source_target_pairs={{4,12},{6,14},{12,20},{14,22},{20,28},{22,30},{28,24},{30,26},{24,... | collective-permute-start | bytes 1572872 | tf_op jit(solution)/shard_map/ppermute | solution.py:134
  96.5 17.5 %collective-permute-start.37 = (bf16[2,128,1024]{2,1,0:T(8,128)(2,1)S(1)}, bf16[2,128,1024]{2,1,0:T(8,128)(2,1)S(1)}, u32[]{:S(2)}, u32[]{:S(2)}) collective-permute-start(bf16[2,128,1024]{2,1,0:T(8,128)(2,1)S(1)} %collective-permute-done.30), channel_id=1, source_target_pairs={{4,0},{6,2},{12,4},{14,6},{20,12},{22,14},{28,20},{30,22},{24,28},... | collective-permute-start | bytes 1572872 | tf_op jit(solution)/shard_map/ppermute | solution.py:134
  101.3 14.3 %collective-permute-start.31 = (bf16[128,2048]{1,0:T(8,128)(2,1)S(1)}, bf16[128,2048]{1,0:T(8,128)(2,1)S(1)}, u32[]{:S(2)}, u32[]{:S(2)}) collective-permute-start(bf16[128,2048]{1,0:T(8,128)(2,1)S(1)} %combine.1), channel_id=1, source_target_pairs={{0,2},{2,0},{4,6},{6,4},{8,10},{10,8},{12,14},{14,12},{16,18},{18,... | collective-permute-start | bytes 1572872 | tf_op jit(solution)/shard_map/ppermute | solution.py:148
  102.7 16.6 %collective-permute-start.40 = (bf16[144,1024]{1,0:T(8,128)(2,1)S(1)}, bf16[144,1024]{1,0:T(8,128)(2,1)S(1)}, u32[]{:S(2)}, u32[]{:S(2)}) collective-permute-start(bf16[144,1024]{1,0:T(8,128)(2,1)S(1)} %slice.42), channel_id=1, source_target_pairs={{4,12},{6,14},{12,20},{14,22},{20,28},{22,30},{28,24},{30,26},{24,... | collective-permute-start | bytes 884744 | tf_op jit(solution)/shard_map/ppermute | solution.py:134
  106.5 12.8 %collective-permute-start.41 = (bf16[112,1024]{1,0:T(8,128)(2,1)S(1)}, bf16[112,1024]{1,0:T(8,128)(2,1)S(1)}, u32[]{:S(2)}, u32[]{:S(2)}) collective-permute-start(bf16[112,1024]{1,0:T(8,128)(2,1)S(1)} %slice.43), channel_id=1, source_target_pairs={{4,0},{6,2},{12,4},{14,6},{20,12},{22,14},{28,20},{30,22},{24,28},... | collective-permute-start | bytes 688136 | tf_op jit(solution)/shard_map/ppermute | solution.py:134
  114.0 10.2 %collective-permute-start.38 = (bf16[128,1024]{1,0:T(8,128)(2,1)S(1)}, bf16[128,1024]{1,0:T(8,128)(2,1)S(1)}, u32[]{:S(2)}, u32[]{:S(2)}) collective-permute-start(bf16[128,1024]{1,0:T(8,128)(2,1)S(1)} %slice_bitcast_fusion.1), channel_id=1, source_target_pairs={{4,12},{6,14},{12,20},{14,22},{20,28},{22,30},{28,24},{30,26},{24,... | collective-permute-start | bytes 786440 | tf_op jit(solution)/shard_map/ppermute | solution.py:134
  (19 other events, 192.4 us)

commit v2 on v1

--- a/solution.py
+++ b/solution.py
@@ -350,9 +350,14 @@
             value = value + base[...]
         if item + 1 < len(items):
             total[...] = value
-    tokens = results[0].shape[0]
+    tokens, width = results[0].shape[0], value.shape[1]
     for part, result in enumerate(results):
-        result[...] = value[part * tokens : (part + 1) * tokens].astype(result.dtype)
+        block = value[part * tokens : (part + 1) * tokens].astype(result.dtype)
+        if result.shape[1] == width:
+            result[...] = block
+        else:
+            first = pl.multiple_of(lax.rem(me[0], CORES) * width, width)
+            result[:, pl.ds(first, width)] = block
 
 
 def project(ring, me, rows, blocks, base, shapes):
@@ -497,8 +502,9 @@
     last(1, rows_held * 8 // 16)
     crossed_rows = swap_core(turned, pool)
     crossed_rows = after(crossed_rows, far[3], far[chips - 3])
+    swapped = swap_core(attended, pool)
     rows = [
-        jnp.concatenate([attended, swap_core(attended, pool)], axis=0),
+        jnp.concatenate([attended, swapped], axis=0),
         jnp.concatenate([turned, crossed_rows], axis=0),
     ]
 
@@ -509,21 +515,16 @@
     early = [0] + [at for step in range(1, half - 1) for at in (step, chips - step)]
     total = project(ring, me, rows, blocks(early), None, sums)[0]
     middle = blocks([half - 1, half + 1]) | {(half, 0): quarters[half, 0]}
-    total = project(ring, me, rows, middle, total, sums)[0]
-    own_out, other_out = project(
-        ring,
-        me,
-        rows,
-        {(half, 1): quarters[half, 1]},
-        total,
-        [jax.ShapeDtypeStruct((tokens, width), jnp.bfloat16)] * 2,
-    )
-    beside = swap_core(other_out, pool)
-    result = jnp.where(
-        core == 0,
-        jnp.concatenate([own_out, beside], axis=1),
-        jnp.concatenate([beside, own_out], axis=1),
-    )
+    sums = [jax.ShapeDtypeStruct((tokens, width), jnp.float32)] * CORES
+    own_total, other_total = project(ring, me, rows, middle, total, sums)
+
+    block = [jax.ShapeDtypeStruct((tokens, width), jnp.bfloat16)]
+    end = {(half, 1): quarters[half, 1]}
+    other_rows = [swapped, crossed_rows]
+    beside = swap_core(project(ring, me, other_rows, end, other_total, block)[0], pool)
+    whole = [jax.ShapeDtypeStruct((tokens, span), jnp.bfloat16)]
+    result = project(ring, me, [attended, turned], end, own_total, whole)[0]
+    result = lax.dynamic_update_slice_in_dim(result, beside, (1 - core) * width, axis=1)
     return result[None]
 
 

time: 128 us -> 128 us (level)
  Pallas kernels: 19.9 us -> 21.5 us
  waiting for transfers between devices: 67.3 us -> 65.8 us
    pallas_call x3 -> x4, Pallas kernels: 6.16 us -> 7.72 us  [project(): pl.pallas_call(functools.partial(project_kernel, items, base is not None)...]
    ppermute x11, waiting for transfers between devices: 2.48 us -> 0.97 us  [swap_core(): return lax.ppermute(value, 'pool', [(at, at ^ 1) for at in range(pool)])]
  transfers between devices with their start and end apart: 43 -> 43, of which waited for: 24 -> 23; matrix products, arithmetic and copies ran while one was open for 2% -> 2% of each run, Pallas kernels for 15% -> 16%
where the time goes in v2:
time: 128 us; the launch traced here: 127 us
  waiting for transfers between devices  65.8 us (51%)
  starting transfers between devices  36.4 us (28%)
  Pallas kernels  21.5 us (17%)
  local copies, waits for them, and re-layouts  3.11 us (2%)
    ppermute x30, waiting for transfers between devices, shift(): return lax.ppermute(value, 'pool', pairs)  62.7 us
    ppermute x30, starting transfers between devices, shift(): return lax.ppermute(value, 'pool', pairs)  31.6 us
    pallas_call x2, Pallas kernels, attend(): pl.pallas_call(functools.partial(attend_kernel, pieces, owned), out_shape...  11.9 us
    pallas_call x4, Pallas kernels, project(): pl.pallas_call(functools.partial(project_kernel, items, base is not None)...  7.72 us
    ppermute x2, starting transfers between devices, swap_plane(): return lax.ppermute(value, 'head', [(0, 1), (1, 0)])  3.59 us
  transfers between devices with their start and end apart: 43, of which 23 were waited for; matrix products, arithmetic and copies ran while one was open for 2% of the time, Pallas kernels for 16%

profile of v2, /device:TPU:0, one launch (start us, length us, event | category | flops | bytes accessed | tf_op | source)
XLA Modules:
  0.0 127.5 jit_solution(15900895577098790700)
XLA Ops:
  0.5 2.5 %collective-permute-start = (bf16[2,4,128,128]{3,2,1,0:T(8,128)(2,1)}, bf16[2,4,128,128]{3,2,1,0:T(8,128)(2,1)S(1)}, u32[]{:S(2)}, u32[]{:S(2)}) collective-permute-start(bf16[2,4,128,128]{3,2,1,0:T(8,128)(2,1)} %refs_0_.3), channel_id=1, source_target_pairs={{4,12},{6,14},{12,20},{14,22},{20,28},{22,30},{28,24},{30,26},{24,... | collective-permute-start | bytes 786440 | tf_op jit(solution)/shard_map/ppermute | solution.py:134
  4.2 2.0 %collective-permute-start.7 = (bf16[128,2048]{1,0:T(8,128)(2,1)S(1)}, bf16[128,2048]{1,0:T(8,128)(2,1)S(1)}, u32[]{:S(2)}, u32[]{:S(2)}) collective-permute-start(bf16[128,2048]{1,0:T(8,128)(2,1)S(1)} %constant_dynamic-slice_fusion), channel_id=1, source_target_pairs={{0,1},{1,0},{2,3},{3,2},{4,5},{5,4},{6,7},{7,6},{8,9},{9,8},{10,11... | collective-permute-start | bytes 1572872 | tf_op jit(solution)/shard_map/ppermute | solution.py:152
  8.3 2.2 %collective-permute-done.refs_1_ = bf16[2,4,128,128]{3,2,1,0:T(8,128)(2,1)S(1)} collective-permute-done((bf16[2,4,128,128]{3,2,1,0:T(8,128)(2,1)}, bf16[2,4,128,128]{3,2,1,0:T(8,128)(2,1)S(1)}, u32[]{:S(2)}, u32[]{:S(2)}) %collective-permute-start) | collective-permute-done | bytes 262176 | tf_op jit(solution)/shard_map/ppermute | solution.py:134
  10.4 1.9 %collective-permute-start.1 = (bf16[2,4,128,128]{3,2,1,0:T(8,128)(2,1)S(1)}, bf16[2,4,128,128]{3,2,1,0:T(8,128)(2,1)S(1)}, u32[]{:S(2)}, u32[]{:S(2)}) collective-permute-start(bf16[2,4,128,128]{3,2,1,0:T(8,128)(2,1)S(1)} %collective-permute-done.refs_1_), channel_id=1, source_target_pairs={{4,12},{6,14},{12,20},{14,22},{20,28},{22,30},{28,24},{30,26},{24,... | collective-permute-start | bytes 786440 | tf_op jit(solution)/shard_map/ppermute | solution.py:134
  12.5 3.6 %collective-permute-done.10.refs_9_ = bf16[2,4,128,128]{3,2,1,0:T(8,128)(2,1)S(1)} collective-permute-done((bf16[2,4,128,128]{3,2,1,0:T(8,128)(2,1)S(1)}, bf16[2,4,128,128]{3,2,1,0:T(8,128)(2,1)S(1)}, u32[]{:S(2)}, u32[]{:S(2)}) %collective-permute-start.10) | collective-permute-done | bytes 262176 | tf_op jit(solution)/shard_map/ppermute | solution.py:134
  16.1 1.9 %collective-permute-start.11 = (bf16[2,4,128,128]{3,2,1,0:T(8,128)(2,1)S(1)}, bf16[2,4,128,128]{3,2,1,0:T(8,128)(2,1)S(1)}, u32[]{:S(2)}, u32[]{:S(2)}) collective-permute-start(bf16[2,4,128,128]{3,2,1,0:T(8,128)(2,1)S(1)} %collective-permute-done.10.refs_9_), channel_id=1, source_target_pairs={{4,12},{6,14},{12,20},{14,22},{20,28},{22,30},{28,24},{30,26},{24,... | collective-permute-start | bytes 786440 | tf_op jit(solution)/shard_map/ppermute | solution.py:134
  18.1 3.6 %collective-permute-done.1.refs_2_ = bf16[2,4,128,128]{3,2,1,0:T(8,128)(2,1)S(1)} collective-permute-done((bf16[2,4,128,128]{3,2,1,0:T(8,128)(2,1)S(1)}, bf16[2,4,128,128]{3,2,1,0:T(8,128)(2,1)S(1)}, u32[]{:S(2)}, u32[]{:S(2)}) %collective-permute-start.1) | collective-permute-done | bytes 262176 | tf_op jit(solution)/shard_map/ppermute | solution.py:134
  21.7 1.9 %collective-permute-done.9.refs_6_ = bf16[2,4,128,128]{3,2,1,0:T(8,128)(2,1)S(1)} collective-permute-done((bf16[2,4,128,128]{3,2,1,0:T(8,128)(2,1)S(1)}, bf16[2,4,128,128]{3,2,1,0:T(8,128)(2,1)S(1)}, u32[]{:S(2)}, u32[]{:S(2)}) %collective-permute-start.9) | collective-permute-done | bytes 262176 | tf_op jit(solution)/shard_map/ppermute | solution.py:134
  24.9 1.6 %collective-permute-start.2 = (bf16[2,4,128,128]{3,2,1,0:T(8,128)(2,1)S(1)}, bf16[2,4,128,128]{3,2,1,0:T(8,128)(2,1)S(1)}, u32[]{:S(2)}, u32[]{:S(2)}) collective-permute-start(bf16[2,4,128,128]{3,2,1,0:T(8,128)(2,1)S(1)} %collective-permute-done.1.refs_2_), channel_id=1, source_target_pairs={{4,12},{6,14},{12,20},{14,22},{20,28},{22,30},{28,24},{30,26},{24,... | collective-permute-start | bytes 786440 | tf_op jit(solution)/shard_map/ppermute | solution.py:134
  28.4 1.6 %collective-permute-start.12 = (bf16[2,128,1024]{2,1,0:T(8,128)(2,1)S(1)}, bf16[2,128,1024]{2,1,0:T(8,128)(2,1)S(1)}, u32[]{:S(2)}, u32[]{:S(2)}) collective-permute-start(bf16[2,128,1024]{2,1,0:T(8,128)(2,1)S(1)} %pad_maximum_fusion.1), channel_id=1, source_target_pairs={{4,12},{6,14},{12,20},{14,22},{20,28},{22,30},{28,24},{30,26},{24,... | collective-permute-start | bytes 1572872 | tf_op jit(solution)/shard_map/ppermute | solution.py:134
  30.5 3.5 %collective-permute-done.2.refs_3_ = bf16[2,4,128,128]{3,2,1,0:T(8,128)(2,1)S(1)} collective-permute-done((bf16[2,4,128,128]{3,2,1,0:T(8,128)(2,1)S(1)}, bf16[2,4,128,128]{3,2,1,0:T(8,128)(2,1)S(1)}, u32[]{:S(2)}, u32[]{:S(2)}) %collective-permute-start.2) | collective-permute-done | bytes 262176 | tf_op jit(solution)/shard_map/ppermute | solution.py:134
  35.7 1.6 %collective-permute-start.17 = (bf16[2,128,1024]{2,1,0:T(8,128)(2,1)S(1)}, bf16[2,128,1024]{2,1,0:T(8,128)(2,1)S(1)}, u32[]{:S(2)}, u32[]{:S(2)}) collective-permute-start(bf16[2,128,1024]{2,1,0:T(8,128)(2,1)S(1)} %collective-permute-done.15), channel_id=1, source_target_pairs={{4,12},{6,14},{12,20},{14,22},{20,28},{22,30},{28,24},{30,26},{24,... | collective-permute-start | bytes 1572872 | tf_op jit(solution)/shard_map/ppermute | solution.py:134
  37.8 14.7 %collective-permute-done.5.refs_13_ = bf16[2,4,128,128]{3,2,1,0:T(8,128)(2,1)S(1)} collective-permute-done((bf16[2,4,128,128]{3,2,1,0:T(8,128)(2,1)S(1)}, bf16[2,4,128,128]{3,2,1,0:T(8,128)(2,1)S(1)}, u32[]{:S(2)}, u32[]{:S(2)}) %collective-permute-start.5) | collective-permute-done | bytes 262176 | tf_op jit(solution)/shard_map/ppermute | solution.py:134
  52.5 1.6 %collective-permute-start.20 = (bf16[2,4,128,128]{3,2,1,0:T(8,128)(2,1)S(1)}, bf16[2,4,128,128]{3,2,1,0:T(8,128)(2,1)S(1)}, u32[]{:S(2)}, u32[]{:S(2)}) collective-permute-start(bf16[2,4,128,128]{3,2,1,0:T(8,128)(2,1)S(1)} %collective-permute-done.11.refs_10_), channel_id=1, source_target_pairs={{4,12},{6,14},{12,20},{14,22},{20,28},{22,30},{28,24},{30,26},{24,... | collective-permute-start | bytes 786440 | tf_op jit(solution)/shard_map/ppermute | solution.py:134
  54.1 1.6 %collective-permute-start.19 = (bf16[2,4,128,128]{3,2,1,0:T(8,128)(2,1)S(1)}, bf16[2,4,128,128]{3,2,1,0:T(8,128)(2,1)S(1)}, u32[]{:S(2)}, u32[]{:S(2)}) collective-permute-start(bf16[2,4,128,128]{3,2,1,0:T(8,128)(2,1)S(1)} %collective-permute-done.2.refs_3_), channel_id=1, source_target_pairs={{4,12},{6,14},{12,20},{14,22},{20,28},{22,30},{28,24},{30,26},{24,... | collective-permute-start | bytes 786440 | tf_op jit(solution)/shard_map/ppermute | solution.py:134
  56.5 1.6 %collective-permute-start.27 = (bf16[2,128,1024]{2,1,0:T(8,128)(2,1)S(1)}, bf16[2,128,1024]{2,1,0:T(8,128)(2,1)S(1)}, u32[]{:S(2)}, u32[]{:S(2)}) collective-permute-start(bf16[2,128,1024]{2,1,0:T(8,128)(2,1)S(1)} %collective-permute-done.12), channel_id=1, source_target_pairs={{4,12},{6,14},{12,20},{14,22},{20,28},{22,30},{28,24},{30,26},{24,... | collective-permute-start | bytes 1572872 | tf_op jit(solution)/shard_map/ppermute | solution.py:134
  58.1 5.7 %collective-permute-done.18 = bf16[2,128,1024]{2,1,0:T(8,128)(2,1)S(1)} collective-permute-done((bf16[2,128,1024]{2,1,0:T(8,128)(2,1)S(1)}, bf16[2,128,1024]{2,1,0:T(8,128)(2,1)S(1)}, u32[]{:S(2)}, u32[]{:S(2)}) %collective-permute-start.18) | collective-permute-done | bytes 524320 | tf_op jit(solution)/shard_map/ppermute | solution.py:134
  64.2 3.5 %collective-permute-done.19.refs_4_ = bf16[2,4,128,128]{3,2,1,0:T(8,128)(2,1)S(1)} collective-permute-done((bf16[2,4,128,128]{3,2,1,0:T(8,128)(2,1)S(1)}, bf16[2,4,128,128]{3,2,1,0:T(8,128)(2,1)S(1)}, u32[]{:S(2)}, u32[]{:S(2)}) %collective-permute-start.19) | collective-permute-done | bytes 262176 | tf_op jit(solution)/shard_map/ppermute | solution.py:134
  67.7 1.6 %collective-permute-done.21.refs_12_ = bf16[2,4,128,128]{3,2,1,0:T(8,128)(2,1)S(1)} collective-permute-done((bf16[2,4,128,128]{3,2,1,0:T(8,128)(2,1)S(1)}, bf16[2,4,128,128]{3,2,1,0:T(8,128)(2,1)S(1)}, u32[]{:S(2)}, u32[]{:S(2)}) %collective-permute-start.21) | collective-permute-done | bytes 262176 | tf_op jit(solution)/shard_map/ppermute | solution.py:134
  69.4 5.6 %attend.2 = (f32[128,512]{1,0:T(8,128)S(1)}, f32[128,512]{1,0:T(8,128)S(1)}, f32[128,512]{1,0:T(8,128)S(1)}, f32[128,512]{1,0:T(8,128)S(1)}, f32[128,128]{1,0:T(8,128)S(1)}) custom-call(s32[16]{0:T(128)S(1)} %get-tuple-element.85.ids, s32[16]{0:T(128)S(1)} %get-tuple-element.84.ranks, s32[16]{0:T(128)S(1)} %copy-done.5, s32[1]{0:T(128)} %bitcast.me, ...), custom_call_target="tpu_custom_call" | custom-call | flops 6442450944 | bytes 4194304 | tf_op jit(solution)/shard_map/attend/pallas_call | solution.py:254
  75.1 1.6 %collective-permute-start.29 = (bf16[2,128,1024]{2,1,0:T(8,128)(2,1)S(1)}, bf16[2,128,1024]{2,1,0:T(8,128)(2,1)S(1)}, u32[]{:S(2)}, u32[]{:S(2)}) collective-permute-start(bf16[2,128,1024]{2,1,0:T(8,128)(2,1)S(1)} %collective-permute-done.17), channel_id=1, source_target_pairs={{4,12},{6,14},{12,20},{14,22},{20,28},{22,30},{28,24},{30,26},{24,... | collective-permute-start | bytes 1572872 | tf_op jit(solution)/shard_map/ppermute | solution.py:134
  77.2 1.6 %collective-permute-done.27 = bf16[2,128,1024]{2,1,0:T(8,128)(2,1)S(1)} collective-permute-done((bf16[2,128,1024]{2,1,0:T(8,128)(2,1)S(1)}, bf16[2,128,1024]{2,1,0:T(8,128)(2,1)S(1)}, u32[]{:S(2)}, u32[]{:S(2)}) %collective-permute-start.27) | collective-permute-done | bytes 524320 | tf_op jit(solution)/shard_map/ppermute | solution.py:134
  83.7 6.3 %attend.3 = (f32[128,512]{1,0:T(8,128)S(1)}, f32[128,512]{1,0:T(8,128)S(1)}, f32[128,512]{1,0:T(8,128)S(1)}, f32[128,512]{1,0:T(8,128)S(1)}, f32[128,128]{1,0:T(8,128)S(1)}) custom-call(s32[16]{0:T(128)S(1)} %get-tuple-element.87.ids, s32[16]{0:T(128)S(1)} %get-tuple-element.86.ranks, s32[16]{0:T(128)S(1)} %copy-done.5, s32[1]{0:T(128)} %bitcast.me, ...), custom_call_target="tpu_custom_call" | custom-call | flops 301989888 | bytes 4194304 | tf_op jit(solution)/shard_map/attend/pallas_call | solution.py:254
  91.5 1.8 %combine.1.own_rows = bf16[128,2048]{1,0:T(8,128)(2,1)S(1)} custom-call(f32[128,512]{1,0:T(8,128)S(1)} %get-tuple-element.63.refs_0_, f32[128,512]{1,0:T(8,128)S(1)} %get-tuple-element.64.refs_1_, f32[128,512]{1,0:T(8,128)S(1)} %get-tuple-element.65.refs_2_, f32[128,512]{1,0:T(8,128)S(1)} %get-tuple-element.66.refs_3_, ...), custom_call_target="tpu_custom_call" | custom-call | flops 1048576 | bytes 2621440 | tf_op jit(solution)/shard_map/combine/pallas_call | solution.py:306
  93.3 1.6 %collective-permute-start.31 = (bf16[128,2048]{1,0:T(8,128)(2,1)S(1)}, bf16[128,2048]{1,0:T(8,128)(2,1)S(1)}, u32[]{:S(2)}, u32[]{:S(2)}) collective-permute-start(bf16[128,2048]{1,0:T(8,128)(2,1)S(1)} %combine.1.own_rows), channel_id=1, source_target_pairs={{0,1},{1,0},{2,3},{3,2},{4,5},{5,4},{6,7},{7,6},{8,9},{9,8},{10,11... | collective-permute-start | bytes 1572872 | tf_op jit(solution)/shard_map/ppermute | solution.py:152
  96.9 4.3 %collective-permute-done.32 = bf16[2,128,1024]{2,1,0:T(8,128)(2,1)S(1)} collective-permute-done((bf16[2,128,1024]{2,1,0:T(8,128)(2,1)S(1)}, bf16[2,128,1024]{2,1,0:T(8,128)(2,1)S(1)}, u32[]{:S(2)}, u32[]{:S(2)}) %collective-permute-start.32) | collective-permute-done | bytes 524320 | tf_op jit(solution)/shard_map/ppermute | solution.py:134
  104.3 2.1 %collective-permute-done.31.other_rows = bf16[128,2048]{1,0:T(8,128)(2,1)S(1)} collective-permute-done((bf16[128,2048]{1,0:T(8,128)(2,1)S(1)}, bf16[128,2048]{1,0:T(8,128)(2,1)S(1)}, u32[]{:S(2)}, u32[]{:S(2)}) %collective-permute-start.31) | collective-permute-done | bytes 524320 | tf_op jit(solution)/shard_map/ppermute | solution.py:152
  107.0 5.5 %collective-permute-done.34 = bf16[2,128,1024]{2,1,0:T(8,128)(2,1)S(1)} collective-permute-done((bf16[2,128,1024]{2,1,0:T(8,128)(2,1)S(1)}, bf16[2,128,1024]{2,1,0:T(8,128)(2,1)S(1)}, u32[]{:S(2)}, u32[]{:S(2)}) %collective-permute-start.34) | collective-permute-done | bytes 524320 | tf_op jit(solution)/shard_map/ppermute | solution.py:134
  116.2 3.0 %project.4.refs_6_ = f32[256,1024]{1,0:T(8,128)S(1)} custom-call(s32[16]{0:T(128)S(1)} %copy-done.5, s32[1]{0:T(128)} %bitcast.me, bf16[256,2048]{1,0:T(8,128)(2,1)S(1)} %pad_maximum_fusion.own_rows, bf16[256,2048]{1,0:T(8,128)(2,1)S(1)} %constant_dynamic-update-slice_fusion.other_rows, bf16[256,1024]{1,0:T(8,128)(2,1)S(1)} %bitcast.41, ...), custom_call_target="tpu_custom_call" | custom-call | flops 1342177280 | bytes 6291456 | tf_op jit(solution)/shard_map/project/pallas_call | solution.py:375
  119.3 2.2 %project.5 = (f32[128,1024]{1,0:T(8,128)S(1)}, f32[128,1024]{1,0:T(8,128)S(1)}) custom-call(s32[16]{0:T(128)S(1)} %copy-done.5, s32[1]{0:T(128)} %bitcast.me, bf16[256,2048]{1,0:T(8,128)(2,1)S(1)} %pad_maximum_fusion.own_rows, bf16[256,2048]{1,0:T(8,128)(2,1)S(1)} %constant_dynamic-update-slice_fusion.other_rows, bf16[256,1024]{1,0:T(8,128)(2,1)S(1)} %bitcast.43, ...), custom_call_target="tpu_custom_call" | custom-call | flops 671088640 | bytes 3670016 | tf_op jit(solution)/shard_map/project/pallas_call | solution.py:375
  121.5 2.6 %collective-permute-done.35.refs_0_ = bf16[128,1024]{1,0:T(8,128)(2,1)S(1)} collective-permute-done((bf16[128,1024]{1,0:T(8,128)(2,1)S(1)}, bf16[128,1024]{1,0:T(8,128)(2,1)S(1)}, u32[]{:S(2)}, u32[]{:S(2)}) %collective-permute-start.35) | collective-permute-done | bytes 262176 | tf_op jit(solution)/shard_map/ppermute | solution.py:134
  125.1 1.6 %project.6 = bf16[128,2048]{1,0:T(8,128)(2,1)} custom-call(s32[16]{0:T(128)S(1)} %copy-done.5, s32[1]{0:T(128)} %bitcast.me, bf16[128,2048]{1,0:T(8,128)(2,1)S(1)} %combine.1.own_rows, bf16[128,2048]{1,0:T(8,128)(2,1)S(1)} %collective-permute-done.31.other_rows, bf16[128,1024]{1,0:T(8,128)(2,1)S(1)} %collective-permute-done.35.refs_0_, ...), custom_call_target="tpu_custom_call" | custom-call | flops 67108864 | bytes 1048576 | tf_op jit(solution)/shard_map/project/pallas_call | solution.py:375
  (96 shorter events, 28.9 us)
Async XLA Ops:
  0.5 10.0 %collective-permute-start = (bf16[2,4,128,128]{3,2,1,0:T(8,128)(2,1)}, bf16[2,4,128,128]{3,2,1,0:T(8,128)(2,1)S(1)}, u32[]{:S(2)}, u32[]{:S(2)}) collective-permute-start(bf16[2,4,128,128]{3,2,1,0:T(8,128)(2,1)} %refs_0_.3), channel_id=1, source_target_pairs={{4,12},{6,14},{12,20},{14,22},{20,28},{22,30},{28,24},{30,26},{24,... | collective-permute-start | bytes 786440 | tf_op jit(solution)/shard_map/ppermute | solution.py:134
  3.0 9.4 %collective-permute-start.8 = (bf16[2,4,128,128]{3,2,1,0:T(8,128)(2,1)}, bf16[2,4,128,128]{3,2,1,0:T(8,128)(2,1)S(1)}, u32[]{:S(2)}, u32[]{:S(2)}) collective-permute-start(bf16[2,4,128,128]{3,2,1,0:T(8,128)(2,1)} %refs_0_.3), channel_id=1, source_target_pairs={{4,0},{6,2},{12,4},{14,6},{20,12},{22,14},{28,20},{30,22},{24,28},... | collective-permute-start | bytes 786440 | tf_op jit(solution)/shard_map/ppermute | solution.py:134
  4.2 19.4 %collective-permute-start.7 = (bf16[128,2048]{1,0:T(8,128)(2,1)S(1)}, bf16[128,2048]{1,0:T(8,128)(2,1)S(1)}, u32[]{:S(2)}, u32[]{:S(2)}) collective-permute-start(bf16[128,2048]{1,0:T(8,128)(2,1)S(1)} %constant_dynamic-slice_fusion), channel_id=1, source_target_pairs={{0,1},{1,0},{2,3},{3,2},{4,5},{5,4},{6,7},{7,6},{8,9},{9,8},{10,11... | collective-permute-start | bytes 1572872 | tf_op jit(solution)/shard_map/ppermute | solution.py:152
  6.2 9.8 %collective-permute-start.10 = (bf16[2,4,128,128]{3,2,1,0:T(8,128)(2,1)S(1)}, bf16[2,4,128,128]{3,2,1,0:T(8,128)(2,1)S(1)}, u32[]{:S(2)}, u32[]{:S(2)}) collective-permute-start(bf16[2,4,128,128]{3,2,1,0:T(8,128)(2,1)S(1)} %copy-done.2), channel_id=1, source_target_pairs={{4,12},{6,14},{12,20},{14,22},{20,28},{22,30},{28,24},{30,26},{24,... | collective-permute-start | bytes 786440 | tf_op jit(solution)/shard_map/ppermute | solution.py:134
  7.7 10.2 %collective-permute-start.3 = (bf16[2,4,128,128]{3,2,1,0:T(8,128)(2,1)S(1)}, bf16[2,4,128,128]{3,2,1,0:T(8,128)(2,1)S(1)}, u32[]{:S(2)}, u32[]{:S(2)}) collective-permute-start(bf16[2,4,128,128]{3,2,1,0:T(8,128)(2,1)S(1)} %copy-done.2), channel_id=1, source_target_pairs={{4,0},{6,2},{12,4},{14,6},{20,12},{22,14},{28,20},{30,22},{24,28},... | collective-permute-start | bytes 786440 | tf_op jit(solution)/shard_map/ppermute | solution.py:134
  10.4 11.2 %collective-permute-start.1 = (bf16[2,4,128,128]{3,2,1,0:T(8,128)(2,1)S(1)}, bf16[2,4,128,128]{3,2,1,0:T(8,128)(2,1)S(1)}, u32[]{:S(2)}, u32[]{:S(2)}) collective-permute-start(bf16[2,4,128,128]{3,2,1,0:T(8,128)(2,1)S(1)} %collective-permute-done.refs_1_), channel_id=1, source_target_pairs={{4,12},{6,14},{12,20},{14,22},{20,28},{22,30},{28,24},{30,26},{24,... | collective-permute-start | bytes 786440 | tf_op jit(solution)/shard_map/ppermute | solution.py:134
  12.4 11.2 %collective-permute-start.9 = (bf16[2,4,128,128]{3,2,1,0:T(8,128)(2,1)S(1)}, bf16[2,4,128,128]{3,2,1,0:T(8,128)(2,1)S(1)}, u32[]{:S(2)}, u32[]{:S(2)}) collective-permute-start(bf16[2,4,128,128]{3,2,1,0:T(8,128)(2,1)S(1)} %collective-permute-done.8.refs_7_), channel_id=1, source_target_pairs={{4,0},{6,2},{12,4},{14,6},{20,12},{22,14},{28,20},{30,22},{24,28},... | collective-permute-start | bytes 786440 | tf_op jit(solution)/shard_map/ppermute | solution.py:134
  16.1 11.0 %collective-permute-start.11 = (bf16[2,4,128,128]{3,2,1,0:T(8,128)(2,1)S(1)}, bf16[2,4,128,128]{3,2,1,0:T(8,128)(2,1)S(1)}, u32[]{:S(2)}, u32[]{:S(2)}) collective-permute-start(bf16[2,4,128,128]{3,2,1,0:T(8,128)(2,1)S(1)} %collective-permute-done.10.refs_9_), channel_id=1, source_target_pairs={{4,12},{6,14},{12,20},{14,22},{20,28},{22,30},{28,24},{30,26},{24,... | collective-permute-start | bytes 786440 | tf_op jit(solution)/shard_map/ppermute | solution.py:134
  18.0 10.5 %collective-permute-start.4 = (bf16[2,4,128,128]{3,2,1,0:T(8,128)(2,1)S(1)}, bf16[2,4,128,128]{3,2,1,0:T(8,128)(2,1)S(1)}, u32[]{:S(2)}, u32[]{:S(2)}) collective-permute-start(bf16[2,4,128,128]{3,2,1,0:T(8,128)(2,1)S(1)} %collective-permute-done.3.refs_15_), channel_id=1, source_target_pairs={{4,0},{6,2},{12,4},{14,6},{20,12},{22,14},{28,20},{30,22},{24,28},... | collective-permute-start | bytes 786440 | tf_op jit(solution)/shard_map/ppermute | solution.py:134
  24.8 10.9 %collective-permute-start.15 = (bf16[2,128,1024]{2,1,0:T(8,128)(2,1)S(1)}, bf16[2,128,1024]{2,1,0:T(8,128)(2,1)S(1)}, u32[]{:S(2)}, u32[]{:S(2)}) collective-permute-start(bf16[2,128,1024]{2,1,0:T(8,128)(2,1)S(1)} %pad_maximum_fusion.2), channel_id=1, source_target_pairs={{0,2},{2,0},{4,6},{6,4},{8,10},{10,8},{12,14},{14,12},{16,18},{18,... | collective-permute-start | bytes 1572872 | tf_op jit(solution)/shard_map/ppermute | solution.py:148
  24.9 9.2 %collective-permute-start.2 = (bf16[2,4,128,128]{3,2,1,0:T(8,128)(2,1)S(1)}, bf16[2,4,128,128]{3,2,1,0:T(8,128)(2,1)S(1)}, u32[]{:S(2)}, u32[]{:S(2)}) collective-permute-start(bf16[2,4,128,128]{3,2,1,0:T(8,128)(2,1)S(1)} %collective-permute-done.1.refs_2_), channel_id=1, source_target_pairs={{4,12},{6,14},{12,20},{14,22},{20,28},{22,30},{28,24},{30,26},{24,... | collective-permute-start | bytes 786440 | tf_op jit(solution)/shard_map/ppermute | solution.py:134
  28.4 25.6 %collective-permute-start.12 = (bf16[2,128,1024]{2,1,0:T(8,128)(2,1)S(1)}, bf16[2,128,1024]{2,1,0:T(8,128)(2,1)S(1)}, u32[]{:S(2)}, u32[]{:S(2)}) collective-permute-start(bf16[2,128,1024]{2,1,0:T(8,128)(2,1)S(1)} %pad_maximum_fusion.1), channel_id=1, source_target_pairs={{4,12},{6,14},{12,20},{14,22},{20,28},{22,30},{28,24},{30,26},{24,... | collective-permute-start | bytes 1572872 | tf_op jit(solution)/shard_map/ppermute | solution.py:134
  30.0 24.1 %collective-permute-start.13 = (bf16[2,128,1024]{2,1,0:T(8,128)(2,1)S(1)}, bf16[2,128,1024]{2,1,0:T(8,128)(2,1)S(1)}, u32[]{:S(2)}, u32[]{:S(2)}) collective-permute-start(bf16[2,128,1024]{2,1,0:T(8,128)(2,1)S(1)} %pad_maximum_fusion.1), channel_id=1, source_target_pairs={{4,0},{6,2},{12,4},{14,6},{20,12},{22,14},{28,20},{30,22},{24,28},... | collective-permute-start | bytes 1572872 | tf_op jit(solution)/shard_map/ppermute | solution.py:134
  34.0 18.5 %collective-permute-start.5 = (bf16[2,4,128,128]{3,2,1,0:T(8,128)(2,1)S(1)}, bf16[2,4,128,128]{3,2,1,0:T(8,128)(2,1)S(1)}, u32[]{:S(2)}, u32[]{:S(2)}) collective-permute-start(bf16[2,4,128,128]{3,2,1,0:T(8,128)(2,1)S(1)} %collective-permute-done.4.refs_14_), channel_id=1, source_target_pairs={{4,0},{6,2},{12,4},{14,6},{20,12},{22,14},{28,20},{30,22},{24,28},... | collective-permute-start | bytes 786440 | tf_op jit(solution)/shard_map/ppermute | solution.py:134
  35.7 20.8 %collective-permute-start.17 = (bf16[2,128,1024]{2,1,0:T(8,128)(2,1)S(1)}, bf16[2,128,1024]{2,1,0:T(8,128)(2,1)S(1)}, u32[]{:S(2)}, u32[]{:S(2)}) collective-permute-start(bf16[2,128,1024]{2,1,0:T(8,128)(2,1)S(1)} %collective-permute-done.15), channel_id=1, source_target_pairs={{4,12},{6,14},{12,20},{14,22},{20,28},{22,30},{28,24},{30,26},{24,... | collective-permute-start | bytes 1572872 | tf_op jit(solution)/shard_map/ppermute | solution.py:134
  37.2 26.5 %collective-permute-start.18 = (bf16[2,128,1024]{2,1,0:T(8,128)(2,1)S(1)}, bf16[2,128,1024]{2,1,0:T(8,128)(2,1)S(1)}, u32[]{:S(2)}, u32[]{:S(2)}) collective-permute-start(bf16[2,128,1024]{2,1,0:T(8,128)(2,1)S(1)} %collective-permute-done.15), channel_id=1, source_target_pairs={{4,0},{6,2},{12,4},{14,6},{20,12},{22,14},{28,20},{30,22},{24,28},... | collective-permute-start | bytes 1572872 | tf_op jit(solution)/shard_map/ppermute | solution.py:134
  52.5 11.7 %collective-permute-start.20 = (bf16[2,4,128,128]{3,2,1,0:T(8,128)(2,1)S(1)}, bf16[2,4,128,128]{3,2,1,0:T(8,128)(2,1)S(1)}, u32[]{:S(2)}, u32[]{:S(2)}) collective-permute-start(bf16[2,4,128,128]{3,2,1,0:T(8,128)(2,1)S(1)} %collective-permute-done.11.refs_10_), channel_id=1, source_target_pairs={{4,12},{6,14},{12,20},{14,22},{20,28},{22,30},{28,24},{30,26},{24,... | collective-permute-start | bytes 786440 | tf_op jit(solution)/shard_map/ppermute | solution.py:134
  54.1 13.6 %collective-permute-start.19 = (bf16[2,4,128,128]{3,2,1,0:T(8,128)(2,1)S(1)}, bf16[2,4,128,128]{3,2,1,0:T(8,128)(2,1)S(1)}, u32[]{:S(2)}, u32[]{:S(2)}) collective-permute-start(bf16[2,4,128,128]{3,2,1,0:T(8,128)(2,1)S(1)} %collective-permute-done.2.refs_3_), channel_id=1, source_target_pairs={{4,12},{6,14},{12,20},{14,22},{20,28},{22,30},{28,24},{30,26},{24,... | collective-permute-start | bytes 786440 | tf_op jit(solution)/shard_map/ppermute | solution.py:134
  55.7 13.6 %collective-permute-start.21 = (bf16[2,4,128,128]{3,2,1,0:T(8,128)(2,1)S(1)}, bf16[2,4,128,128]{3,2,1,0:T(8,128)(2,1)S(1)}, u32[]{:S(2)}, u32[]{:S(2)}) collective-permute-start(bf16[2,4,128,128]{3,2,1,0:T(8,128)(2,1)S(1)} %collective-permute-done.5.refs_13_), channel_id=1, source_target_pairs={{4,0},{6,2},{12,4},{14,6},{20,12},{22,14},{28,20},{30,22},{24,28},... | collective-permute-start | bytes 786440 | tf_op jit(solution)/shard_map/ppermute | solution.py:134
  56.5 22.3 %collective-permute-start.27 = (bf16[2,128,1024]{2,1,0:T(8,128)(2,1)S(1)}, bf16[2,128,1024]{2,1,0:T(8,128)(2,1)S(1)}, u32[]{:S(2)}, u32[]{:S(2)}) collective-permute-start(bf16[2,128,1024]{2,1,0:T(8,128)(2,1)S(1)} %collective-permute-done.12), channel_id=1, source_target_pairs={{4,12},{6,14},{12,20},{14,22},{20,28},{22,30},{28,24},{30,26},{24,... | collective-permute-start | bytes 1572872 | tf_op jit(solution)/shard_map/ppermute | solution.py:134
  63.7 16.4 %collective-permute-start.28 = (bf16[2,128,1024]{2,1,0:T(8,128)(2,1)S(1)}, bf16[2,128,1024]{2,1,0:T(8,128)(2,1)S(1)}, u32[]{:S(2)}, u32[]{:S(2)}) collective-permute-start(bf16[2,128,1024]{2,1,0:T(8,128)(2,1)S(1)} %collective-permute-done.13), channel_id=1, source_target_pairs={{4,0},{6,2},{12,4},{14,6},{20,12},{22,14},{28,20},{30,22},{24,28},... | collective-permute-start | bytes 1572872 | tf_op jit(solution)/shard_map/ppermute | solution.py:134
  75.1 14.9 %collective-permute-start.29 = (bf16[2,128,1024]{2,1,0:T(8,128)(2,1)S(1)}, bf16[2,128,1024]{2,1,0:T(8,128)(2,1)S(1)}, u32[]{:S(2)}, u32[]{:S(2)}) collective-permute-start(bf16[2,128,1024]{2,1,0:T(8,128)(2,1)S(1)} %collective-permute-done.17), channel_id=1, source_target_pairs={{4,12},{6,14},{12,20},{14,22},{20,28},{22,30},{28,24},{30,26},{24,... | collective-permute-start | bytes 1572872 | tf_op jit(solution)/shard_map/ppermute | solution.py:134
  76.7 14.8 %collective-permute-start.30 = (bf16[2,128,1024]{2,1,0:T(8,128)(2,1)S(1)}, bf16[2,128,1024]{2,1,0:T(8,128)(2,1)S(1)}, u32[]{:S(2)}, u32[]{:S(2)}) collective-permute-start(bf16[2,128,1024]{2,1,0:T(8,128)(2,1)S(1)} %collective-permute-done.18), channel_id=1, source_target_pairs={{4,0},{6,2},{12,4},{14,6},{20,12},{22,14},{28,20},{30,22},{24,28},... | collective-permute-start | bytes 1572872 | tf_op jit(solution)/shard_map/ppermute | solution.py:134
  81.6 19.6 %collective-permute-start.32 = (bf16[2,128,1024]{2,1,0:T(8,128)(2,1)S(1)}, bf16[2,128,1024]{2,1,0:T(8,128)(2,1)S(1)}, u32[]{:S(2)}, u32[]{:S(2)}) collective-permute-start(bf16[2,128,1024]{2,1,0:T(8,128)(2,1)S(1)} %collective-permute-done.27), channel_id=1, source_target_pairs={{4,12},{6,14},{12,20},{14,22},{20,28},{22,30},{28,24},{30,26},{24,... | collective-permute-start | bytes 1572872 | tf_op jit(solution)/shard_map/ppermute | solution.py:134
  83.2 19.5 %collective-permute-start.33 = (bf16[2,128,1024]{2,1,0:T(8,128)(2,1)S(1)}, bf16[2,128,1024]{2,1,0:T(8,128)(2,1)S(1)}, u32[]{:S(2)}, u32[]{:S(2)}) collective-permute-start(bf16[2,128,1024]{2,1,0:T(8,128)(2,1)S(1)} %collective-permute-done.28), channel_id=1, source_target_pairs={{4,0},{6,2},{12,4},{14,6},{20,12},{22,14},{28,20},{30,22},{24,28},... | collective-permute-start | bytes 1572872 | tf_op jit(solution)/shard_map/ppermute | solution.py:134
  93.3 13.1 %collective-permute-start.31 = (bf16[128,2048]{1,0:T(8,128)(2,1)S(1)}, bf16[128,2048]{1,0:T(8,128)(2,1)S(1)}, u32[]{:S(2)}, u32[]{:S(2)}) collective-permute-start(bf16[128,2048]{1,0:T(8,128)(2,1)S(1)} %combine.1.own_rows), channel_id=1, source_target_pairs={{0,1},{1,0},{2,3},{3,2},{4,5},{5,4},{6,7},{7,6},{8,9},{9,8},{10,11... | collective-permute-start | bytes 1572872 | tf_op jit(solution)/shard_map/ppermute | solution.py:152
  94.9 17.6 %collective-permute-start.34 = (bf16[2,128,1024]{2,1,0:T(8,128)(2,1)S(1)}, bf16[2,128,1024]{2,1,0:T(8,128)(2,1)S(1)}, u32[]{:S(2)}, u32[]{:S(2)}) collective-permute-start(bf16[2,128,1024]{2,1,0:T(8,128)(2,1)S(1)} %collective-permute-done.29), channel_id=1, source_target_pairs={{4,12},{6,14},{12,20},{14,22},{20,28},{22,30},{28,24},{30,26},{24,... | collective-permute-start | bytes 1572872 | tf_op jit(solution)/shard_map/ppermute | solution.py:134
  96.5 17.5 %collective-permute-start.36 = (bf16[2,128,1024]{2,1,0:T(8,128)(2,1)S(1)}, bf16[2,128,1024]{2,1,0:T(8,128)(2,1)S(1)}, u32[]{:S(2)}, u32[]{:S(2)}) collective-permute-start(bf16[2,128,1024]{2,1,0:T(8,128)(2,1)S(1)} %collective-permute-done.30), channel_id=1, source_target_pairs={{4,0},{6,2},{12,4},{14,6},{20,12},{22,14},{28,20},{30,22},{24,28},... | collective-permute-start | bytes 1572872 | tf_op jit(solution)/shard_map/ppermute | solution.py:134
  101.3 14.3 %collective-permute-start.38 = (bf16[128,2048]{1,0:T(8,128)(2,1)S(1)}, bf16[128,2048]{1,0:T(8,128)(2,1)S(1)}, u32[]{:S(2)}, u32[]{:S(2)}) collective-permute-start(bf16[128,2048]{1,0:T(8,128)(2,1)S(1)} %combine.1.own_rows), channel_id=1, source_target_pairs={{0,2},{2,0},{4,6},{6,4},{8,10},{10,8},{12,14},{14,12},{16,18},{18,... | collective-permute-start | bytes 1572872 | tf_op jit(solution)/shard_map/ppermute | solution.py:148
  102.7 16.6 %collective-permute-start.40 = (bf16[144,1024]{1,0:T(8,128)(2,1)S(1)}, bf16[144,1024]{1,0:T(8,128)(2,1)S(1)}, u32[]{:S(2)}, u32[]{:S(2)}) collective-permute-start(bf16[144,1024]{1,0:T(8,128)(2,1)S(1)} %slice.42), channel_id=1, source_target_pairs={{4,12},{6,14},{12,20},{14,22},{20,28},{22,30},{28,24},{30,26},{24,... | collective-permute-start | bytes 884744 | tf_op jit(solution)/shard_map/ppermute | solution.py:134
  106.5 12.8 %collective-permute-start.41 = (bf16[112,1024]{1,0:T(8,128)(2,1)S(1)}, bf16[112,1024]{1,0:T(8,128)(2,1)S(1)}, u32[]{:S(2)}, u32[]{:S(2)}) collective-permute-start(bf16[112,1024]{1,0:T(8,128)(2,1)S(1)} %slice.43), channel_id=1, source_target_pairs={{4,0},{6,2},{12,4},{14,6},{20,12},{22,14},{28,20},{30,22},{24,28},... | collective-permute-start | bytes 688136 | tf_op jit(solution)/shard_map/ppermute | solution.py:134
  114.0 10.2 %collective-permute-start.35 = (bf16[128,1024]{1,0:T(8,128)(2,1)S(1)}, bf16[128,1024]{1,0:T(8,128)(2,1)S(1)}, u32[]{:S(2)}, u32[]{:S(2)}) collective-permute-start(bf16[128,1024]{1,0:T(8,128)(2,1)S(1)} %slice_bitcast_fusion.1), channel_id=1, source_target_pairs={{4,12},{6,14},{12,20},{14,22},{20,28},{22,30},{28,24},{30,26},{24,... | collective-permute-start | bytes 786440 | tf_op jit(solution)/shard_map/ppermute | solution.py:134
  (19 other events, 192.6 us)

commit v3 on v1

--- a/solution.py
+++ b/solution.py
@@ -314,7 +314,7 @@
     )(*state, *state_in)
 
 
-def project_kernel(items, based, ring, me, own_rows, other_rows, *refs):
+def project_kernel(items, based, direct, ring, me, own_rows, other_rows, *refs):
     count = sum(len(heights) for _, _, heights in items)
     blocks, refs = refs[:count], refs[count:]
     base = None
@@ -325,6 +325,8 @@
     copies, at = [], 0
     for item, (_, _, heights) in enumerate(items):
         copies.append([])
+        if direct:
+            continue
         for i, height in enumerate(heights):
             target = held.at[item, pl.ds(sum(heights[:i]), height)]
             copies[-1].append(pltpu.make_async_copy(blocks[at], target, sems.at[at]))
@@ -341,7 +343,7 @@
         columns = pl.ds(pl.multiple_of(home * span, span), span)
         value = jnp.dot(
             jnp.concatenate([rows[:, columns] for rows in (own_rows, other_rows)], axis=1),
-            held[item],
+            jnp.concatenate([block[...] for block in blocks], axis=0) if direct else held[item],
             preferred_element_type=jnp.float32,
         )
         if item:
@@ -355,7 +357,7 @@
         result[...] = value[part * tokens : (part + 1) * tokens].astype(result.dtype)
 
 
-def project(ring, me, rows, blocks, base, shapes):
+def project(ring, me, rows, blocks, base, shapes, direct=False):
     flat = [part.reshape(-1, part.shape[-1]) for parts in blocks.values() for part in parts]
     heights = iter([part.shape[0] for part in flat])
     items = tuple(
@@ -368,11 +370,11 @@
     smem = pl.BlockSpec(memory_space=pltpu.SMEM)
     vmem = pl.BlockSpec(memory_space=pltpu.VMEM)
     return pl.pallas_call(
-        functools.partial(project_kernel, items, base is not None),
+        functools.partial(project_kernel, items, base is not None, direct),
         out_shape=shapes,
         in_specs=[smem] * 2
         + [vmem] * 2
-        + [pl.BlockSpec(memory_space=pl.ANY)] * len(flat)
+        + [vmem if direct else pl.BlockSpec(memory_space=pl.ANY)] * len(flat)
         + ([vmem] if base is not None else []),
         out_specs=[vmem] * len(shapes),
         scratch_shapes=[
@@ -517,6 +519,7 @@
         {(half, 1): quarters[half, 1]},
         total,
         [jax.ShapeDtypeStruct((tokens, width), jnp.bfloat16)] * 2,
+        direct=True,
     )
     beside = swap_core(other_out, pool)
     result = jnp.where(

time: 128 us -> 128 us (level)
  no operation moved by 1% of the time
where the time goes in v3:
time: 128 us
  waiting for transfers between devices  67.3 us (53%)
  starting transfers between devices  36.4 us (28%)
  Pallas kernels  19.9 us (16%)
  local copies, waits for them, and re-layouts  2.38 us (2%)
  other arithmetic  1.33 us (1%)
    ppermute x30, waiting for transfers between devices, shift(): return lax.ppermute(value, 'pool', pairs)  62.7 us
    ppermute x30, starting transfers between devices, shift(): return lax.ppermute(value, 'pool', pairs)  31.6 us
    pallas_call x2, Pallas kernels, attend(): pl.pallas_call(functools.partial(attend_kernel, pieces, owned), out_shape...  11.9 us
    pallas_call x3, Pallas kernels, project(): pl.pallas_call(functools.partial(project_kernel, items, base is not None,...  6.11 us
    ppermute x2, starting transfers between devices, swap_plane(): return lax.ppermute(value, 'head', [(0, 1), (1, 0)])  3.59 us
  transfers between devices with their start and end apart: 43, of which 24 were waited for; matrix products, arithmetic and copies ran while one was open for 2% of the time, Pallas kernels for 15%

profile of v3, /device:TPU:0, one launch (start us, length us, event | category | flops | bytes accessed | tf_op | source)
XLA Modules:
  0.0 127.6 jit_solution(1054625078862584298)
XLA Ops:
  0.5 2.5 %collective-permute-start = (bf16[2,4,128,128]{3,2,1,0:T(8,128)(2,1)}, bf16[2,4,128,128]{3,2,1,0:T(8,128)(2,1)S(1)}, u32[]{:S(2)}, u32[]{:S(2)}) collective-permute-start(bf16[2,4,128,128]{3,2,1,0:T(8,128)(2,1)} %refs_0_.3), channel_id=1, source_target_pairs={{4,12},{6,14},{12,20},{14,22},{20,28},{22,30},{28,24},{30,26},{24,... | collective-permute-start | bytes 786440 | tf_op jit(solution)/shard_map/ppermute | solution.py:134
  4.2 2.0 %collective-permute-start.7 = (bf16[128,2048]{1,0:T(8,128)(2,1)S(1)}, bf16[128,2048]{1,0:T(8,128)(2,1)S(1)}, u32[]{:S(2)}, u32[]{:S(2)}) collective-permute-start(bf16[128,2048]{1,0:T(8,128)(2,1)S(1)} %constant_dynamic-slice_fusion), channel_id=1, source_target_pairs={{0,1},{1,0},{2,3},{3,2},{4,5},{5,4},{6,7},{7,6},{8,9},{9,8},{10,11... | collective-permute-start | bytes 1572872 | tf_op jit(solution)/shard_map/ppermute | solution.py:152
  8.3 2.2 %collective-permute-done.refs_1_ = bf16[2,4,128,128]{3,2,1,0:T(8,128)(2,1)S(1)} collective-permute-done((bf16[2,4,128,128]{3,2,1,0:T(8,128)(2,1)}, bf16[2,4,128,128]{3,2,1,0:T(8,128)(2,1)S(1)}, u32[]{:S(2)}, u32[]{:S(2)}) %collective-permute-start) | collective-permute-done | bytes 262176 | tf_op jit(solution)/shard_map/ppermute | solution.py:134
  10.4 1.9 %collective-permute-start.1 = (bf16[2,4,128,128]{3,2,1,0:T(8,128)(2,1)S(1)}, bf16[2,4,128,128]{3,2,1,0:T(8,128)(2,1)S(1)}, u32[]{:S(2)}, u32[]{:S(2)}) collective-permute-start(bf16[2,4,128,128]{3,2,1,0:T(8,128)(2,1)S(1)} %collective-permute-done.refs_1_), channel_id=1, source_target_pairs={{4,12},{6,14},{12,20},{14,22},{20,28},{22,30},{28,24},{30,26},{24,... | collective-permute-start | bytes 786440 | tf_op jit(solution)/shard_map/ppermute | solution.py:134
  12.5 3.6 %collective-permute-done.10.refs_9_ = bf16[2,4,128,128]{3,2,1,0:T(8,128)(2,1)S(1)} collective-permute-done((bf16[2,4,128,128]{3,2,1,0:T(8,128)(2,1)S(1)}, bf16[2,4,128,128]{3,2,1,0:T(8,128)(2,1)S(1)}, u32[]{:S(2)}, u32[]{:S(2)}) %collective-permute-start.10) | collective-permute-done | bytes 262176 | tf_op jit(solution)/shard_map/ppermute | solution.py:134
  16.1 1.9 %collective-permute-start.11 = (bf16[2,4,128,128]{3,2,1,0:T(8,128)(2,1)S(1)}, bf16[2,4,128,128]{3,2,1,0:T(8,128)(2,1)S(1)}, u32[]{:S(2)}, u32[]{:S(2)}) collective-permute-start(bf16[2,4,128,128]{3,2,1,0:T(8,128)(2,1)S(1)} %collective-permute-done.10.refs_9_), channel_id=1, source_target_pairs={{4,12},{6,14},{12,20},{14,22},{20,28},{22,30},{28,24},{30,26},{24,... | collective-permute-start | bytes 786440 | tf_op jit(solution)/shard_map/ppermute | solution.py:134
  18.1 3.6 %collective-permute-done.1.refs_2_ = bf16[2,4,128,128]{3,2,1,0:T(8,128)(2,1)S(1)} collective-permute-done((bf16[2,4,128,128]{3,2,1,0:T(8,128)(2,1)S(1)}, bf16[2,4,128,128]{3,2,1,0:T(8,128)(2,1)S(1)}, u32[]{:S(2)}, u32[]{:S(2)}) %collective-permute-start.1) | collective-permute-done | bytes 262176 | tf_op jit(solution)/shard_map/ppermute | solution.py:134
  21.7 1.9 %collective-permute-done.9.refs_6_ = bf16[2,4,128,128]{3,2,1,0:T(8,128)(2,1)S(1)} collective-permute-done((bf16[2,4,128,128]{3,2,1,0:T(8,128)(2,1)S(1)}, bf16[2,4,128,128]{3,2,1,0:T(8,128)(2,1)S(1)}, u32[]{:S(2)}, u32[]{:S(2)}) %collective-permute-start.9) | collective-permute-done | bytes 262176 | tf_op jit(solution)/shard_map/ppermute | solution.py:134
  24.9 1.6 %collective-permute-start.2 = (bf16[2,4,128,128]{3,2,1,0:T(8,128)(2,1)S(1)}, bf16[2,4,128,128]{3,2,1,0:T(8,128)(2,1)S(1)}, u32[]{:S(2)}, u32[]{:S(2)}) collective-permute-start(bf16[2,4,128,128]{3,2,1,0:T(8,128)(2,1)S(1)} %collective-permute-done.1.refs_2_), channel_id=1, source_target_pairs={{4,12},{6,14},{12,20},{14,22},{20,28},{22,30},{28,24},{30,26},{24,... | collective-permute-start | bytes 786440 | tf_op jit(solution)/shard_map/ppermute | solution.py:134
  28.4 1.6 %collective-permute-start.12 = (bf16[2,128,1024]{2,1,0:T(8,128)(2,1)S(1)}, bf16[2,128,1024]{2,1,0:T(8,128)(2,1)S(1)}, u32[]{:S(2)}, u32[]{:S(2)}) collective-permute-start(bf16[2,128,1024]{2,1,0:T(8,128)(2,1)S(1)} %pad_maximum_fusion.1), channel_id=1, source_target_pairs={{4,12},{6,14},{12,20},{14,22},{20,28},{22,30},{28,24},{30,26},{24,... | collective-permute-start | bytes 1572872 | tf_op jit(solution)/shard_map/ppermute | solution.py:134
  30.5 3.5 %collective-permute-done.2.refs_3_ = bf16[2,4,128,128]{3,2,1,0:T(8,128)(2,1)S(1)} collective-permute-done((bf16[2,4,128,128]{3,2,1,0:T(8,128)(2,1)S(1)}, bf16[2,4,128,128]{3,2,1,0:T(8,128)(2,1)S(1)}, u32[]{:S(2)}, u32[]{:S(2)}) %collective-permute-start.2) | collective-permute-done | bytes 262176 | tf_op jit(solution)/shard_map/ppermute | solution.py:134
  35.7 1.6 %collective-permute-start.17 = (bf16[2,128,1024]{2,1,0:T(8,128)(2,1)S(1)}, bf16[2,128,1024]{2,1,0:T(8,128)(2,1)S(1)}, u32[]{:S(2)}, u32[]{:S(2)}) collective-permute-start(bf16[2,128,1024]{2,1,0:T(8,128)(2,1)S(1)} %collective-permute-done.15), channel_id=1, source_target_pairs={{4,12},{6,14},{12,20},{14,22},{20,28},{22,30},{28,24},{30,26},{24,... | collective-permute-start | bytes 1572872 | tf_op jit(solution)/shard_map/ppermute | solution.py:134
  37.8 14.7 %collective-permute-done.5.refs_13_ = bf16[2,4,128,128]{3,2,1,0:T(8,128)(2,1)S(1)} collective-permute-done((bf16[2,4,128,128]{3,2,1,0:T(8,128)(2,1)S(1)}, bf16[2,4,128,128]{3,2,1,0:T(8,128)(2,1)S(1)}, u32[]{:S(2)}, u32[]{:S(2)}) %collective-permute-start.5) | collective-permute-done | bytes 262176 | tf_op jit(solution)/shard_map/ppermute | solution.py:134
  52.5 1.6 %collective-permute-start.20 = (bf16[2,4,128,128]{3,2,1,0:T(8,128)(2,1)S(1)}, bf16[2,4,128,128]{3,2,1,0:T(8,128)(2,1)S(1)}, u32[]{:S(2)}, u32[]{:S(2)}) collective-permute-start(bf16[2,4,128,128]{3,2,1,0:T(8,128)(2,1)S(1)} %collective-permute-done.11.refs_10_), channel_id=1, source_target_pairs={{4,12},{6,14},{12,20},{14,22},{20,28},{22,30},{28,24},{30,26},{24,... | collective-permute-start | bytes 786440 | tf_op jit(solution)/shard_map/ppermute | solution.py:134
  54.1 1.6 %collective-permute-start.19 = (bf16[2,4,128,128]{3,2,1,0:T(8,128)(2,1)S(1)}, bf16[2,4,128,128]{3,2,1,0:T(8,128)(2,1)S(1)}, u32[]{:S(2)}, u32[]{:S(2)}) collective-permute-start(bf16[2,4,128,128]{3,2,1,0:T(8,128)(2,1)S(1)} %collective-permute-done.2.refs_3_), channel_id=1, source_target_pairs={{4,12},{6,14},{12,20},{14,22},{20,28},{22,30},{28,24},{30,26},{24,... | collective-permute-start | bytes 786440 | tf_op jit(solution)/shard_map/ppermute | solution.py:134
  56.5 1.6 %collective-permute-start.27 = (bf16[2,128,1024]{2,1,0:T(8,128)(2,1)S(1)}, bf16[2,128,1024]{2,1,0:T(8,128)(2,1)S(1)}, u32[]{:S(2)}, u32[]{:S(2)}) collective-permute-start(bf16[2,128,1024]{2,1,0:T(8,128)(2,1)S(1)} %collective-permute-done.12), channel_id=1, source_target_pairs={{4,12},{6,14},{12,20},{14,22},{20,28},{22,30},{28,24},{30,26},{24,... | collective-permute-start | bytes 1572872 | tf_op jit(solution)/shard_map/ppermute | solution.py:134
  58.1 5.7 %collective-permute-done.18 = bf16[2,128,1024]{2,1,0:T(8,128)(2,1)S(1)} collective-permute-done((bf16[2,128,1024]{2,1,0:T(8,128)(2,1)S(1)}, bf16[2,128,1024]{2,1,0:T(8,128)(2,1)S(1)}, u32[]{:S(2)}, u32[]{:S(2)}) %collective-permute-start.18) | collective-permute-done | bytes 524320 | tf_op jit(solution)/shard_map/ppermute | solution.py:134
  64.2 3.5 %collective-permute-done.19.refs_4_ = bf16[2,4,128,128]{3,2,1,0:T(8,128)(2,1)S(1)} collective-permute-done((bf16[2,4,128,128]{3,2,1,0:T(8,128)(2,1)S(1)}, bf16[2,4,128,128]{3,2,1,0:T(8,128)(2,1)S(1)}, u32[]{:S(2)}, u32[]{:S(2)}) %collective-permute-start.19) | collective-permute-done | bytes 262176 | tf_op jit(solution)/shard_map/ppermute | solution.py:134
  67.7 1.6 %collective-permute-done.21.refs_12_ = bf16[2,4,128,128]{3,2,1,0:T(8,128)(2,1)S(1)} collective-permute-done((bf16[2,4,128,128]{3,2,1,0:T(8,128)(2,1)S(1)}, bf16[2,4,128,128]{3,2,1,0:T(8,128)(2,1)S(1)}, u32[]{:S(2)}, u32[]{:S(2)}) %collective-permute-start.21) | collective-permute-done | bytes 262176 | tf_op jit(solution)/shard_map/ppermute | solution.py:134
  69.4 5.6 %attend.2 = (f32[128,512]{1,0:T(8,128)S(1)}, f32[128,512]{1,0:T(8,128)S(1)}, f32[128,512]{1,0:T(8,128)S(1)}, f32[128,512]{1,0:T(8,128)S(1)}, f32[128,128]{1,0:T(8,128)S(1)}) custom-call(s32[16]{0:T(128)S(1)} %get-tuple-element.85.ids, s32[16]{0:T(128)S(1)} %get-tuple-element.84.ranks, s32[16]{0:T(128)S(1)} %copy-done.5, s32[1]{0:T(128)} %bitcast.me, ...), custom_call_target="tpu_custom_call" | custom-call | flops 6442450944 | bytes 4194304 | tf_op jit(solution)/shard_map/attend/pallas_call | solution.py:254
  75.1 1.6 %collective-permute-start.29 = (bf16[2,128,1024]{2,1,0:T(8,128)(2,1)S(1)}, bf16[2,128,1024]{2,1,0:T(8,128)(2,1)S(1)}, u32[]{:S(2)}, u32[]{:S(2)}) collective-permute-start(bf16[2,128,1024]{2,1,0:T(8,128)(2,1)S(1)} %collective-permute-done.17), channel_id=1, source_target_pairs={{4,12},{6,14},{12,20},{14,22},{20,28},{22,30},{28,24},{30,26},{24,... | collective-permute-start | bytes 1572872 | tf_op jit(solution)/shard_map/ppermute | solution.py:134
  77.2 1.6 %collective-permute-done.27 = bf16[2,128,1024]{2,1,0:T(8,128)(2,1)S(1)} collective-permute-done((bf16[2,128,1024]{2,1,0:T(8,128)(2,1)S(1)}, bf16[2,128,1024]{2,1,0:T(8,128)(2,1)S(1)}, u32[]{:S(2)}, u32[]{:S(2)}) %collective-permute-start.27) | collective-permute-done | bytes 524320 | tf_op jit(solution)/shard_map/ppermute | solution.py:134
  83.7 6.3 %attend.3 = (f32[128,512]{1,0:T(8,128)S(1)}, f32[128,512]{1,0:T(8,128)S(1)}, f32[128,512]{1,0:T(8,128)S(1)}, f32[128,512]{1,0:T(8,128)S(1)}, f32[128,128]{1,0:T(8,128)S(1)}) custom-call(s32[16]{0:T(128)S(1)} %get-tuple-element.87.ids, s32[16]{0:T(128)S(1)} %get-tuple-element.86.ranks, s32[16]{0:T(128)S(1)} %copy-done.5, s32[1]{0:T(128)} %bitcast.me, ...), custom_call_target="tpu_custom_call" | custom-call | flops 301989888 | bytes 4194304 | tf_op jit(solution)/shard_map/attend/pallas_call | solution.py:254
  91.5 1.8 %combine.1 = bf16[128,2048]{1,0:T(8,128)(2,1)S(1)} custom-call(f32[128,512]{1,0:T(8,128)S(1)} %get-tuple-element.63.refs_0_, f32[128,512]{1,0:T(8,128)S(1)} %get-tuple-element.64.refs_1_, f32[128,512]{1,0:T(8,128)S(1)} %get-tuple-element.65.refs_2_, f32[128,512]{1,0:T(8,128)S(1)} %get-tuple-element.66.refs_3_, f32[128,128]{1,0:T(8,128)S(1)} %get-tuple-element.67.refs_4_, ...), custom_call_target="tpu_custom_call" | custom-call | flops 1048576 | bytes 2621440 | tf_op jit(solution)/shard_map/combine/pallas_call | solution.py:306
  93.3 1.6 %collective-permute-start.32 = (bf16[128,2048]{1,0:T(8,128)(2,1)S(1)}, bf16[128,2048]{1,0:T(8,128)(2,1)S(1)}, u32[]{:S(2)}, u32[]{:S(2)}) collective-permute-start(bf16[128,2048]{1,0:T(8,128)(2,1)S(1)} %combine.1), channel_id=1, source_target_pairs={{0,1},{1,0},{2,3},{3,2},{4,5},{5,4},{6,7},{7,6},{8,9},{9,8},{10,11... | collective-permute-start | bytes 1572872 | tf_op jit(solution)/shard_map/ppermute | solution.py:152
  94.9 1.6 %collective-permute-start.36 = (bf16[2,128,1024]{2,1,0:T(8,128)(2,1)S(1)}, bf16[2,128,1024]{2,1,0:T(8,128)(2,1)S(1)}, u32[]{:S(2)}, u32[]{:S(2)}) collective-permute-start(bf16[2,128,1024]{2,1,0:T(8,128)(2,1)S(1)} %collective-permute-done.29), channel_id=1, source_target_pairs={{4,12},{6,14},{12,20},{14,22},{20,28},{22,30},{28,24},{30,26},{24,... | collective-permute-start | bytes 1572872 | tf_op jit(solution)/shard_map/ppermute | solution.py:134
  96.9 4.3 %collective-permute-done.33 = bf16[2,128,1024]{2,1,0:T(8,128)(2,1)S(1)} collective-permute-done((bf16[2,128,1024]{2,1,0:T(8,128)(2,1)S(1)}, bf16[2,128,1024]{2,1,0:T(8,128)(2,1)S(1)}, u32[]{:S(2)}, u32[]{:S(2)}) %collective-permute-start.33) | collective-permute-done | bytes 524320 | tf_op jit(solution)/shard_map/ppermute | solution.py:134
  104.3 2.1 %collective-permute-done.32 = bf16[128,2048]{1,0:T(8,128)(2,1)S(1)} collective-permute-done((bf16[128,2048]{1,0:T(8,128)(2,1)S(1)}, bf16[128,2048]{1,0:T(8,128)(2,1)S(1)}, u32[]{:S(2)}, u32[]{:S(2)}) %collective-permute-start.32) | collective-permute-done | bytes 524320 | tf_op jit(solution)/shard_map/ppermute | solution.py:152
  107.0 5.5 %collective-permute-done.36 = bf16[2,128,1024]{2,1,0:T(8,128)(2,1)S(1)} collective-permute-done((bf16[2,128,1024]{2,1,0:T(8,128)(2,1)S(1)}, bf16[2,128,1024]{2,1,0:T(8,128)(2,1)S(1)}, u32[]{:S(2)}, u32[]{:S(2)}) %collective-permute-start.36) | collective-permute-done | bytes 524320 | tf_op jit(solution)/shard_map/ppermute | solution.py:134
  116.2 3.0 %project.3.refs_6_ = f32[256,1024]{1,0:T(8,128)S(1)} custom-call(s32[16]{0:T(128)S(1)} %copy-done.5, s32[1]{0:T(128)} %bitcast.me, bf16[256,2048]{1,0:T(8,128)(2,1)S(1)} %pad_maximum_fusion.own_rows, bf16[256,2048]{1,0:T(8,128)(2,1)S(1)} %constant_dynamic-update-slice_fusion.other_rows, bf16[256,1024]{1,0:T(8,128)(2,1)S(1)} %bitcast.40, ...), custom_call_target="tpu_custom_call" | custom-call | flops 1342177280 | bytes 6291456 | tf_op jit(solution)/shard_map/project/pallas_call | solution.py:372
  119.3 2.2 %project.4.refs_2_ = f32[256,1024]{1,0:T(8,128)S(1)} custom-call(s32[16]{0:T(128)S(1)} %copy-done.5, s32[1]{0:T(128)} %bitcast.me, bf16[256,2048]{1,0:T(8,128)(2,1)S(1)} %pad_maximum_fusion.own_rows, bf16[256,2048]{1,0:T(8,128)(2,1)S(1)} %constant_dynamic-update-slice_fusion.other_rows, bf16[256,1024]{1,0:T(8,128)(2,1)S(1)} %bitcast.42, ...), custom_call_target="tpu_custom_call" | custom-call | flops 671088640 | bytes 3670016 | tf_op jit(solution)/shard_map/project/pallas_call | solution.py:372
  121.5 2.6 %collective-permute-done.38.refs_0_ = bf16[128,1024]{1,0:T(8,128)(2,1)S(1)} collective-permute-done((bf16[128,1024]{1,0:T(8,128)(2,1)S(1)}, bf16[128,1024]{1,0:T(8,128)(2,1)S(1)}, u32[]{:S(2)}, u32[]{:S(2)}) %collective-permute-start.38) | collective-permute-done | bytes 262176 | tf_op jit(solution)/shard_map/ppermute | solution.py:134
  (95 shorter events, 29.0 us)
Async XLA Ops:
  0.5 10.0 %collective-permute-start = (bf16[2,4,128,128]{3,2,1,0:T(8,128)(2,1)}, bf16[2,4,128,128]{3,2,1,0:T(8,128)(2,1)S(1)}, u32[]{:S(2)}, u32[]{:S(2)}) collective-permute-start(bf16[2,4,128,128]{3,2,1,0:T(8,128)(2,1)} %refs_0_.3), channel_id=1, source_target_pairs={{4,12},{6,14},{12,20},{14,22},{20,28},{22,30},{28,24},{30,26},{24,... | collective-permute-start | bytes 786440 | tf_op jit(solution)/shard_map/ppermute | solution.py:134
  3.0 9.4 %collective-permute-start.8 = (bf16[2,4,128,128]{3,2,1,0:T(8,128)(2,1)}, bf16[2,4,128,128]{3,2,1,0:T(8,128)(2,1)S(1)}, u32[]{:S(2)}, u32[]{:S(2)}) collective-permute-start(bf16[2,4,128,128]{3,2,1,0:T(8,128)(2,1)} %refs_0_.3), channel_id=1, source_target_pairs={{4,0},{6,2},{12,4},{14,6},{20,12},{22,14},{28,20},{30,22},{24,28},... | collective-permute-start | bytes 786440 | tf_op jit(solution)/shard_map/ppermute | solution.py:134
  4.2 19.4 %collective-permute-start.7 = (bf16[128,2048]{1,0:T(8,128)(2,1)S(1)}, bf16[128,2048]{1,0:T(8,128)(2,1)S(1)}, u32[]{:S(2)}, u32[]{:S(2)}) collective-permute-start(bf16[128,2048]{1,0:T(8,128)(2,1)S(1)} %constant_dynamic-slice_fusion), channel_id=1, source_target_pairs={{0,1},{1,0},{2,3},{3,2},{4,5},{5,4},{6,7},{7,6},{8,9},{9,8},{10,11... | collective-permute-start | bytes 1572872 | tf_op jit(solution)/shard_map/ppermute | solution.py:152
  6.2 9.8 %collective-permute-start.10 = (bf16[2,4,128,128]{3,2,1,0:T(8,128)(2,1)S(1)}, bf16[2,4,128,128]{3,2,1,0:T(8,128)(2,1)S(1)}, u32[]{:S(2)}, u32[]{:S(2)}) collective-permute-start(bf16[2,4,128,128]{3,2,1,0:T(8,128)(2,1)S(1)} %copy-done.2), channel_id=1, source_target_pairs={{4,12},{6,14},{12,20},{14,22},{20,28},{22,30},{28,24},{30,26},{24,... | collective-permute-start | bytes 786440 | tf_op jit(solution)/shard_map/ppermute | solution.py:134
  7.7 10.2 %collective-permute-start.3 = (bf16[2,4,128,128]{3,2,1,0:T(8,128)(2,1)S(1)}, bf16[2,4,128,128]{3,2,1,0:T(8,128)(2,1)S(1)}, u32[]{:S(2)}, u32[]{:S(2)}) collective-permute-start(bf16[2,4,128,128]{3,2,1,0:T(8,128)(2,1)S(1)} %copy-done.2), channel_id=1, source_target_pairs={{4,0},{6,2},{12,4},{14,6},{20,12},{22,14},{28,20},{30,22},{24,28},... | collective-permute-start | bytes 786440 | tf_op jit(solution)/shard_map/ppermute | solution.py:134
  10.4 11.2 %collective-permute-start.1 = (bf16[2,4,128,128]{3,2,1,0:T(8,128)(2,1)S(1)}, bf16[2,4,128,128]{3,2,1,0:T(8,128)(2,1)S(1)}, u32[]{:S(2)}, u32[]{:S(2)}) collective-permute-start(bf16[2,4,128,128]{3,2,1,0:T(8,128)(2,1)S(1)} %collective-permute-done.refs_1_), channel_id=1, source_target_pairs={{4,12},{6,14},{12,20},{14,22},{20,28},{22,30},{28,24},{30,26},{24,... | collective-permute-start | bytes 786440 | tf_op jit(solution)/shard_map/ppermute | solution.py:134
  12.4 11.2 %collective-permute-start.9 = (bf16[2,4,128,128]{3,2,1,0:T(8,128)(2,1)S(1)}, bf16[2,4,128,128]{3,2,1,0:T(8,128)(2,1)S(1)}, u32[]{:S(2)}, u32[]{:S(2)}) collective-permute-start(bf16[2,4,128,128]{3,2,1,0:T(8,128)(2,1)S(1)} %collective-permute-done.8.refs_7_), channel_id=1, source_target_pairs={{4,0},{6,2},{12,4},{14,6},{20,12},{22,14},{28,20},{30,22},{24,28},... | collective-permute-start | bytes 786440 | tf_op jit(solution)/shard_map/ppermute | solution.py:134
  16.1 11.0 %collective-permute-start.11 = (bf16[2,4,128,128]{3,2,1,0:T(8,128)(2,1)S(1)}, bf16[2,4,128,128]{3,2,1,0:T(8,128)(2,1)S(1)}, u32[]{:S(2)}, u32[]{:S(2)}) collective-permute-start(bf16[2,4,128,128]{3,2,1,0:T(8,128)(2,1)S(1)} %collective-permute-done.10.refs_9_), channel_id=1, source_target_pairs={{4,12},{6,14},{12,20},{14,22},{20,28},{22,30},{28,24},{30,26},{24,... | collective-permute-start | bytes 786440 | tf_op jit(solution)/shard_map/ppermute | solution.py:134
  18.0 10.5 %collective-permute-start.4 = (bf16[2,4,128,128]{3,2,1,0:T(8,128)(2,1)S(1)}, bf16[2,4,128,128]{3,2,1,0:T(8,128)(2,1)S(1)}, u32[]{:S(2)}, u32[]{:S(2)}) collective-permute-start(bf16[2,4,128,128]{3,2,1,0:T(8,128)(2,1)S(1)} %collective-permute-done.3.refs_15_), channel_id=1, source_target_pairs={{4,0},{6,2},{12,4},{14,6},{20,12},{22,14},{28,20},{30,22},{24,28},... | collective-permute-start | bytes 786440 | tf_op jit(solution)/shard_map/ppermute | solution.py:134
  24.8 10.9 %collective-permute-start.15 = (bf16[2,128,1024]{2,1,0:T(8,128)(2,1)S(1)}, bf16[2,128,1024]{2,1,0:T(8,128)(2,1)S(1)}, u32[]{:S(2)}, u32[]{:S(2)}) collective-permute-start(bf16[2,128,1024]{2,1,0:T(8,128)(2,1)S(1)} %pad_maximum_fusion.2), channel_id=1, source_target_pairs={{0,2},{2,0},{4,6},{6,4},{8,10},{10,8},{12,14},{14,12},{16,18},{18,... | collective-permute-start | bytes 1572872 | tf_op jit(solution)/shard_map/ppermute | solution.py:148
  24.9 9.2 %collective-permute-start.2 = (bf16[2,4,128,128]{3,2,1,0:T(8,128)(2,1)S(1)}, bf16[2,4,128,128]{3,2,1,0:T(8,128)(2,1)S(1)}, u32[]{:S(2)}, u32[]{:S(2)}) collective-permute-start(bf16[2,4,128,128]{3,2,1,0:T(8,128)(2,1)S(1)} %collective-permute-done.1.refs_2_), channel_id=1, source_target_pairs={{4,12},{6,14},{12,20},{14,22},{20,28},{22,30},{28,24},{30,26},{24,... | collective-permute-start | bytes 786440 | tf_op jit(solution)/shard_map/ppermute | solution.py:134
  28.4 25.6 %collective-permute-start.12 = (bf16[2,128,1024]{2,1,0:T(8,128)(2,1)S(1)}, bf16[2,128,1024]{2,1,0:T(8,128)(2,1)S(1)}, u32[]{:S(2)}, u32[]{:S(2)}) collective-permute-start(bf16[2,128,1024]{2,1,0:T(8,128)(2,1)S(1)} %pad_maximum_fusion.1), channel_id=1, source_target_pairs={{4,12},{6,14},{12,20},{14,22},{20,28},{22,30},{28,24},{30,26},{24,... | collective-permute-start | bytes 1572872 | tf_op jit(solution)/shard_map/ppermute | solution.py:134
  30.0 24.1 %collective-permute-start.13 = (bf16[2,128,1024]{2,1,0:T(8,128)(2,1)S(1)}, bf16[2,128,1024]{2,1,0:T(8,128)(2,1)S(1)}, u32[]{:S(2)}, u32[]{:S(2)}) collective-permute-start(bf16[2,128,1024]{2,1,0:T(8,128)(2,1)S(1)} %pad_maximum_fusion.1), channel_id=1, source_target_pairs={{4,0},{6,2},{12,4},{14,6},{20,12},{22,14},{28,20},{30,22},{24,28},... | collective-permute-start | bytes 1572872 | tf_op jit(solution)/shard_map/ppermute | solution.py:134
  34.0 18.5 %collective-permute-start.5 = (bf16[2,4,128,128]{3,2,1,0:T(8,128)(2,1)S(1)}, bf16[2,4,128,128]{3,2,1,0:T(8,128)(2,1)S(1)}, u32[]{:S(2)}, u32[]{:S(2)}) collective-permute-start(bf16[2,4,128,128]{3,2,1,0:T(8,128)(2,1)S(1)} %collective-permute-done.4.refs_14_), channel_id=1, source_target_pairs={{4,0},{6,2},{12,4},{14,6},{20,12},{22,14},{28,20},{30,22},{24,28},... | collective-permute-start | bytes 786440 | tf_op jit(solution)/shard_map/ppermute | solution.py:134
  35.7 20.8 %collective-permute-start.17 = (bf16[2,128,1024]{2,1,0:T(8,128)(2,1)S(1)}, bf16[2,128,1024]{2,1,0:T(8,128)(2,1)S(1)}, u32[]{:S(2)}, u32[]{:S(2)}) collective-permute-start(bf16[2,128,1024]{2,1,0:T(8,128)(2,1)S(1)} %collective-permute-done.15), channel_id=1, source_target_pairs={{4,12},{6,14},{12,20},{14,22},{20,28},{22,30},{28,24},{30,26},{24,... | collective-permute-start | bytes 1572872 | tf_op jit(solution)/shard_map/ppermute | solution.py:134
  37.2 26.5 %collective-permute-start.18 = (bf16[2,128,1024]{2,1,0:T(8,128)(2,1)S(1)}, bf16[2,128,1024]{2,1,0:T(8,128)(2,1)S(1)}, u32[]{:S(2)}, u32[]{:S(2)}) collective-permute-start(bf16[2,128,1024]{2,1,0:T(8,128)(2,1)S(1)} %collective-permute-done.15), channel_id=1, source_target_pairs={{4,0},{6,2},{12,4},{14,6},{20,12},{22,14},{28,20},{30,22},{24,28},... | collective-permute-start | bytes 1572872 | tf_op jit(solution)/shard_map/ppermute | solution.py:134
  52.5 11.7 %collective-permute-start.20 = (bf16[2,4,128,128]{3,2,1,0:T(8,128)(2,1)S(1)}, bf16[2,4,128,128]{3,2,1,0:T(8,128)(2,1)S(1)}, u32[]{:S(2)}, u32[]{:S(2)}) collective-permute-start(bf16[2,4,128,128]{3,2,1,0:T(8,128)(2,1)S(1)} %collective-permute-done.11.refs_10_), channel_id=1, source_target_pairs={{4,12},{6,14},{12,20},{14,22},{20,28},{22,30},{28,24},{30,26},{24,... | collective-permute-start | bytes 786440 | tf_op jit(solution)/shard_map/ppermute | solution.py:134
  54.1 13.6 %collective-permute-start.19 = (bf16[2,4,128,128]{3,2,1,0:T(8,128)(2,1)S(1)}, bf16[2,4,128,128]{3,2,1,0:T(8,128)(2,1)S(1)}, u32[]{:S(2)}, u32[]{:S(2)}) collective-permute-start(bf16[2,4,128,128]{3,2,1,0:T(8,128)(2,1)S(1)} %collective-permute-done.2.refs_3_), channel_id=1, source_target_pairs={{4,12},{6,14},{12,20},{14,22},{20,28},{22,30},{28,24},{30,26},{24,... | collective-permute-start | bytes 786440 | tf_op jit(solution)/shard_map/ppermute | solution.py:134
  55.7 13.6 %collective-permute-start.21 = (bf16[2,4,128,128]{3,2,1,0:T(8,128)(2,1)S(1)}, bf16[2,4,128,128]{3,2,1,0:T(8,128)(2,1)S(1)}, u32[]{:S(2)}, u32[]{:S(2)}) collective-permute-start(bf16[2,4,128,128]{3,2,1,0:T(8,128)(2,1)S(1)} %collective-permute-done.5.refs_13_), channel_id=1, source_target_pairs={{4,0},{6,2},{12,4},{14,6},{20,12},{22,14},{28,20},{30,22},{24,28},... | collective-permute-start | bytes 786440 | tf_op jit(solution)/shard_map/ppermute | solution.py:134
  56.5 22.3 %collective-permute-start.27 = (bf16[2,128,1024]{2,1,0:T(8,128)(2,1)S(1)}, bf16[2,128,1024]{2,1,0:T(8,128)(2,1)S(1)}, u32[]{:S(2)}, u32[]{:S(2)}) collective-permute-start(bf16[2,128,1024]{2,1,0:T(8,128)(2,1)S(1)} %collective-permute-done.12), channel_id=1, source_target_pairs={{4,12},{6,14},{12,20},{14,22},{20,28},{22,30},{28,24},{30,26},{24,... | collective-permute-start | bytes 1572872 | tf_op jit(solution)/shard_map/ppermute | solution.py:134
  63.7 16.4 %collective-permute-start.28 = (bf16[2,128,1024]{2,1,0:T(8,128)(2,1)S(1)}, bf16[2,128,1024]{2,1,0:T(8,128)(2,1)S(1)}, u32[]{:S(2)}, u32[]{:S(2)}) collective-permute-start(bf16[2,128,1024]{2,1,0:T(8,128)(2,1)S(1)} %collective-permute-done.13), channel_id=1, source_target_pairs={{4,0},{6,2},{12,4},{14,6},{20,12},{22,14},{28,20},{30,22},{24,28},... | collective-permute-start | bytes 1572872 | tf_op jit(solution)/shard_map/ppermute | solution.py:134
  75.1 14.9 %collective-permute-start.29 = (bf16[2,128,1024]{2,1,0:T(8,128)(2,1)S(1)}, bf16[2,128,1024]{2,1,0:T(8,128)(2,1)S(1)}, u32[]{:S(2)}, u32[]{:S(2)}) collective-permute-start(bf16[2,128,1024]{2,1,0:T(8,128)(2,1)S(1)} %collective-permute-done.17), channel_id=1, source_target_pairs={{4,12},{6,14},{12,20},{14,22},{20,28},{22,30},{28,24},{30,26},{24,... | collective-permute-start | bytes 1572872 | tf_op jit(solution)/shard_map/ppermute | solution.py:134
  76.7 14.8 %collective-permute-start.30 = (bf16[2,128,1024]{2,1,0:T(8,128)(2,1)S(1)}, bf16[2,128,1024]{2,1,0:T(8,128)(2,1)S(1)}, u32[]{:S(2)}, u32[]{:S(2)}) collective-permute-start(bf16[2,128,1024]{2,1,0:T(8,128)(2,1)S(1)} %collective-permute-done.18), channel_id=1, source_target_pairs={{4,0},{6,2},{12,4},{14,6},{20,12},{22,14},{28,20},{30,22},{24,28},... | collective-permute-start | bytes 1572872 | tf_op jit(solution)/shard_map/ppermute | solution.py:134
  81.6 19.6 %collective-permute-start.33 = (bf16[2,128,1024]{2,1,0:T(8,128)(2,1)S(1)}, bf16[2,128,1024]{2,1,0:T(8,128)(2,1)S(1)}, u32[]{:S(2)}, u32[]{:S(2)}) collective-permute-start(bf16[2,128,1024]{2,1,0:T(8,128)(2,1)S(1)} %collective-permute-done.27), channel_id=1, source_target_pairs={{4,12},{6,14},{12,20},{14,22},{20,28},{22,30},{28,24},{30,26},{24,... | collective-permute-start | bytes 1572872 | tf_op jit(solution)/shard_map/ppermute | solution.py:134
  83.2 19.5 %collective-permute-start.34 = (bf16[2,128,1024]{2,1,0:T(8,128)(2,1)S(1)}, bf16[2,128,1024]{2,1,0:T(8,128)(2,1)S(1)}, u32[]{:S(2)}, u32[]{:S(2)}) collective-permute-start(bf16[2,128,1024]{2,1,0:T(8,128)(2,1)S(1)} %collective-permute-done.28), channel_id=1, source_target_pairs={{4,0},{6,2},{12,4},{14,6},{20,12},{22,14},{28,20},{30,22},{24,28},... | collective-permute-start | bytes 1572872 | tf_op jit(solution)/shard_map/ppermute | solution.py:134
  93.3 13.1 %collective-permute-start.32 = (bf16[128,2048]{1,0:T(8,128)(2,1)S(1)}, bf16[128,2048]{1,0:T(8,128)(2,1)S(1)}, u32[]{:S(2)}, u32[]{:S(2)}) collective-permute-start(bf16[128,2048]{1,0:T(8,128)(2,1)S(1)} %combine.1), channel_id=1, source_target_pairs={{0,1},{1,0},{2,3},{3,2},{4,5},{5,4},{6,7},{7,6},{8,9},{9,8},{10,11... | collective-permute-start | bytes 1572872 | tf_op jit(solution)/shard_map/ppermute | solution.py:152
  94.9 17.6 %collective-permute-start.36 = (bf16[2,128,1024]{2,1,0:T(8,128)(2,1)S(1)}, bf16[2,128,1024]{2,1,0:T(8,128)(2,1)S(1)}, u32[]{:S(2)}, u32[]{:S(2)}) collective-permute-start(bf16[2,128,1024]{2,1,0:T(8,128)(2,1)S(1)} %collective-permute-done.29), channel_id=1, source_target_pairs={{4,12},{6,14},{12,20},{14,22},{20,28},{22,30},{28,24},{30,26},{24,... | collective-permute-start | bytes 1572872 | tf_op jit(solution)/shard_map/ppermute | solution.py:134
  96.5 17.5 %collective-permute-start.37 = (bf16[2,128,1024]{2,1,0:T(8,128)(2,1)S(1)}, bf16[2,128,1024]{2,1,0:T(8,128)(2,1)S(1)}, u32[]{:S(2)}, u32[]{:S(2)}) collective-permute-start(bf16[2,128,1024]{2,1,0:T(8,128)(2,1)S(1)} %collective-permute-done.30), channel_id=1, source_target_pairs={{4,0},{6,2},{12,4},{14,6},{20,12},{22,14},{28,20},{30,22},{24,28},... | collective-permute-start | bytes 1572872 | tf_op jit(solution)/shard_map/ppermute | solution.py:134
  101.3 14.3 %collective-permute-start.31 = (bf16[128,2048]{1,0:T(8,128)(2,1)S(1)}, bf16[128,2048]{1,0:T(8,128)(2,1)S(1)}, u32[]{:S(2)}, u32[]{:S(2)}) collective-permute-start(bf16[128,2048]{1,0:T(8,128)(2,1)S(1)} %combine.1), channel_id=1, source_target_pairs={{0,2},{2,0},{4,6},{6,4},{8,10},{10,8},{12,14},{14,12},{16,18},{18,... | collective-permute-start | bytes 1572872 | tf_op jit(solution)/shard_map/ppermute | solution.py:148
  102.7 16.6 %collective-permute-start.40 = (bf16[144,1024]{1,0:T(8,128)(2,1)S(1)}, bf16[144,1024]{1,0:T(8,128)(2,1)S(1)}, u32[]{:S(2)}, u32[]{:S(2)}) collective-permute-start(bf16[144,1024]{1,0:T(8,128)(2,1)S(1)} %slice.42), channel_id=1, source_target_pairs={{4,12},{6,14},{12,20},{14,22},{20,28},{22,30},{28,24},{30,26},{24,... | collective-permute-start | bytes 884744 | tf_op jit(solution)/shard_map/ppermute | solution.py:134
  106.5 12.8 %collective-permute-start.41 = (bf16[112,1024]{1,0:T(8,128)(2,1)S(1)}, bf16[112,1024]{1,0:T(8,128)(2,1)S(1)}, u32[]{:S(2)}, u32[]{:S(2)}) collective-permute-start(bf16[112,1024]{1,0:T(8,128)(2,1)S(1)} %slice.43), channel_id=1, source_target_pairs={{4,0},{6,2},{12,4},{14,6},{20,12},{22,14},{28,20},{30,22},{24,28},... | collective-permute-start | bytes 688136 | tf_op jit(solution)/shard_map/ppermute | solution.py:134
  114.0 10.2 %collective-permute-start.38 = (bf16[128,1024]{1,0:T(8,128)(2,1)S(1)}, bf16[128,1024]{1,0:T(8,128)(2,1)S(1)}, u32[]{:S(2)}, u32[]{:S(2)}) collective-permute-start(bf16[128,1024]{1,0:T(8,128)(2,1)S(1)} %slice_bitcast_fusion.1), channel_id=1, source_target_pairs={{4,12},{6,14},{12,20},{14,22},{20,28},{22,30},{28,24},{30,26},{24,... | collective-permute-start | bytes 786440 | tf_op jit(solution)/shard_map/ppermute | solution.py:134
  (19 other events, 192.4 us)
